TPU v7x, 128 devices: a whole 4x4x4 slice. The times are simulated.
128 devices in a mesh: pack: 4 (over y), seq: 32 (over x, z, core).
Axes of the slice: x: 4, y: 4, z: 4, core: 2. Of those that a mesh axis runs over, the one named last changes fastest.
Arguments:
- query_rows: bfloat16 [4, 4096, 4096], P('pack', 'seq'), may hold values from -8 to 8
- key_rows: bfloat16 [4, 4096, 4096], P('pack', 'seq'), may hold values from -8 to 8
- value_rows: bfloat16 [4, 4096, 4096], P('pack', 'seq'), may hold values from -6 to 6
- target_rows: bfloat16 [4, 4096, 4096], P('pack', 'seq'), may hold values from -6 to 6
- norm_gains: float32 [2, 32, 128], P(None, 'seq'), may hold values from 0.5 to 3.2
- segment_ids: int32 [4, 4096], P('pack', 'seq'), may hold values from 0 to 15, never falling along the last dimension, each value on 1 to 1024 neighbouring positions
- group_labels: int32 [4, 16], P('pack'), may hold values from 0 to 7, as said below
- mixture: float32 [8], replicated, may hold values from 0.05 to 0.5
Outputs:
- attended: bfloat16 [4, 4096, 4096], P('pack', 'seq')
- grad_query: bfloat16 [4, 4096, 4096], P('pack', 'seq')
- grad_key: bfloat16 [4, 4096, 4096], P('pack', 'seq')
- grad_value: bfloat16 [4, 4096, 4096], P('pack', 'seq')
- grad_gains: float32 [2, 32, 128], P(None, 'seq')
- new_mixture: float32 [8], replicated
Inputs may be any that keep to these rules, and one draw needn't show every extreme that they name: `segment_ids`: segment numbers never fall along a pack's rows; each image of a pack has 1 to 1024 patches, one exactly 1024. `group_labels`: every group labels one or more images of each pack.
All inputs are finite; a program needn't handle non-finite values.
Results may differ from a plain program's by a relative error of at most 0.0028.
The roundings to bfloat16 on the way count: a program that leaves them out, or rounds other values in their place, can miss the bound.
Values may be sent and summed in bfloat16 or wider, within the bound.
No kernel may reach another device: no remote copies, remote signals or barrier semaphores. Data moves between devices by JAX's collectives and lax.ppermute only.
A program may use at most 128 MiB of HBM per device.

v0:
```python
import jax
import jax.numpy as jnp
from jax import lax
from jax.sharding import PartitionSpec as P

HEADS = 32
HEAD_DIM = 128
IMAGES = 16
GROUPS = 8


NEG = -1e30
EPS = 1e-06
ETA = 2.0


def norm_forward(values, gain):
    centre = values - jnp.mean(values, -1, keepdims=True)
    inverse = lax.rsqrt(jnp.mean(centre * centre, -1, keepdims=True) + EPS)
    normed = centre * inverse
    return (normed, inverse, normed * gain)


def norm_backward(grad_hat, normed, inverse, gain):
    grad_gain = jnp.sum(grad_hat * normed, -2)
    grad_normed = grad_hat * gain
    inner = jnp.mean(grad_normed * normed, -1, keepdims=True)
    grad_in = inverse * (grad_normed - jnp.mean(grad_normed, -1, keepdims=True) - normed * inner)
    return (grad_in, grad_gain)


def unchanged(value):
    return value


def on_device(
    query_rows, key_rows, value_rows, target_rows, norm_gains, segment_ids, group_labels, mixture
):
    seg_whole = lax.all_gather(segment_ids, "seq", axis=1, tiled=True)[0]
    head_q, head_k, head_v, head_t = (
        lax.all_to_all(query_rows, "seq", split_axis=2, concat_axis=1, tiled=True),
        lax.all_to_all(key_rows, "seq", split_axis=2, concat_axis=1, tiled=True),
        lax.all_to_all(value_rows, "seq", split_axis=2, concat_axis=1, tiled=True),
        lax.all_to_all(target_rows, "seq", split_axis=2, concat_axis=1, tiled=True),
    )
    seq_length = head_q.shape[1]
    local_heads = head_q.shape[2] // HEAD_DIM
    block_rows = min(512, seq_length)
    block_count = seq_length // block_rows
    score_scale = HEAD_DIM ** (-0.5)

    def split_heads(values):
        return values[0].reshape(seq_length, local_heads, HEAD_DIM).transpose(1, 0, 2)

    def merge_heads(values):
        return values.transpose(1, 0, 2).reshape(1, seq_length, local_heads * HEAD_DIM)

    def merge_blocks(stacked):
        return stacked.transpose(1, 0, 2, 3).reshape(local_heads, seq_length, stacked.shape[-1])

    image_hot = (seg_whole[:, None] == jnp.arange(IMAGES, dtype=jnp.int32)[None, :]).astype(
        jnp.float32
    )
    label_hot = (group_labels[0][:, None] == jnp.arange(GROUPS, dtype=jnp.int32)[None, :]).astype(
        jnp.float32
    )
    group_hot = jnp.dot(image_hot, label_hot, precision=lax.Precision.HIGHEST)
    counts = lax.psum(jnp.sum(group_hot, 0), "pack")
    shares = mixture / jnp.sum(mixture)
    row_coef = jnp.sum(group_hot * (shares / (counts * (HEADS * HEAD_DIM)))[None, :], 1)
    gain_query = norm_gains[0][:, None, :]
    gain_key = norm_gains[1][:, None, :]
    q_normed, q_inverse, q_hat = norm_forward(split_heads(head_q).astype(jnp.float32), gain_query)
    k_normed, k_inverse, k_hat = norm_forward(split_heads(head_k).astype(jnp.float32), gain_key)
    query_low = q_hat.astype(jnp.bfloat16)
    key_low = k_hat.astype(jnp.bfloat16)
    value_low = split_heads(head_v)
    target_heads = split_heads(head_t)

    def take_rows(values, first_row, axis):
        return lax.dynamic_slice_in_dim(values, first_row, block_rows, axis)

    def masked_scores(query_block, segment_block, key_block, key_segments):
        logits = (
            jnp.einsum("hqd,hkd->hqk", query_block, key_block, preferred_element_type=jnp.float32)
            * score_scale
        )
        return jnp.where((segment_block[:, None] == key_segments[None, :])[None], logits, NEG)

    def tile_used(row_index, col_index):
        row_first = seg_whole[row_index * block_rows]
        row_last = seg_whole[row_index * block_rows + block_rows - 1]
        col_first = seg_whole[col_index * block_rows]
        col_last = seg_whole[col_index * block_rows + block_rows - 1]
        return (row_first <= col_last) & (col_first <= row_last)

    def sparse_stats(row_index, query_block, segment_block):

        def visit_tile(col_index, state_now):

            def add_tile(state_in):
                row_top, row_total = state_in
                start_col = col_index * block_rows
                logits = masked_scores(
                    query_block,
                    segment_block,
                    take_rows(key_low, start_col, 1),
                    take_rows(seg_whole, start_col, 0),
                )
                new_top = jnp.maximum(row_top, jnp.max(logits, -1))
                row_total = row_total * jnp.exp(row_top - new_top) + jnp.sum(
                    jnp.exp(logits - new_top[..., None]), -1
                )
                return (new_top, row_total)

            return lax.cond(tile_used(row_index, col_index), add_tile, unchanged, state_now)

        initial = (
            jnp.full((local_heads, block_rows), NEG, jnp.float32),
            jnp.zeros((local_heads, block_rows), jnp.float32),
        )
        return lax.fori_loop(0, block_count, visit_tile, initial)

    def sparse_output(row_index, query_block, segment_block, row_top, row_total):

        def visit_tile(col_index, out_now):

            def add_tile(out_in):
                start_col = col_index * block_rows
                logits = masked_scores(
                    query_block,
                    segment_block,
                    take_rows(key_low, start_col, 1),
                    take_rows(seg_whole, start_col, 0),
                )
                softmax_rows = jnp.exp(logits - row_top[..., None]) / row_total[..., None]
                return out_in + jnp.einsum(
                    "hqk,hkd->hqd",
                    softmax_rows.astype(jnp.bfloat16),
                    take_rows(value_low, start_col, 1),
                    preferred_element_type=jnp.float32,
                )

            return lax.cond(tile_used(row_index, col_index), add_tile, unchanged, out_now)

        return lax.fori_loop(
            0, block_count, visit_tile, jnp.zeros((local_heads, block_rows, HEAD_DIM), jnp.float32)
        )

    def forward_rows(row_index):
        query_block = take_rows(query_low, row_index * block_rows, 1)
        segment_block = take_rows(seg_whole, row_index * block_rows, 0)
        stats = sparse_stats(row_index, query_block, segment_block)
        head_out = sparse_output(row_index, query_block, segment_block, stats[0], stats[1])
        return (head_out, stats)

    def loss_rows(row_index, head_out):
        misfit = head_out - take_rows(target_heads, row_index * block_rows, 1).astype(jnp.float32)
        row_loss = 0.5 * jnp.sum(misfit * misfit, (0, 2))
        grad_out = take_rows(row_coef, row_index * block_rows, 0)[None, :, None] * misfit
        row_inner = jnp.sum(grad_out * head_out, -1)
        return (row_loss, grad_out.astype(jnp.bfloat16), row_inner)

    def backward_rows(row_index, stats, grad_low, row_inner, grad_key, grad_value):
        query_block = take_rows(query_low, row_index * block_rows, 1)
        segment_block = take_rows(seg_whole, row_index * block_rows, 0)
        row_top, row_total = stats

        def visit_tile(col_index, state_now):

            def add_tile(state_in):
                grad_query, grad_key, grad_value = state_in
                start_col = col_index * block_rows
                key_block = take_rows(key_low, start_col, 1)
                value_block = take_rows(value_low, start_col, 1)
                logits = masked_scores(
                    query_block, segment_block, key_block, take_rows(seg_whole, start_col, 0)
                )
                softmax_rows = jnp.exp(logits - row_top[..., None]) / row_total[..., None]
                value_part = jnp.einsum(
                    "hqk,hqd->hkd",
                    softmax_rows.astype(jnp.bfloat16),
                    grad_low,
                    preferred_element_type=jnp.float32,
                )
                prob_grads = jnp.einsum(
                    "hqd,hkd->hqk", grad_low, value_block, preferred_element_type=jnp.float32
                )
                score_grads = (
                    softmax_rows * (prob_grads - row_inner[..., None]) * score_scale
                ).astype(jnp.bfloat16)
                grad_query = grad_query + jnp.einsum(
                    "hqk,hkd->hqd", score_grads, key_block, preferred_element_type=jnp.float32
                )
                key_part = jnp.einsum(
                    "hqk,hqd->hkd", score_grads, query_block, preferred_element_type=jnp.float32
                )
                grad_key = lax.dynamic_update_slice_in_dim(
                    grad_key, take_rows(grad_key, start_col, 1) + key_part, start_col, 1
                )
                grad_value = lax.dynamic_update_slice_in_dim(
                    grad_value, take_rows(grad_value, start_col, 1) + value_part, start_col, 1
                )
                return (grad_query, grad_key, grad_value)

            return lax.cond(tile_used(row_index, col_index), add_tile, unchanged, state_now)

        initial = (
            jnp.zeros((local_heads, block_rows, HEAD_DIM), jnp.float32),
            grad_key,
            grad_value,
        )
        grad_query, grad_key, grad_value = lax.fori_loop(0, block_count, visit_tile, initial)
        return (grad_query, grad_key, grad_value)

    zero_heads = jnp.zeros((local_heads, seq_length, HEAD_DIM), jnp.float32)
    block_ids = jnp.arange(block_count, dtype=jnp.int32)

    def block_step(state_now, row_index):
        grad_khat, grad_vall = state_now
        head_out, stats = forward_rows(row_index)
        row_loss, grad_low, row_inner = loss_rows(row_index, head_out)
        grad_query, grad_khat, grad_vall = backward_rows(
            row_index, stats, grad_low, row_inner, grad_khat, grad_vall
        )
        return ((grad_khat, grad_vall), (head_out.astype(jnp.bfloat16), grad_query, row_loss))

    carried, stacked = lax.scan(block_step, (zero_heads, zero_heads), block_ids)
    grad_khat, grad_vall = carried
    out_all = merge_blocks(stacked[0])
    grad_qhat = merge_blocks(stacked[1])
    losses = stacked[2].reshape(seq_length)
    grad_query, gain_grad_q = norm_backward(grad_qhat, q_normed, q_inverse, gain_query)
    grad_key, gain_grad_k = norm_backward(grad_khat, k_normed, k_inverse, gain_key)
    query_back = merge_heads(grad_query.astype(jnp.bfloat16))
    key_back = merge_heads(grad_key.astype(jnp.bfloat16))
    gain_terms = jnp.stack([gain_grad_q, gain_grad_k])
    attended, grad_query, grad_key, grad_value = (
        lax.all_to_all(merge_heads(out_all), "seq", split_axis=1, concat_axis=2, tiled=True),
        lax.all_to_all(query_back, "seq", split_axis=1, concat_axis=2, tiled=True),
        lax.all_to_all(key_back, "seq", split_axis=1, concat_axis=2, tiled=True),
        lax.all_to_all(
            merge_heads(grad_vall.astype(jnp.bfloat16)),
            "seq",
            split_axis=1,
            concat_axis=2,
            tiled=True,
        ),
    )
    grad_gains = lax.psum(gain_terms, "pack")
    group_part = jnp.dot(losses, group_hot, precision=lax.Precision.HIGHEST)
    group_total = lax.psum(group_part, ("pack", "seq"))
    group_loss = group_total / (counts * (HEADS * HEAD_DIM))
    raised = shares * jnp.exp(ETA * group_loss)
    return (attended, grad_query, grad_key, grad_value, grad_gains, raised / jnp.sum(raised))


def solution(mesh):
    in_specs = (
        P("pack", "seq", None),
        P("pack", "seq", None),
        P("pack", "seq", None),
        P("pack", "seq", None),
        P(None, "seq", None),
        P("pack", "seq"),
        P("pack", None),
        P(),
    )
    out_specs = (
        P("pack", "seq", None),
        P("pack", "seq", None),
        P("pack", "seq", None),
        P("pack", "seq", None),
        P(None, "seq", None),
        P(),
    )
    return jax.shard_map(
        on_device, mesh=mesh, in_specs=in_specs, out_specs=out_specs, check_vma=False
    )
```

profile of v0, /device:TPU:1, one launch (start us, length us, event | category | flops | bytes accessed | tf_op | source)
XLA Modules:
  0.0 1544.9 jit_solution(4077890830279023680)
XLA Ops:
  39.2 29.7 %all_gather.3 = s32[1,4096]{1,0:T(1,128)S(1)} all-gather(s32[1,128]{1,0:T(1,128)S(1)} %copy-done.20), channel_id=1, replica_groups=mesh['pack'=4,'seq'=32] {'seq'}, dimensions={1}, use_global_device_ids=true | all-gather | bytes 16896 | tf_op jit(solution)/shard_map/all_gather | solution.py:39
  83.4 23.4 %reduce.30 = bf16[4096,128]{1,0:T(8,128)(2,1)} reduce(bf16[4096,1,128]{2,1,0:T(2,128)(2,1)S(1)} %bitcast.256, bf16[]{:T(256)} %broadcast.552), dimensions={1}, to_apply=%bitcast.189.reduce_sub_computation | reduce | bytes 2097154
  144.4 23.9 %reduce.33 = bf16[4096,128]{1,0:T(8,128)(2,1)} reduce(bf16[4096,1,128]{2,1,0:T(2,128)(2,1)S(1)} %bitcast.258, bf16[]{:T(256)} %broadcast.552), dimensions={1}, to_apply=%bitcast.195.reduce_sub_computation | reduce | bytes 2097154
  217.1 65.6 %multiply_reduce_fusion.7 = (f32[4096]{0:T(1024)S(1)}, f32[1,4096,128]{2,0,1:T(1,128)}) fusion(f32[1,4096,128]{2,0,1:T(1,128)} %bitcast.239, f32[4096]{0:T(1024)S(1)} %bitcast.286), kind=kLoop, calls=%fused_computation.86 | loop fusion | flops 1568768 | bytes 4227072 | tf_op jit(solution)/shard_map/reduce_sum | solution.py:19
  332.5 896.7 %while.122 = (s32[]{:T(128)}, f32[1,4096,128]{2,1,0:T(8,128)S(1)}, f32[1,4096,128]{2,1,0:T(8,128)}, bf16[8,1,512,128]{3,2,1,0:T(8,128)(2,1)}, f32[8,1,512,128]{3...) while((s32[]{:T(128)}, f32[1,4096,128]{2,1,0:T(8,128)S(1)}, ...), condition=%wide.region_25.26_spmd, body=%wide.region_8.25_spmd.sunk | while | flops 543490560 | bytes 12806464 | solution.py:228
  335.4 29.2 %while.123 = (s32[]{:T(128)}, f32[1,512]{1,0:T(1,128)S(1)}, f32[1,512]{1,0:T(1,128)S(1)}, s32[4096]{0:T(1024)S(1)}, s32[1]{0:T(128)}, /*index=5*/s32[1]{0:T(128)...) while((s32[]{:T(128)}, f32[1,512]{1,0:T(1,128)S(1)}, ...), condition=%wide.region_14.14_spmd, body=%wide.region_9.13_spmd.sunk | while | flops 68682768 | bytes 2394545 | solution.py:122
  364.6 29.6 %while.124 = (s32[]{:T(128)}, f32[1,512,128]{2,1,0:T(8,128)S(1)}, s32[4096]{0:T(1024)S(1)}, s32[1]{0:T(128)}, s32[1]{0:T(128)}, /*index=5*/s32[512]{0:T(512)S(1)...) while((s32[]{:T(128)}, f32[1,512,128]{2,1,0:T(8,128)S(1)}, ...), condition=%wide.region_18.18_spmd, body=%wide.region_15.17_spmd.sunk | while | flops 135856144 | bytes 931245 | solution.py:146
  395.6 38.0 %while.125 = (s32[]{:T(128)}, f32[1,512,128]{2,1,0:T(8,128)S(1)}, f32[1,4096,128]{2,1,0:T(8,128)S(1)}, f32[1,4096,128]{2,1,0:T(8,128)}, s32[4096]{0:T(1024)S(1)}...) while((s32[]{:T(128)}, f32[1,512,128]{2,1,0:T(8,128)S(1)}, ...), condition=%wide.region_23.23_spmd, body=%wide.region_20.0_spmd.sunk | while | flops 338362368 | bytes 7223857 | solution.py:213
  438.0 30.7 %while.123 = (s32[]{:T(128)}, f32[1,512]{1,0:T(1,128)S(1)}, f32[1,512]{1,0:T(1,128)S(1)}, s32[4096]{0:T(1024)S(1)}, s32[1]{0:T(128)}, /*index=5*/s32[1]{0:T(128)...) while((s32[]{:T(128)}, f32[1,512]{1,0:T(1,128)S(1)}, ...), condition=%wide.region_14.14_spmd, body=%wide.region_9.13_spmd.sunk | while | flops 68682768 | bytes 2394545 | solution.py:122
  468.7 31.4 %while.124 = (s32[]{:T(128)}, f32[1,512,128]{2,1,0:T(8,128)S(1)}, s32[4096]{0:T(1024)S(1)}, s32[1]{0:T(128)}, s32[1]{0:T(128)}, /*index=5*/s32[512]{0:T(512)S(1)...) while((s32[]{:T(128)}, f32[1,512,128]{2,1,0:T(8,128)S(1)}, ...), condition=%wide.region_18.18_spmd, body=%wide.region_15.17_spmd.sunk | while | flops 135856144 | bytes 931245 | solution.py:146
  501.5 44.2 %while.125 = (s32[]{:T(128)}, f32[1,512,128]{2,1,0:T(8,128)S(1)}, f32[1,4096,128]{2,1,0:T(8,128)S(1)}, f32[1,4096,128]{2,1,0:T(8,128)}, s32[4096]{0:T(1024)S(1)}...) while((s32[]{:T(128)}, f32[1,512,128]{2,1,0:T(8,128)S(1)}, ...), condition=%wide.region_23.23_spmd, body=%wide.region_20.0_spmd.sunk | while | flops 338362368 | bytes 7223857 | solution.py:213
  550.0 30.7 %while.123 = (s32[]{:T(128)}, f32[1,512]{1,0:T(1,128)S(1)}, f32[1,512]{1,0:T(1,128)S(1)}, s32[4096]{0:T(1024)S(1)}, s32[1]{0:T(128)}, /*index=5*/s32[1]{0:T(128)...) while((s32[]{:T(128)}, f32[1,512]{1,0:T(1,128)S(1)}, ...), condition=%wide.region_14.14_spmd, body=%wide.region_9.13_spmd.sunk | while | flops 68682768 | bytes 2394545 | solution.py:122
  580.8 31.4 %while.124 = (s32[]{:T(128)}, f32[1,512,128]{2,1,0:T(8,128)S(1)}, s32[4096]{0:T(1024)S(1)}, s32[1]{0:T(128)}, s32[1]{0:T(128)}, /*index=5*/s32[512]{0:T(512)S(1)...) while((s32[]{:T(128)}, f32[1,512,128]{2,1,0:T(8,128)S(1)}, ...), condition=%wide.region_18.18_spmd, body=%wide.region_15.17_spmd.sunk | while | flops 135856144 | bytes 931245 | solution.py:146
  613.5 44.2 %while.125 = (s32[]{:T(128)}, f32[1,512,128]{2,1,0:T(8,128)S(1)}, f32[1,4096,128]{2,1,0:T(8,128)S(1)}, f32[1,4096,128]{2,1,0:T(8,128)}, s32[4096]{0:T(1024)S(1)}...) while((s32[]{:T(128)}, f32[1,512,128]{2,1,0:T(8,128)S(1)}, ...), condition=%wide.region_23.23_spmd, body=%wide.region_20.0_spmd.sunk | while | flops 338362368 | bytes 7223857 | solution.py:213
  662.1 32.3 %while.123 = (s32[]{:T(128)}, f32[1,512]{1,0:T(1,128)S(1)}, f32[1,512]{1,0:T(1,128)S(1)}, s32[4096]{0:T(1024)S(1)}, s32[1]{0:T(128)}, /*index=5*/s32[1]{0:T(128)...) while((s32[]{:T(128)}, f32[1,512]{1,0:T(1,128)S(1)}, ...), condition=%wide.region_14.14_spmd, body=%wide.region_9.13_spmd.sunk | while | flops 68682768 | bytes 2394545 | solution.py:122
  694.4 33.2 %while.124 = (s32[]{:T(128)}, f32[1,512,128]{2,1,0:T(8,128)S(1)}, s32[4096]{0:T(1024)S(1)}, s32[1]{0:T(128)}, s32[1]{0:T(128)}, /*index=5*/s32[512]{0:T(512)S(1)...) while((s32[]{:T(128)}, f32[1,512,128]{2,1,0:T(8,128)S(1)}, ...), condition=%wide.region_18.18_spmd, body=%wide.region_15.17_spmd.sunk | while | flops 135856144 | bytes 931245 | solution.py:146
  729.0 50.4 %while.125 = (s32[]{:T(128)}, f32[1,512,128]{2,1,0:T(8,128)S(1)}, f32[1,4096,128]{2,1,0:T(8,128)S(1)}, f32[1,4096,128]{2,1,0:T(8,128)}, s32[4096]{0:T(1024)S(1)}...) while((s32[]{:T(128)}, f32[1,512,128]{2,1,0:T(8,128)S(1)}, ...), condition=%wide.region_23.23_spmd, body=%wide.region_20.0_spmd.sunk | while | flops 338362368 | bytes 7223857 | solution.py:213
  783.8 30.7 %while.123 = (s32[]{:T(128)}, f32[1,512]{1,0:T(1,128)S(1)}, f32[1,512]{1,0:T(1,128)S(1)}, s32[4096]{0:T(1024)S(1)}, s32[1]{0:T(128)}, /*index=5*/s32[1]{0:T(128)...) while((s32[]{:T(128)}, f32[1,512]{1,0:T(1,128)S(1)}, ...), condition=%wide.region_14.14_spmd, body=%wide.region_9.13_spmd.sunk | while | flops 68682768 | bytes 2394545 | solution.py:122
  814.5 31.4 %while.124 = (s32[]{:T(128)}, f32[1,512,128]{2,1,0:T(8,128)S(1)}, s32[4096]{0:T(1024)S(1)}, s32[1]{0:T(128)}, s32[1]{0:T(128)}, /*index=5*/s32[512]{0:T(512)S(1)...) while((s32[]{:T(128)}, f32[1,512,128]{2,1,0:T(8,128)S(1)}, ...), condition=%wide.region_18.18_spmd, body=%wide.region_15.17_spmd.sunk | while | flops 135856144 | bytes 931245 | solution.py:146
  847.3 44.2 %while.125 = (s32[]{:T(128)}, f32[1,512,128]{2,1,0:T(8,128)S(1)}, f32[1,4096,128]{2,1,0:T(8,128)S(1)}, f32[1,4096,128]{2,1,0:T(8,128)}, s32[4096]{0:T(1024)S(1)}...) while((s32[]{:T(128)}, f32[1,512,128]{2,1,0:T(8,128)S(1)}, ...), condition=%wide.region_23.23_spmd, body=%wide.region_20.0_spmd.sunk | while | flops 338362368 | bytes 7223857 | solution.py:213
  895.8 32.3 %while.123 = (s32[]{:T(128)}, f32[1,512]{1,0:T(1,128)S(1)}, f32[1,512]{1,0:T(1,128)S(1)}, s32[4096]{0:T(1024)S(1)}, s32[1]{0:T(128)}, /*index=5*/s32[1]{0:T(128)...) while((s32[]{:T(128)}, f32[1,512]{1,0:T(1,128)S(1)}, ...), condition=%wide.region_14.14_spmd, body=%wide.region_9.13_spmd.sunk | while | flops 68682768 | bytes 2394545 | solution.py:122
  928.1 33.2 %while.124 = (s32[]{:T(128)}, f32[1,512,128]{2,1,0:T(8,128)S(1)}, s32[4096]{0:T(1024)S(1)}, s32[1]{0:T(128)}, s32[1]{0:T(128)}, /*index=5*/s32[512]{0:T(512)S(1)...) while((s32[]{:T(128)}, f32[1,512,128]{2,1,0:T(8,128)S(1)}, ...), condition=%wide.region_18.18_spmd, body=%wide.region_15.17_spmd.sunk | while | flops 135856144 | bytes 931245 | solution.py:146
  962.7 50.4 %while.125 = (s32[]{:T(128)}, f32[1,512,128]{2,1,0:T(8,128)S(1)}, f32[1,4096,128]{2,1,0:T(8,128)S(1)}, f32[1,4096,128]{2,1,0:T(8,128)}, s32[4096]{0:T(1024)S(1)}...) while((s32[]{:T(128)}, f32[1,512,128]{2,1,0:T(8,128)S(1)}, ...), condition=%wide.region_23.23_spmd, body=%wide.region_20.0_spmd.sunk | while | flops 338362368 | bytes 7223857 | solution.py:213
  1017.4 30.7 %while.123 = (s32[]{:T(128)}, f32[1,512]{1,0:T(1,128)S(1)}, f32[1,512]{1,0:T(1,128)S(1)}, s32[4096]{0:T(1024)S(1)}, s32[1]{0:T(128)}, /*index=5*/s32[1]{0:T(128)...) while((s32[]{:T(128)}, f32[1,512]{1,0:T(1,128)S(1)}, ...), condition=%wide.region_14.14_spmd, body=%wide.region_9.13_spmd.sunk | while | flops 68682768 | bytes 2394545 | solution.py:122
  1048.2 31.4 %while.124 = (s32[]{:T(128)}, f32[1,512,128]{2,1,0:T(8,128)S(1)}, s32[4096]{0:T(1024)S(1)}, s32[1]{0:T(128)}, s32[1]{0:T(128)}, /*index=5*/s32[512]{0:T(512)S(1)...) while((s32[]{:T(128)}, f32[1,512,128]{2,1,0:T(8,128)S(1)}, ...), condition=%wide.region_18.18_spmd, body=%wide.region_15.17_spmd.sunk | while | flops 135856144 | bytes 931245 | solution.py:146
  1080.9 44.2 %while.125 = (s32[]{:T(128)}, f32[1,512,128]{2,1,0:T(8,128)S(1)}, f32[1,4096,128]{2,1,0:T(8,128)S(1)}, f32[1,4096,128]{2,1,0:T(8,128)}, s32[4096]{0:T(1024)S(1)}...) while((s32[]{:T(128)}, f32[1,512,128]{2,1,0:T(8,128)S(1)}, ...), condition=%wide.region_23.23_spmd, body=%wide.region_20.0_spmd.sunk | while | flops 338362368 | bytes 7223857 | solution.py:213
  1129.5 29.2 %while.123 = (s32[]{:T(128)}, f32[1,512]{1,0:T(1,128)S(1)}, f32[1,512]{1,0:T(1,128)S(1)}, s32[4096]{0:T(1024)S(1)}, s32[1]{0:T(128)}, /*index=5*/s32[1]{0:T(128)...) while((s32[]{:T(128)}, f32[1,512]{1,0:T(1,128)S(1)}, ...), condition=%wide.region_14.14_spmd, body=%wide.region_9.13_spmd.sunk | while | flops 68682768 | bytes 2394545 | solution.py:122
  1158.7 29.6 %while.124 = (s32[]{:T(128)}, f32[1,512,128]{2,1,0:T(8,128)S(1)}, s32[4096]{0:T(1024)S(1)}, s32[1]{0:T(128)}, s32[1]{0:T(128)}, /*index=5*/s32[512]{0:T(512)S(1)...) while((s32[]{:T(128)}, f32[1,512,128]{2,1,0:T(8,128)S(1)}, ...), condition=%wide.region_18.18_spmd, body=%wide.region_15.17_spmd.sunk | while | flops 135856144 | bytes 931245 | solution.py:146
  1189.7 38.0 %while.125 = (s32[]{:T(128)}, f32[1,512,128]{2,1,0:T(8,128)S(1)}, f32[1,4096,128]{2,1,0:T(8,128)S(1)}, f32[1,4096,128]{2,1,0:T(8,128)}, s32[4096]{0:T(1024)S(1)}...) while((s32[]{:T(128)}, f32[1,512,128]{2,1,0:T(8,128)S(1)}, ...), condition=%wide.region_23.23_spmd, body=%wide.region_20.0_spmd.sunk | while | flops 338362368 | bytes 7223857 | solution.py:213
  1305.1 23.4 %reduce.35 = bf16[4096,128]{1,0:T(8,128)(2,1)} reduce(bf16[4096,1,128]{2,1,0:T(2,128)(2,1)S(1)} %fusion.73, bf16[]{:T(256)} %broadcast.552), dimensions={1}, to_apply=%fusion.73.reduce_sub_computation | reduce | bytes 2097154
  1391.8 23.4 %reduce.34 = bf16[4096,128]{1,0:T(8,128)(2,1)} reduce(bf16[4096,1,128]{2,1,0:T(2,128)(2,1)S(1)} %bitcast.253, bf16[]{:T(256)} %broadcast.552), dimensions={1}, to_apply=%bitcast.221.reduce_sub_computation | reduce | bytes 2097154
  1425.5 85.7 %psum.23 = f32[8]{0:T(128)S(1)} all-reduce(f32[8]{0:T(128)S(1)} %convolution_bitcast_fusion.3), channel_id=1, replica_groups=mesh['pack'=4,'seq'=32] {'pack','seq'}, use_global_device_ids=true, to_apply=%region_33.34 | all-reduce | flops 8 | bytes 64 | tf_op jit(solution)/shard_map/psum | solution.py:252
  (981 shorter events, 992.3 us)
Async XLA Ops:
  28.6 10.6 copy-start.20
  28.6 40.3 %copy-start.19 = (s32[1,16]{1,0:T(1,128)S(1)}, s32[1,16]{1,0:T(1,128)}, u32[]{:S(2)}) copy-start(s32[1,16]{1,0:T(1,128)} %param.28) | copy-start | bytes 196
  29.7 142.1 %all-to-all-start.1 = ((bf16[32,2,8192]{2,1,0:T(2,128)(2,1)}), bf16[32,2,8192]{2,1,0:T(2,128)(2,1)}, u32[]{:S(2)}, u32[]{:S(2)}) async-start(bf16[32,2,8192]{2,1,0:T(2,128)(2,1)} %reshape.887), calls=%async_computation.1 | async-start | bytes 2097152 | tf_op jit(solution)/shard_map/all_to_all | solution.py:42
  69.3 102.4 %copy-start.6 = (f32[4096,8]{0,1:T(8,128)}, f32[4096,8]{0,1:T(8,128)S(1)}, u32[]{:S(2)}) copy-start(f32[4096,8]{0,1:T(8,128)S(1)} %get-tuple-element.1987) | copy-start | bytes 393220
  78.3 93.3 %copy-start.16 = (f32[8]{0:T(128)}, f32[8]{0:T(128)S(1)}, u32[]{:S(2)}) copy-start(f32[8]{0:T(128)S(1)} %psum.21) | copy-start | bytes 100
  144.4 26.1 %copy-start.14 = (f32[8]{0:T(128)S(1)}, f32[8]{0:T(128)}, u32[]{:S(2)}) copy-start(f32[8]{0:T(128)} %param.29) | copy-start | bytes 100
  168.3 11.3 copy-start.18
  171.8 24.8 %all-to-all-start = ((bf16[32,2,8192]{2,1,0:T(2,128)(2,1)}), bf16[32,2,8192]{2,1,0:T(2,128)(2,1)}, u32[]{:S(2)}, u32[]{:S(2)}) async-start(bf16[32,2,8192]{2,1,0:T(2,128)(2,1)} %reshape.885), calls=%async_computation | async-start | bytes 2097152 | tf_op jit(solution)/shard_map/all_to_all | solution.py:41
  179.7 111.2 %copy-start.12 = (f32[128]{0:T(128)}, f32[128]{0:T(128)S(1)}, u32[]{:S(2)}) copy-start(f32[128]{0:T(128)S(1)} %get-tuple-element.1985) | copy-start | bytes 1540
  189.2 138.6 %copy-start.1 = (f32[1,128,32,128]{3,1,2,0:T(8,128)}, f32[1,128,32,128]{3,1,2,0:T(8,128)S(1)}, u32[]{:S(2)}) copy-start(f32[1,128,32,128]{3,1,2,0:T(8,128)S(1)} %copy.147) | copy-start | bytes 6291460
  196.6 86.7 %all-to-all-start.2 = ((bf16[32,2,8192]{2,1,0:T(2,128)(2,1)}), bf16[32,2,8192]{2,1,0:T(2,128)(2,1)}, u32[]{:S(2)}, u32[]{:S(2)}) async-start(bf16[32,2,8192]{2,1,0:T(2,128)(2,1)} %reshape.889), calls=%async_computation.2 | async-start | bytes 2097152 | tf_op jit(solution)/shard_map/all_to_all | solution.py:43
  282.7 21.0 %copy-start.8 = (f32[4096]{0:T(1024)}, f32[4096]{0:T(1024)S(1)}, u32[]{:S(2)}) copy-start(f32[4096]{0:T(1024)S(1)} %add_rsqrt_fusion.1) | copy-start | bytes 49156
  283.3 33.7 %all-to-all-start.3 = ((bf16[32,2,8192]{2,1,0:T(2,128)(2,1)}), bf16[32,2,8192]{2,1,0:T(2,128)(2,1)}, u32[]{:S(2)}, u32[]{:S(2)}) async-start(bf16[32,2,8192]{2,1,0:T(2,128)(2,1)} %reshape.891), calls=%async_computation.3 | async-start | bytes 2097152 | tf_op jit(solution)/shard_map/all_to_all | solution.py:44
  1229.2 3.8 copy-start.2
  1275.0 8.5 copy-start.4
  1275.0 8.5 copy-start.10
  1275.0 8.5 copy-start.11
  1275.0 8.5 copy-start.13
  1276.1 54.6 %all-to-all-start.6 = ((bf16[32,2,8192]{2,1,0:T(2,128)(2,1)}), bf16[32,2,8192]{2,1,0:T(2,128)(2,1)S(1)}, u32[]{:S(2)}, u32[]{:S(2)}) async-start(bf16[32,2,8192]{2,1,0:T(2,128)(2,1)} %reshape.897), calls=%async_computation.6 | async-start | bytes 2097152 | tf_op jit(solution)/shard_map/all_to_all | solution.py:241
  1283.5 3.8 copy-start.3
  1283.5 3.8 copy-start.5
  1283.6 3.8 copy-start.9
  1328.4 10.3 copy-start
  1330.7 50.4 %all-to-all-start.5 = ((bf16[32,2,8192]{2,1,0:T(2,128)(2,1)}), bf16[32,2,8192]{2,1,0:T(2,128)(2,1)}, u32[]{:S(2)}, u32[]{:S(2)}) async-start(bf16[32,2,8192]{2,1,0:T(2,128)(2,1)} %reshape.895), calls=%async_computation.5 | async-start | bytes 2097152 | tf_op jit(solution)/shard_map/all_to_all | solution.py:240
  1381.1 36.2 %all-to-all-start.7 = ((bf16[32,2,8192]{2,1,0:T(2,128)(2,1)}), bf16[32,2,8192]{2,1,0:T(2,128)(2,1)}, u32[]{:S(2)}, u32[]{:S(2)}) async-start(bf16[32,2,8192]{2,1,0:T(2,128)(2,1)} %reshape.899), calls=%async_computation.7 | async-start | bytes 2097152 | tf_op jit(solution)/shard_map/all_to_all | solution.py:242
  1415.1 10.0 copy-start.7
  1415.1 104.7 %copy-start.15 = (f32[8]{0:T(128)S(1)}, f32[8]{0:T(128)}, u32[]{:S(2)}) copy-start(f32[8]{0:T(128)} %param.29) | copy-start | bytes 100
  1415.1 104.7 %copy-start.17 = (f32[8]{0:T(128)S(1)}, f32[8]{0:T(128)}, u32[]{:S(2)}) copy-start(f32[8]{0:T(128)} %copy-done.16) | copy-start | bytes 100
  1417.3 120.9 %all-to-all-start.4 = ((bf16[32,2,8192]{2,1,0:T(2,128)(2,1)}), bf16[32,2,8192]{2,1,0:T(2,128)(2,1)}, u32[]{:S(2)}, u32[]{:S(2)}) async-start(bf16[32,2,8192]{2,1,0:T(2,128)(2,1)} %reshape.893), calls=%async_computation.4 | async-start | bytes 2097152 | tf_op jit(solution)/shard_map/all_to_all | solution.py:239
where the time goes:
time: 1560 us; the launch traced here: 1540 us
  loops' own time  506 us (32%)
  other arithmetic  332 us (21%)
  local copies, waits for them, and re-layouts  290 us (19%)
  matrix products  216 us (14%)
  blocking collectives  133 us (9%)
  starting transfers between devices  59.9 us (4%)
    unnamed x10, other arithmetic  203 us
    another operation x8, loops' own time, sparse_stats(): return lax.fori_loop(0, block_count, visit_tile, initial)  166 us
    another operation x8, loops' own time, sparse_output(): lax.fori_loop(0, block_count, visit_tile, jnp.zeros((local_heads, block_r...  166 us
    another operation x8, loops' own time, backward_rows(): lax.fori_loop(0, block_count, visit_tile, initial)  165 us
    dynamic_slice x192, local copies, waits for them, and re-layouts, tile_used(): col_first = seg_whole[col_index * block_rows]  124 us
    psum x1, blocking collectives, on_device(): group_total = lax.psum(group_part, ('pack', 'seq'))  85.7 us
    unnamed x78, local copies, waits for them, and re-layouts  83 us
    reduce_sum x2, other arithmetic, norm_forward(): inverse = lax.rsqrt(jnp.mean(centre * centre, -1, keepdims=True) + EPS)  67 us
  transfers between devices with their start and end apart: 8, of which 1 were waited for; matrix products, arithmetic and copies ran while one was open for 23% of the time, Pallas kernels for 0%

commit v1 on v0

v1 whole, which is shorter than its diff:
```python
import functools

import jax
import jax.numpy as jnp
from jax import lax
from jax.experimental import pallas as pl
from jax.experimental.pallas import tpu as pltpu
from jax.sharding import PartitionSpec as P

HEADS = 32
HEAD_DIM = 128
IMAGES = 16
GROUPS = 8
PACKS = 4
LENGTH = 4096

NEG = -1e30
EPS = 1e-06
ETA = 2.0
SCALE = HEAD_DIM ** (-0.5)
EXP_SCALE = SCALE * 1.4426950408889634

BLOCK = 128
BLOCKS = LENGTH // BLOCK
TILE = 512
TILES = LENGTH // TILE
PAIR = TILE // BLOCK
STATS_KEYS = 256
FORWARD_KEYS = 512
BACKWARD_KEYS = 256
EXTRA = 16
VMEM_LIMIT = 56 * 1024 * 1024

BF16 = jnp.bfloat16
F32 = jnp.float32
I32 = jnp.int32

VMEM_SPEC = pl.BlockSpec(memory_space=pltpu.VMEM)
SMEM_SPEC = pl.BlockSpec(memory_space=pltpu.SMEM)
ANY_SPEC = pl.BlockSpec(memory_space=pl.ANY)


def shape(dims, dtype):
    return jax.ShapeDtypeStruct(dims, dtype)


def head_columns(h):
    return pl.ds(h * HEAD_DIM, HEAD_DIM)


def pack_kernel(*refs):
    *row_refs, extra_ref, out_ref, sems = refs
    copies = []
    for n, ref in enumerate(row_refs):
        for h in range(HEADS):
            copy = pltpu.make_async_copy(
                ref.at[0, :, head_columns(h)],
                out_ref.at[h, pl.ds(n * BLOCK, BLOCK), :],
                sems.at[n, h],
            )
            copy.start()
            copies.append(copy)
    lines = extra_ref.shape[0]
    tile = extra_ref[...].astype(F32)
    tile = jnp.concatenate([tile, jnp.zeros((EXTRA - lines, 128), F32)], 0).astype(BF16)
    out_ref[:, len(row_refs) * BLOCK :, :] = jnp.broadcast_to(tile[None], (HEADS, EXTRA, 128))
    for copy in copies:
        copy.wait()


def pack_rows(rows, extra, name):
    return pl.pallas_call(
        pack_kernel,
        in_specs=[ANY_SPEC] * len(rows) + [VMEM_SPEC],
        out_specs=VMEM_SPEC,
        out_shape=shape((HEADS, len(rows) * BLOCK + EXTRA, 128), BF16),
        scratch_shapes=[pltpu.SemaphoreType.DMA((len(rows), HEADS))],
        compiler_params=pltpu.CompilerParams(vmem_limit_bytes=VMEM_LIMIT),
        name=name,
    )(*rows, extra)


def unpack_kernel(in_ref, *refs):
    *row_refs, sems = refs
    copies = []
    for n, ref in enumerate(row_refs):
        for h in range(HEADS):
            copy = pltpu.make_async_copy(
                in_ref.at[h, pl.ds(n * BLOCK, BLOCK), :],
                ref.at[0, :, head_columns(h)],
                sems.at[n, h],
            )
            copy.start()
            copies.append(copy)
    for copy in copies:
        copy.wait()


def unpack_rows(slab, count, name):
    return pl.pallas_call(
        unpack_kernel,
        in_specs=[VMEM_SPEC],
        out_specs=[ANY_SPEC] * count,
        out_shape=[shape((1, BLOCK, HEADS * HEAD_DIM), BF16)] * count,
        scratch_shapes=[pltpu.SemaphoreType.DMA((count, HEADS))],
        compiler_params=pltpu.CompilerParams(vmem_limit_bytes=VMEM_LIMIT),
        name=name,
    )(slab)


def normalise(rows):
    values = rows.astype(F32)
    centre = values - jnp.mean(values, -1, keepdims=True)
    inverse = lax.rsqrt(jnp.mean(centre * centre, -1, keepdims=True) + EPS)
    return centre * inverse, inverse


def denormalise(grad_hat, normed, inverse, gain):
    grad_gain = jnp.sum(grad_hat * normed, 0, keepdims=True)
    grad_normed = grad_hat * gain
    inner = jnp.mean(grad_normed * normed, -1, keepdims=True)
    grad_in = inverse * (grad_normed - jnp.mean(grad_normed, -1, keepdims=True) - normed * inner)
    return grad_in, grad_gain


def dot(a, b, contract=((1,), (0,))):
    return lax.dot_general(a, b, (contract, ((), ())), preferred_element_type=F32)


def tile_rows(ref, i, part, size=TILE):
    blocks = size // BLOCK
    return ref[pl.ds(i, blocks), part * BLOCK : (part + 1) * BLOCK, :].reshape(size, HEAD_DIM)


def key_span(span_ref, i, step):
    low, high = span_ref[0, i], span_ref[1, i]
    steps = (high - low + step - 1) // step
    return jnp.minimum(low, LENGTH - steps * step), steps


def key_mask(span_rows_ref, i, start, step):
    first = span_rows_ref[i, 0:1, :] - start
    count = span_rows_ref[i, 1:2, :]
    row = lax.broadcasted_iota(I32, (step, TILE), 0)
    return (row - first).astype(jnp.uint32) < count.astype(jnp.uint32)


def stats_kernel(
    recv_ref, gains_ref,
    q_hat_ref, k_hat_ref, k_turned_ref, span_ref, span_rows_ref, norm_ref,
    starts, scores,
):
    gain_q = gains_ref[0:1, :]
    gain_k = gains_ref[1:2, :]

    seg_all = recv_ref[:, 2 * BLOCK, :].astype(F32)
    for s in range(IMAGES + 1):
        starts[s] = jnp.sum((seg_all < float(s)).astype(F32)).astype(I32)
    first = jnp.zeros((BLOCKS, 128), I32)
    count = jnp.zeros((BLOCKS, 128), I32)
    for s in range(IMAGES):
        here = seg_all == float(s)
        first = jnp.where(here, starts[s], first)
        count = jnp.where(here, starts[s + 1] - starts[s], count)
    for b in range(BLOCKS):
        at = slice((b % PAIR) * BLOCK, (b % PAIR + 1) * BLOCK)
        span_rows_ref[b // PAIR, 0:1, at] = first[b : b + 1, :]
        span_rows_ref[b // PAIR, 1:2, at] = count[b : b + 1, :]

    def span(i, carry):
        low, high = jnp.int32(0), jnp.int32(LENGTH)
        for s in range(1, IMAGES):
            low = jnp.where(starts[s] <= i * TILE, starts[s], low)
        for s in range(IMAGES - 1, 0, -1):
            high = jnp.where(starts[s] > i * TILE + TILE - 1, starts[s], high)
        span_ref[0, i] = (low // BLOCK) * BLOCK
        span_ref[1, i] = high
        return carry

    lax.fori_loop(0, TILES, span, 0)

    def prepare(i, carry):
        rows = pl.ds(pl.multiple_of(i * TILE, TILE), TILE)
        normed, _ = normalise(tile_rows(recv_ref, i * PAIR, 0))
        q_hat_ref[rows, :] = (normed * gain_q).astype(BF16)
        normed, _ = normalise(tile_rows(recv_ref, i * PAIR, 1))
        low = (normed * gain_k).astype(BF16)
        k_hat_ref[rows, :] = low
        k_turned_ref[:, rows] = low.T
        return carry

    lax.fori_loop(0, TILES, prepare, 0)

    step = STATS_KEYS

    def query_tile(i, carry):
        start, steps = key_span(span_ref, i, step)
        query = q_hat_ref[pl.ds(pl.multiple_of(i * TILE, TILE), TILE), :]

        def score_tile(j, top):
            at = pl.multiple_of(start + j * step, BLOCK)
            tile = dot(k_hat_ref[pl.ds(at, step), :], query, ((1,), (1,)))
            tile = jnp.where(key_mask(span_rows_ref, i, at, step), tile, NEG)
            scores[j] = tile
            return jnp.maximum(top, jnp.max(tile.reshape(step // 8, 8, TILE), 0))

        top = lax.fori_loop(0, steps, score_tile, jnp.full((8, TILE), NEG, F32))
        top = jnp.max(top, 0, keepdims=True) * EXP_SCALE

        def exp_tile(j, total):
            tile = jnp.exp2(scores[j] * EXP_SCALE - top)
            return total + jnp.sum(tile.reshape(step // 8, 8, TILE), 0)

        total = lax.fori_loop(0, steps, exp_tile, jnp.zeros((8, TILE), F32))
        norm_ref[i, 0:1, :] = top
        norm_ref[i, 1:2, :] = 1.0 / jnp.sum(total, 0, keepdims=True)
        return carry

    lax.fori_loop(0, TILES, query_tile, 0)


def run_stats(received, gains):
    most = 2 * 1024 // STATS_KEYS + TILE // STATS_KEYS + 2
    return pl.pallas_call(
        stats_kernel,
        in_specs=[VMEM_SPEC, VMEM_SPEC],
        out_specs=[VMEM_SPEC] * 3 + [SMEM_SPEC] + [VMEM_SPEC] * 2,
        out_shape=[
            shape((LENGTH, HEAD_DIM), BF16),
            shape((LENGTH, HEAD_DIM), BF16),
            shape((HEAD_DIM, LENGTH), BF16),
            shape((2, TILES), I32),
            shape((TILES, 2, TILE), I32),
            shape((TILES, 2, TILE), F32),
        ],
        scratch_shapes=[
            pltpu.SMEM((IMAGES + 1,), I32),
            pltpu.VMEM((most, STATS_KEYS, TILE), F32),
        ],
        compiler_params=pltpu.CompilerParams(vmem_limit_bytes=VMEM_LIMIT),
        name="score_stats",
    )(received, gains)


def softmax_tile(k_hat_ref, query, span_rows_ref, top, inverse_total, i, at, step):
    tile = dot(k_hat_ref[pl.ds(at, step), :], query, ((1,), (1,)))
    tile = jnp.where(key_mask(span_rows_ref, i, at, step), tile, NEG)
    return jnp.exp2(tile * EXP_SCALE - top) * inverse_total


def forward_kernel(
    span_ref, labels_ref, mixture_ref,
    seg_ref, recv_ref, q_hat_ref, k_hat_ref, span_rows_ref, norm_ref,
    send_ref, grad_ref, grad_turned_ref, inner_ref, counts_ref,
    coef_rows, loss_rows, v_turned, acc,
):
    seg_all = seg_ref[:, 2 * BLOCK, :].astype(F32)
    group = jnp.zeros((BLOCKS, 128), F32)
    for s in range(IMAGES):
        group = jnp.where(seg_all == float(s), labels_ref[0, s].astype(F32), group)
    others = [recv_ref[:, 2 * BLOCK + p, :].astype(F32) for p in range(PACKS)]
    total_mix = mixture_ref[0]
    for g in range(1, GROUPS):
        total_mix = total_mix + mixture_ref[g]
    coef = jnp.zeros((BLOCKS, 128), F32)
    lane = lax.broadcasted_iota(I32, (1, 128), 1)
    count_row = jnp.zeros((1, 128), F32)
    for g in range(GROUPS):
        hits = sum((o == float(g)).astype(F32) for o in others)
        count = jnp.sum(jnp.sum(hits, 0, keepdims=True), 1, keepdims=True)
        share = jnp.full((1, 1), mixture_ref[g], F32) / total_mix
        coef = jnp.where(group == float(g), share / (count * (HEADS * HEAD_DIM)), coef)
        count_row = jnp.where(lane == g, count, count_row)
    counts_ref[...] = count_row
    for b in range(BLOCKS):
        at = slice((b % PAIR) * BLOCK, (b % PAIR + 1) * BLOCK)
        coef_rows[b // PAIR, 0:1, at] = coef[b : b + 1, :]

    def prepare(i, carry):
        rows = pl.ds(pl.multiple_of(i * TILE, TILE), TILE)
        v_turned[:, rows] = tile_rows(recv_ref, i * PAIR, 0).T
        return carry

    lax.fori_loop(0, TILES, prepare, 0)

    step = FORWARD_KEYS

    def query_tile(i, carry):
        start, steps = key_span(span_ref, i, step)
        query_rows = pl.ds(pl.multiple_of(i * TILE, TILE), TILE)
        query = q_hat_ref[query_rows, :]
        top, inverse_total = norm_ref[i, 0:1, :], norm_ref[i, 1:2, :]
        acc[...] = jnp.zeros_like(acc)

        def out_tile(j, inside):
            at = pl.multiple_of(start + j * step, BLOCK)
            tile = softmax_tile(k_hat_ref, query, span_rows_ref, top, inverse_total, i, at, step)
            acc[...] += dot(v_turned[:, pl.ds(at, step)], tile.astype(BF16))
            return inside

        lax.fori_loop(0, steps, out_tile, 0)

        head_out = acc[...]
        target = tile_rows(recv_ref, i * PAIR, 1).T
        misfit = head_out - target.astype(F32)
        loss_rows[i, 0:1, :] = 0.5 * jnp.sum(misfit * misfit, 0, keepdims=True)
        grad_out = coef_rows[i, 0:1, :] * misfit
        inner_ref[i, 0:1, :] = jnp.sum(grad_out * head_out, 0, keepdims=True)
        grad_turned = grad_out.astype(BF16)
        grad_turned_ref[:, query_rows] = grad_turned
        grad_ref[query_rows, :] = grad_turned.T
        send_ref[pl.ds(i * PAIR, PAIR), 0:BLOCK, :] = head_out.astype(BF16).T.reshape(
            PAIR, BLOCK, HEAD_DIM
        )
        return carry

    lax.fori_loop(0, TILES, query_tile, 0)

    losses = jnp.concatenate(
        [
            loss_rows[b // PAIR, 0:1, (b % PAIR) * BLOCK : (b % PAIR + 1) * BLOCK]
            for b in range(BLOCKS)
        ],
        0,
    )
    loss_row = jnp.zeros((1, 128), F32)
    for g in range(GROUPS):
        part = jnp.where(group == float(g), losses, 0.0)
        part = jnp.sum(jnp.sum(part, 0, keepdims=True), 1, keepdims=True)
        loss_row = jnp.where(lane == g, part, loss_row)
    high = loss_row.astype(BF16)
    left = loss_row - high.astype(F32)
    middle = left.astype(BF16)
    low = (left - middle.astype(F32)).astype(BF16)
    row = lax.broadcasted_iota(I32, (EXTRA, 128), 0)
    pieces = jnp.zeros((EXTRA, 128), F32)
    for n, piece in enumerate((high, middle, low)):
        pieces = jnp.where(row == n, piece.astype(F32), pieces)
    send_ref[:, BLOCK:, :] = jnp.broadcast_to(pieces.astype(BF16)[None], (BLOCKS, EXTRA, 128))


def run_forward(spans, labels, mixture, first, second, q_hat, k_hat, span_rows, norms):
    return pl.pallas_call(
        forward_kernel,
        in_specs=[SMEM_SPEC] * 3 + [VMEM_SPEC] * 6,
        out_specs=[VMEM_SPEC] * 5,
        out_shape=[
            shape((BLOCKS, BLOCK + EXTRA, 128), BF16),
            shape((LENGTH, HEAD_DIM), BF16),
            shape((HEAD_DIM, LENGTH), BF16),
            shape((TILES, 1, TILE), F32),
            shape((1, 128), F32),
        ],
        scratch_shapes=[
            pltpu.VMEM((TILES, 8, TILE), F32),
            pltpu.VMEM((TILES, 8, TILE), F32),
            pltpu.VMEM((HEAD_DIM, LENGTH), BF16),
            pltpu.VMEM((HEAD_DIM, TILE), F32),
        ],
        compiler_params=pltpu.CompilerParams(vmem_limit_bytes=VMEM_LIMIT),
        name="forward",
    )(spans, labels, mixture, first, second, q_hat, k_hat, span_rows, norms)


def backward_kernel(
    span_ref,
    first_ref, recv_ref, gains_ref, q_hat_ref, k_hat_ref, k_turned_ref, span_rows_ref, norm_ref,
    grad_ref, grad_turned_ref, inner_ref,
    send_ref, gain_out_ref,
    grad_k, grad_v, acc,
):
    gain_q = gains_ref[0:1, :]
    gain_k = gains_ref[1:2, :]
    zero_gain = jnp.zeros((1, HEAD_DIM), F32)
    grad_k[...] = jnp.zeros_like(grad_k)
    grad_v[...] = jnp.zeros_like(grad_v)

    step = BACKWARD_KEYS

    def query_tile(i, gain_sum):
        start, steps = key_span(span_ref, i, step)
        query_rows = pl.ds(pl.multiple_of(i * TILE, TILE), TILE)
        query = q_hat_ref[query_rows, :]
        top, inverse_total = norm_ref[i, 0:1, :], norm_ref[i, 1:2, :]
        grad_low = grad_ref[query_rows, :]
        grad_turned = grad_turned_ref[:, query_rows]
        row_inner = inner_ref[i, 0:1, :]
        acc[...] = jnp.zeros_like(acc)

        def back_tile(j, inside):
            at = pl.multiple_of(start + j * step, BLOCK)
            keys = pl.ds(at, step)
            tile = softmax_tile(k_hat_ref, query, span_rows_ref, top, inverse_total, i, at, step)
            value = tile_rows(recv_ref, at // BLOCK, 0, step)
            prob_grads = dot(value, grad_turned)
            grad_v[keys, :] += dot(tile.astype(BF16), grad_low)
            score_grads = (tile * (prob_grads - row_inner) * SCALE).astype(BF16)
            grad_k[keys, :] += dot(score_grads, query)
            acc[...] += dot(k_turned_ref[:, keys], score_grads)
            return inside

        lax.fori_loop(0, steps, back_tile, 0)

        normed, inverse = normalise(tile_rows(first_ref, i * PAIR, 0))
        grad_in, grad_gain = denormalise(acc[...].T, normed, inverse, gain_q)
        send_ref[pl.ds(i * PAIR, PAIR), 0:BLOCK, :] = grad_in.astype(BF16).reshape(
            PAIR, BLOCK, HEAD_DIM
        )
        return gain_sum + grad_gain

    gain_out_ref[0:1, :] = lax.fori_loop(0, TILES, query_tile, zero_gain)

    def key_tile(i, gain_sum):
        rows = pl.ds(pl.multiple_of(i * TILE, TILE), TILE)
        normed, inverse = normalise(tile_rows(first_ref, i * PAIR, 1))
        grad_in, grad_gain = denormalise(grad_k[rows, :], normed, inverse, gain_k)
        at = pl.ds(i * PAIR, PAIR)
        send_ref[at, BLOCK : 2 * BLOCK, :] = grad_in.astype(BF16).reshape(PAIR, BLOCK, HEAD_DIM)
        send_ref[at, 2 * BLOCK :, :] = grad_v[rows, :].astype(BF16).reshape(PAIR, BLOCK, HEAD_DIM)
        return gain_sum + grad_gain

    gain_out_ref[1:2, :] = lax.fori_loop(0, TILES, key_tile, zero_gain)


def run_backward(spans, first, second, gains, q_hat, k_hat, k_turned, span_rows, norms, grads):
    return pl.pallas_call(
        backward_kernel,
        in_specs=[SMEM_SPEC] + [VMEM_SPEC] * 11,
        out_specs=[VMEM_SPEC] * 2,
        out_shape=[shape((BLOCKS, 3 * BLOCK, 128), BF16), shape((2, HEAD_DIM), F32)],
        scratch_shapes=[
            pltpu.VMEM((LENGTH, HEAD_DIM), F32),
            pltpu.VMEM((LENGTH, HEAD_DIM), F32),
            pltpu.VMEM((HEAD_DIM, TILE), F32),
        ],
        compiler_params=pltpu.CompilerParams(vmem_limit_bytes=VMEM_LIMIT),
        name="backward",
    )(spans, first, second, gains, q_hat, k_hat, k_turned, span_rows, norms, *grads)


def over_packs(value):
    moved = [value]
    for shift in range(1, PACKS):
        pairs = [(i, (i + shift) % PACKS) for i in range(PACKS)]
        moved.append(lax.ppermute(value, "pack", pairs))
    return moved


def exchange(slab):
    return lax.all_to_all(slab, "seq", split_axis=0, concat_axis=0, tiled=True)


def on_device(
    query_rows, key_rows, value_rows, target_rows, norm_gains, segment_ids, group_labels, mixture
):
    gains = norm_gains.reshape(2, HEAD_DIM)
    first = exchange(pack_rows((query_rows, key_rows), segment_ids, "pack_first"))

    image_hot = segment_ids[0][:, None] == jnp.arange(IMAGES, dtype=I32)[None, :]
    labels = jnp.sum(jnp.where(image_hot, group_labels[0][None, :], 0), 1)[None, :]
    extra = jnp.concatenate(over_packs(labels.astype(F32)), 0)
    second = exchange(pack_rows((value_rows, target_rows), extra, "pack_second"))

    q_hat, k_hat, k_turned, spans, span_rows, norms = run_stats(first, gains)
    send, *grads, counts = run_forward(
        spans, group_labels, mixture, first, second, q_hat, k_hat, span_rows, norms
    )
    back = exchange(send)
    send, gain_part = run_backward(
        spans, first, second, gains, q_hat, k_hat, k_turned, span_rows, norms, grads
    )
    last = exchange(send)
    (attended,) = unpack_rows(back, 1, "unpack_first")
    losses = jnp.sum(back[:, BLOCK : BLOCK + 3, :GROUPS].astype(F32), (0, 1))
    group_total = sum(over_packs(losses))
    group_loss = group_total / (counts[0, :GROUPS] * (HEADS * HEAD_DIM))
    shares = mixture / jnp.sum(mixture)
    raised = shares * jnp.exp(ETA * group_loss)
    new_mixture = raised / jnp.sum(raised)
    grad_gains = sum(over_packs(gain_part)).reshape(2, 1, HEAD_DIM)
    grad_query, grad_key, grad_value = unpack_rows(last, 3, "unpack_last")
    return (attended, grad_query, grad_key, grad_value, grad_gains, new_mixture)


def solution(mesh):
    rows = P("pack", "seq", None)
    gains = P(None, "seq", None)
    return jax.shard_map(
        on_device,
        mesh=mesh,
        in_specs=(rows, rows, rows, rows, gains, P("pack", "seq"), P("pack", None), P()),
        out_specs=(rows, rows, rows, rows, gains, P()),
        check_vma=False,
    )
```

time: 1560 us -> 192 us (0.12)
  the two profiles are of different devices: /device:TPU:1 before, /device:TPU:25 now
where the time goes in v1:
time: 192 us; the launch traced here: 191 us
  Pallas kernels  89.4 us (47%)
  waiting for transfers between devices  61.1 us (32%)
  starting transfers between devices  32.2 us (17%)
  other arithmetic  5.16 us (3%)
  local copies, waits for them, and re-layouts  2.67 us (1%)
    all_to_all x4, waiting for transfers between devices, exchange(): return lax.all_to_all(slab, 'seq', split_axis=0, concat_axis=0, tiled=True)  52.7 us
    pallas_call x1, Pallas kernels, run_backward(): pl.pallas_call(backward_kernel, in_specs=[SMEM_SPEC] + [VMEM_SPEC] * 11,...  33.4 us
    all_to_all x4, starting transfers between devices, exchange(): return lax.all_to_all(slab, 'seq', split_axis=0, concat_axis=0, tiled=True)  25.9 us
    pallas_call x1, Pallas kernels, run_forward(): pl.pallas_call(forward_kernel, in_specs=[SMEM_SPEC] * 3 + [VMEM_SPEC] * 6...  20.8 us
    pallas_call x1, Pallas kernels, run_stats(): pl.pallas_call(stats_kernel, in_specs=[VMEM_SPEC, VMEM_SPEC], out_specs=[...  20.1 us
    ppermute x9, waiting for transfers between devices, over_packs(): moved.append(lax.ppermute(value, 'pack', pairs))  8.31 us
    pallas_call x2, Pallas kernels, pack_rows(): pl.pallas_call(pack_kernel, in_specs=[ANY_SPEC] * len(rows) + [VMEM_SPEC]...  8.28 us
    pallas_call x2, Pallas kernels, unpack_rows(): pl.pallas_call(unpack_kernel, in_specs=[VMEM_SPEC], out_specs=[ANY_SPEC]...  6.86 us
  transfers between devices with their start and end apart: 13, of which 11 were waited for; matrix products, arithmetic and copies ran while one was open for 3% of the time, Pallas kernels for 31%

profile of v1, /device:TPU:25, one launch (start us, length us, event | category | flops | bytes accessed | tf_op | source)
XLA Modules:
  0.0 191.2 jit_solution(12142793317207347710)
XLA Ops:
  0.6 4.1 %pack_first.1 = bf16[32,272,128]{2,1,0:T(8,128)(2,1)} custom-call(bf16[1,128,4096]{2,1,0:T(8,128)(2,1)} %refs_0_.2, bf16[1,128,4096]{2,1,0:T(8,128)(2,1)} %refs_1_.2, s32[1,128]{1,0:T(1,128)} %refs_2_.1), custom_call_target="tpu_custom_call" | custom-call | tf_op jit(solution)/shard_map/pack_first/pallas_call | solution.py:72
  4.8 8.6 %all-to-all-start = ((bf16[32,272,128]{2,1,0:T(8,128)(2,1)}), bf16[32,272,128]{2,1,0:T(8,128)(2,1)S(1)}, u32[]{:S(2)}, u32[]{:S(2)}) async-start(bf16[32,272,128]{2,1,0:T(8,128)(2,1)} %pack_first.1), calls=%async_computation | async-start | bytes 4456448 | tf_op jit(solution)/shard_map/all_to_all | solution.py:450
  13.6 2.2 %collective-permute-start.1 = (f32[1,128]{1,0:T(1,128)S(1)}, f32[1,128]{1,0:T(1,128)S(1)}, u32[]{:S(2)}, u32[]{:S(2)}) collective-permute-start(f32[1,128]{1,0:T(1,128)S(1)} %convert_bitcast_fusion), channel_id=1, source_target_pairs={{0,64},{32,96},{64,0},{96,32},{1,65},{33,97},{65,1},{97,33},{2,66}... | collective-permute-start | bytes 1544 | tf_op jit(solution)/shard_map/ppermute | solution.py:445
  16.3 1.3 collective-permute-done.1
  17.6 2.2 %collective-permute-done.2 = f32[1,128]{1,0:T(1,128)S(1)} collective-permute-done((f32[1,128]{1,0:T(1,128)S(1)}, f32[1,128]{1,0:T(1,128)S(1)}, u32[]{:S(2)}, u32[]{:S(2)}) %collective-permute-start.2) | collective-permute-done | bytes 544 | tf_op jit(solution)/shard_map/ppermute | solution.py:445
  19.7 0.6 pad_maximum_fusion.refs_2_
  20.3 4.1 %pack_second.1 = bf16[32,272,128]{2,1,0:T(8,128)(2,1)} custom-call(bf16[1,128,4096]{2,1,0:T(8,128)(2,1)} %refs_0_.3, bf16[1,128,4096]{2,1,0:T(8,128)(2,1)} %refs_1_.3, f32[4,128]{1,0:T(4,128)} %pad_maximum_fusion.refs_2_), custom_call_target="tpu_custom_call" | custom-call | tf_op jit(solution)/shard_map/pack_second/pallas_call | solution.py:72
  24.5 18.6 %all-to-all-done.recv_ref.seg_ref.first_ref = bf16[32,272,128]{2,1,0:T(8,128)(2,1)S(1)} async-done(((bf16[32,272,128]{2,1,0:T(8,128)(2,1)}), bf16[32,272,128]{2,1,0:T(8,128)(2,1)S(1)}, u32[]{:S(2)}, u32[]{:S(2)}) %all-to-all-start) | async-done | bytes 2228256 | tf_op jit(solution)/shard_map/all_to_all | solution.py:450
  43.1 5.3 %all-to-all-start.1 = ((bf16[32,272,128]{2,1,0:T(8,128)(2,1)}), bf16[32,272,128]{2,1,0:T(8,128)(2,1)}, u32[]{:S(2)}, u32[]{:S(2)}) async-start(bf16[32,272,128]{2,1,0:T(8,128)(2,1)} %pack_second.1), calls=%async_computation.1 | async-start | bytes 4456448 | tf_op jit(solution)/shard_map/all_to_all | solution.py:450
  48.4 20.1 %score_stats.1 = (bf16[4096,128]{1,0:T(8,128)(2,1)}, bf16[4096,128]{1,0:T(8,128)(2,1)}, bf16[128,4096]{1,0:T(8,128)(2,1)}, s32[2,8]{1,0:T(2,128)}, s32[8,2,512]{2,1,0:T(2,128)}, /*index=5*/f32[8,2,512]{2,1,0:T(2,128)}) custom-call(bf16[32,272,128]{2,1,0:T(8,128)(2,1)} %copy-done, f32[2,128]{1,0:T(2,128)} %bitcast.13), custom_call_target="tpu_custom_call" | custom-call | tf_op jit(solution)/shard_map/score_stats/pallas_call | solution.py:224
  68.5 9.7 %all-to-all-done.1.recv_ref = bf16[32,272,128]{2,1,0:T(8,128)(2,1)} async-done(((bf16[32,272,128]{2,1,0:T(8,128)(2,1)}), bf16[32,272,128]{2,1,0:T(8,128)(2,1)}, u32[]{:S(2)}, u32[]{:S(2)}) %all-to-all-start.1) | async-done | bytes 2228256 | tf_op jit(solution)/shard_map/all_to_all | solution.py:450
  78.3 20.8 %forward.1 = (bf16[32,144,128]{2,1,0:T(8,128)(2,1)}, bf16[4096,128]{1,0:T(8,128)(2,1)}, bf16[128,4096]{1,0:T(8,128)(2,1)}, f32[8,1,512]{2,1,0:T(1,128)}, f32[1,128]{1,0:T(1,128)}) custom-call(s32[2,8]{1,0:T(2,128)} %get-tuple-element.22.span_ref, s32[1,16]{1,0:T(1,128)} %labels_ref.1, f32[8]{0:T(128)} %mixture_ref.1, bf16[32,272,128]{2,1,0:T(8,128)(2,1)} %copy-done, ...), custom_call_target="tpu_custom_call" | custom-call | tf_op jit(solution)/shard_map/forward/pallas_call | solution.py:343
  99.0 4.5 %all-to-all-start.2 = ((bf16[32,144,128]{2,1,0:T(8,128)(2,1)}), bf16[32,144,128]{2,1,0:T(8,128)(2,1)S(1)}, u32[]{:S(2)}, u32[]{:S(2)}) async-start(bf16[32,144,128]{2,1,0:T(8,128)(2,1)} %get-tuple-element.27), calls=%async_computation.2 | async-start | bytes 2359296 | tf_op jit(solution)/shard_map/all_to_all | solution.py:450
  103.5 33.4 %backward.1 = (bf16[32,384,128]{2,1,0:T(8,128)(2,1)}, f32[2,128]{1,0:T(2,128)}) custom-call(s32[2,8]{1,0:T(2,128)} %get-tuple-element.22.span_ref, bf16[32,272,128]{2,1,0:T(8,128)(2,1)} %copy-done, bf16[32,272,128]{2,1,0:T(8,128)(2,1)} %all-to-all-done.1.recv_ref, f32[2,128]{1,0:T(2,128)} %bitcast.14, bf16[4096,128]{1,0:T(8,128)(2,1)} %get-tuple-element.23.q_hat_ref, ...), custom_call_target="tpu_custom_call" | custom-call | tf_op jit(solution)/shard_map/backward/pallas_call | solution.py:426
  137.0 1.0 copy-done.2
  138.0 7.5 %all-to-all-start.3 = ((bf16[32,384,128]{2,1,0:T(8,128)(2,1)}), bf16[32,384,128]{2,1,0:T(8,128)(2,1)S(1)}, u32[]{:S(2)}, u32[]{:S(2)}) async-start(bf16[32,384,128]{2,1,0:T(8,128)(2,1)} %get-tuple-element.32), calls=%async_computation.3 | async-start | bytes 6291456 | tf_op jit(solution)/shard_map/all_to_all | solution.py:450
  145.7 1.4 collective-permute-start.5
  147.0 0.6 reduce_sum.37
  147.6 0.6 collective-permute-done.3
  148.3 1.3 collective-permute-done.4
  149.6 1.1 collective-permute-done.5
  151.2 0.9 convert_reduce_fusion
  152.1 1.5 collective-permute-start.6
  153.7 0.9 collective-permute-start.7
  154.6 2.5 %unpack_first.1 = bf16[1,128,4096]{2,1,0:T(8,128)(2,1)} custom-call(bf16[32,144,128]{2,1,0:T(8,128)(2,1)} %copy-done.2), custom_call_target="tpu_custom_call" | custom-call | tf_op jit(solution)/shard_map/unpack_first/pallas_call | solution.py:100
  157.1 0.8 collective-permute-done.7
  157.8 0.6 collective-permute-done.8
  158.5 1.3 fusion
  159.7 1.2 broadcast_divide_fusion
  160.9 24.4 %all-to-all-done.3.in_ref = bf16[32,384,128]{2,1,0:T(8,128)(2,1)S(1)} async-done(((bf16[32,384,128]{2,1,0:T(8,128)(2,1)}), bf16[32,384,128]{2,1,0:T(8,128)(2,1)S(1)}, u32[]{:S(2)}, u32[]{:S(2)}) %all-to-all-start.3) | async-done | bytes 3145760 | tf_op jit(solution)/shard_map/all_to_all | solution.py:450
  185.2 1.6 copy-done.1
  186.9 4.4 %unpack_last.1 = (bf16[1,128,4096]{2,1,0:T(8,128)(2,1)}, bf16[1,128,4096]{2,1,0:T(8,128)(2,1)}, bf16[1,128,4096]{2,1,0:T(8,128)(2,1)}) custom-call(bf16[32,384,128]{2,1,0:T(8,128)(2,1)} %copy-done.1), custom_call_target="tpu_custom_call" | custom-call | tf_op jit(solution)/shard_map/unpack_last/pallas_call | solution.py:100
  (25 shorter events, 1.4 us)
Async XLA Ops:
  4.8 8.6 %copy-start.5 = (s32[1,128]{1,0:T(1,128)S(1)}, s32[1,128]{1,0:T(1,128)}, u32[]{:S(2)}) copy-start(s32[1,128]{1,0:T(1,128)} %refs_2_.1) | copy-start | bytes 1540
  4.8 8.6 %copy-start.6 = (s32[1,16]{1,0:T(1,128)S(1)}, s32[1,16]{1,0:T(1,128)}, u32[]{:S(2)}) copy-start(s32[1,16]{1,0:T(1,128)} %labels_ref.1) | copy-start | bytes 196
  4.8 38.3 %all-to-all-start = ((bf16[32,272,128]{2,1,0:T(8,128)(2,1)}), bf16[32,272,128]{2,1,0:T(8,128)(2,1)S(1)}, u32[]{:S(2)}, u32[]{:S(2)}) async-start(bf16[32,272,128]{2,1,0:T(8,128)(2,1)} %pack_first.1), calls=%async_computation | async-start | bytes 4456448 | tf_op jit(solution)/shard_map/all_to_all | solution.py:450
  13.5 2.7 %collective-permute-start = (f32[1,128]{1,0:T(1,128)S(1)}, f32[1,128]{1,0:T(1,128)S(1)}, u32[]{:S(2)}, u32[]{:S(2)}) collective-permute-start(f32[1,128]{1,0:T(1,128)S(1)} %convert_bitcast_fusion), channel_id=1, source_target_pairs={{0,32},{32,64},{64,96},{96,0},{1,33},{33,65},{65,97},{97,1},{2,34}... | collective-permute-start | bytes 1544 | tf_op jit(solution)/shard_map/ppermute | solution.py:445
  13.6 4.0 %collective-permute-start.1 = (f32[1,128]{1,0:T(1,128)S(1)}, f32[1,128]{1,0:T(1,128)S(1)}, u32[]{:S(2)}, u32[]{:S(2)}) collective-permute-start(f32[1,128]{1,0:T(1,128)S(1)} %convert_bitcast_fusion), channel_id=1, source_target_pairs={{0,64},{32,96},{64,0},{96,32},{1,65},{33,97},{65,1},{97,33},{2,66}... | collective-permute-start | bytes 1544 | tf_op jit(solution)/shard_map/ppermute | solution.py:445
  15.8 3.9 %collective-permute-start.2 = (f32[1,128]{1,0:T(1,128)S(1)}, f32[1,128]{1,0:T(1,128)S(1)}, u32[]{:S(2)}, u32[]{:S(2)}) collective-permute-start(f32[1,128]{1,0:T(1,128)S(1)} %convert_bitcast_fusion), channel_id=1, source_target_pairs={{0,96},{32,0},{64,32},{96,64},{1,97},{33,1},{65,33},{97,65},{2,98}... | collective-permute-start | bytes 1544 | tf_op jit(solution)/shard_map/ppermute | solution.py:445
  43.1 5.3 %copy-start = (bf16[32,272,128]{2,1,0:T(8,128)(2,1)}, bf16[32,272,128]{2,1,0:T(8,128)(2,1)S(1)}, u32[]{:S(2)}) copy-start(bf16[32,272,128]{2,1,0:T(8,128)(2,1)S(1)} %all-to-all-done.recv_ref.seg_ref.first_ref) | copy-start | bytes 6684676
  43.1 35.2 %all-to-all-start.1 = ((bf16[32,272,128]{2,1,0:T(8,128)(2,1)}), bf16[32,272,128]{2,1,0:T(8,128)(2,1)}, u32[]{:S(2)}, u32[]{:S(2)}) async-start(bf16[32,272,128]{2,1,0:T(8,128)(2,1)} %pack_second.1), calls=%async_computation.1 | async-start | bytes 4456448 | tf_op jit(solution)/shard_map/all_to_all | solution.py:450
  99.0 37.9 %all-to-all-start.2 = ((bf16[32,144,128]{2,1,0:T(8,128)(2,1)}), bf16[32,144,128]{2,1,0:T(8,128)(2,1)S(1)}, u32[]{:S(2)}, u32[]{:S(2)}) async-start(bf16[32,144,128]{2,1,0:T(8,128)(2,1)} %get-tuple-element.27), calls=%async_computation.2 | async-start | bytes 2359296 | tf_op jit(solution)/shard_map/all_to_all | solution.py:450
  136.9 1.0 copy-start.2
  137.0 8.5 %copy-start.4 = (f32[2,128]{1,0:T(2,128)S(1)}, f32[2,128]{1,0:T(2,128)}, u32[]{:S(2)}) copy-start(f32[2,128]{1,0:T(2,128)} %get-tuple-element.36) | copy-start | bytes 3076
  137.0 10.1 %copy-start.3 = (f32[8]{0:T(128)S(1)}, f32[8]{0:T(128)}, u32[]{:S(2)}) copy-start(f32[8]{0:T(128)} %mixture_ref.1) | copy-start | bytes 100
  138.0 47.3 %all-to-all-start.3 = ((bf16[32,384,128]{2,1,0:T(8,128)(2,1)}), bf16[32,384,128]{2,1,0:T(8,128)(2,1)S(1)}, u32[]{:S(2)}, u32[]{:S(2)}) async-start(bf16[32,384,128]{2,1,0:T(8,128)(2,1)} %get-tuple-element.32), calls=%async_computation.3 | async-start | bytes 6291456 | tf_op jit(solution)/shard_map/all_to_all | solution.py:450
  145.5 13.0 %copy-start.7 = (f32[1,128]{1,0:T(1,128)S(1)}, f32[1,128]{1,0:T(1,128)}, u32[]{:S(2)}) copy-start(f32[1,128]{1,0:T(1,128)} %get-tuple-element.37) | copy-start | bytes 1540
  145.5 2.8 %collective-permute-start.3 = (f32[2,128]{1,0:T(2,128)S(1)}, f32[2,128]{1,0:T(2,128)S(1)}, u32[]{:S(2)}, u32[]{:S(2)}) collective-permute-start(f32[2,128]{1,0:T(2,128)S(1)} %copy-done.4), channel_id=1, source_target_pairs={{0,32},{32,64},{64,96},{96,0},{1,33},{33,65},{65,97},{97,1},{2,34}... | collective-permute-start | bytes 3080 | tf_op jit(solution)/shard_map/ppermute | solution.py:445
  145.6 4.0 %collective-permute-start.4 = (f32[2,128]{1,0:T(2,128)S(1)}, f32[2,128]{1,0:T(2,128)S(1)}, u32[]{:S(2)}, u32[]{:S(2)}) collective-permute-start(f32[2,128]{1,0:T(2,128)S(1)} %copy-done.4), channel_id=1, source_target_pairs={{0,64},{32,96},{64,0},{96,32},{1,65},{33,97},{65,1},{97,33},{2,66}... | collective-permute-start | bytes 3080 | tf_op jit(solution)/shard_map/ppermute | solution.py:445
  145.7 5.0 %collective-permute-start.5 = (f32[2,128]{1,0:T(2,128)S(1)}, f32[2,128]{1,0:T(2,128)S(1)}, u32[]{:S(2)}, u32[]{:S(2)}) collective-permute-start(f32[2,128]{1,0:T(2,128)S(1)} %copy-done.4), channel_id=1, source_target_pairs={{0,96},{32,0},{64,32},{96,64},{1,97},{33,1},{65,33},{97,65},{2,98}... | collective-permute-start | bytes 3080 | tf_op jit(solution)/shard_map/ppermute | solution.py:445
  152.1 4.9 %collective-permute-start.6 = (f32[8]{0:T(128)S(1)}, f32[8]{0:T(128)S(1)}, u32[]{:S(2)}, u32[]{:S(2)}) collective-permute-start(f32[8]{0:T(128)S(1)} %convert_reduce_fusion), channel_id=1, source_target_pairs={{0,32},{32,64},{64,96},{96,0},{1,33},{33,65},{65,97},{97,1},{2,34}... | collective-permute-start | bytes 104 | tf_op jit(solution)/shard_map/ppermute | solution.py:445
  153.7 4.2 %collective-permute-start.7 = (f32[8]{0:T(128)S(1)}, f32[8]{0:T(128)S(1)}, u32[]{:S(2)}, u32[]{:S(2)}) collective-permute-start(f32[8]{0:T(128)S(1)} %convert_reduce_fusion), channel_id=1, source_target_pairs={{0,64},{32,96},{64,0},{96,32},{1,65},{33,97},{65,1},{97,33},{2,66}... | collective-permute-start | bytes 104 | tf_op jit(solution)/shard_map/ppermute | solution.py:445
  154.6 3.9 %collective-permute-start.8 = (f32[8]{0:T(128)S(1)}, f32[8]{0:T(128)S(1)}, u32[]{:S(2)}, u32[]{:S(2)}) collective-permute-start(f32[8]{0:T(128)S(1)} %convert_reduce_fusion), channel_id=1, source_target_pairs={{0,96},{32,0},{64,32},{96,64},{1,97},{33,1},{65,33},{97,65},{2,98}... | collective-permute-start | bytes 104 | tf_op jit(solution)/shard_map/ppermute | solution.py:445
  185.2 1.6 copy-start.1

commit v2 on v1

v2 whole, which is shorter than its diff:
```python
import functools

import jax
import jax.numpy as jnp
from jax import lax
from jax.experimental import pallas as pl
from jax.experimental.pallas import tpu as pltpu
from jax.sharding import PartitionSpec as P

HEADS = 32
HEAD_DIM = 128
IMAGES = 16
GROUPS = 8
PACKS = 4
LENGTH = 4096

NEG = -1e30
EPS = 1e-06
ETA = 2.0
SCALE = HEAD_DIM ** (-0.5)
EXP_SCALE = SCALE * 1.4426950408889634

BLOCK = 128
BLOCKS = LENGTH // BLOCK
TILE = 256
TILES = LENGTH // TILE
PAIR = TILE // BLOCK
KEYS = 256
STATS_KEYS = 512
FORWARD_UNROLL = 4
BACKWARD_UNROLL = 4
MOST_UNROLL = max(FORWARD_UNROLL, BACKWARD_UNROLL)
MOST_PAIRS = TILES * 10 + MOST_UNROLL
EXTRA = 16
VMEM_LIMIT = 28 * 1024 * 1024

BF16 = jnp.bfloat16
F32 = jnp.float32
I32 = jnp.int32

VMEM_SPEC = pl.BlockSpec(memory_space=pltpu.VMEM)
SMEM_SPEC = pl.BlockSpec(memory_space=pltpu.SMEM)
ANY_SPEC = pl.BlockSpec(memory_space=pl.ANY)


def shape(dims, dtype):
    return jax.ShapeDtypeStruct(dims, dtype)


def head_columns(h):
    return pl.ds(h * HEAD_DIM, HEAD_DIM)


def pack_kernel(count, *refs):
    row_refs, extra_refs, (out_ref, sems) = refs[:count], refs[count:-2], refs[-2:]
    copies = []
    for n, ref in enumerate(row_refs):
        for h in range(HEADS):
            copy = pltpu.make_async_copy(
                ref.at[0, :, head_columns(h)],
                out_ref.at[h, pl.ds(n * BLOCK, BLOCK), :],
                sems.at[n, h],
            )
            copy.start()
            copies.append(copy)
    for extra_ref in extra_refs:
        tile = jnp.broadcast_to(extra_ref[...].astype(F32), (EXTRA, 128)).astype(BF16)
        out_ref[:, len(row_refs) * BLOCK :, :] = jnp.broadcast_to(tile[None], (HEADS, EXTRA, 128))
    for copy in copies:
        copy.wait()


def pack_rows(rows, extra, name):
    extras = () if extra is None else (extra,)
    return pl.pallas_call(
        functools.partial(pack_kernel, len(rows)),
        in_specs=[ANY_SPEC] * len(rows) + [VMEM_SPEC] * len(extras),
        out_specs=VMEM_SPEC,
        out_shape=shape((HEADS, len(rows) * BLOCK + EXTRA * len(extras), 128), BF16),
        scratch_shapes=[pltpu.SemaphoreType.DMA((len(rows), HEADS))],
        compiler_params=pltpu.CompilerParams(vmem_limit_bytes=VMEM_LIMIT),
        name=name,
    )(*rows, *extras)


def unpack_kernel(in_ref, *refs):
    *row_refs, sems = refs
    copies = []
    for n, ref in enumerate(row_refs):
        for h in range(HEADS):
            copy = pltpu.make_async_copy(
                in_ref.at[h, pl.ds(n * BLOCK, BLOCK), :],
                ref.at[0, :, head_columns(h)],
                sems.at[n, h],
            )
            copy.start()
            copies.append(copy)
    for copy in copies:
        copy.wait()


def unpack_rows(slab, count, name):
    return pl.pallas_call(
        unpack_kernel,
        in_specs=[VMEM_SPEC],
        out_specs=[ANY_SPEC] * count,
        out_shape=[shape((1, BLOCK, HEADS * HEAD_DIM), BF16)] * count,
        scratch_shapes=[pltpu.SemaphoreType.DMA((count, HEADS))],
        compiler_params=pltpu.CompilerParams(vmem_limit_bytes=VMEM_LIMIT),
        name=name,
    )(slab)


def dot(a, b, contract=((1,), (0,))):
    return lax.dot_general(a, b, (contract, ((), ())), preferred_element_type=F32)


def tile_rows(ref, i, part, size=TILE):
    blocks = size // BLOCK
    return ref[pl.ds(i, blocks), part * BLOCK : (part + 1) * BLOCK, :].reshape(size, HEAD_DIM)


def tile_at(i, size=TILE):
    return pl.ds(pl.multiple_of(i * size, size), size)


def mean_down(values):
    return jnp.sum(values, 0, keepdims=True) * (1.0 / HEAD_DIM)


def block_row(b):
    return b // PAIR, slice((b % PAIR) * BLOCK, (b % PAIR + 1) * BLOCK)


def group_sums(group, values):
    lane = lax.broadcasted_iota(I32, (1, 128), 1)
    sums = jnp.zeros((1, 128), F32)
    for g in range(GROUPS):
        part = jnp.sum(jnp.where(group == float(g), values, 0.0), 0, keepdims=True)
        sums = jnp.where(lane == g, jnp.sum(part, 1, keepdims=True), sums)
    return sums


def groups_kernel(labels_ref, seg_ref, group_ref, counts_ref, span_ref, pair_ref, span_rows_ref, starts):
    seg_all = seg_ref[:, 0, :].astype(F32)
    group = jnp.zeros((BLOCKS, 128), F32)
    for s in range(IMAGES):
        group = jnp.where(seg_all == float(s), labels_ref[0, s].astype(F32), group)
    group_ref[...] = group
    counts_ref[...] = group_sums(group, jnp.ones((BLOCKS, 128), F32))

    for s in range(IMAGES + 1):
        starts[s] = jnp.sum((seg_all < float(s)).astype(F32)).astype(I32)
    first = jnp.zeros((BLOCKS, 128), I32)
    count = jnp.zeros((BLOCKS, 128), I32)
    for s in range(IMAGES):
        here = seg_all == float(s)
        first = jnp.where(here, starts[s], first)
        count = jnp.where(here, starts[s + 1] - starts[s], count)
    for b in range(BLOCKS):
        tile, at = block_row(b)
        span_rows_ref[tile, 0:1, at] = first[b : b + 1, :]
        span_rows_ref[tile, 1:2, at] = count[b : b + 1, :]

    def span(i, total):
        low, high = jnp.int32(0), jnp.int32(LENGTH)
        for s in range(1, IMAGES):
            low = jnp.where(starts[s] <= i * TILE, starts[s], low)
        for s in range(IMAGES - 1, 0, -1):
            high = jnp.where(starts[s] > i * TILE + TILE - 1, starts[s], high)
        low = (low // BLOCK) * BLOCK
        span_ref[0, i] = low
        span_ref[1, i] = high
        steps = (high - low + KEYS - 1) // KEYS
        low = jnp.minimum(low, LENGTH - steps * KEYS)

        def add(j, carry):
            pair_ref[0, total + j] = i
            pair_ref[1, total + j] = low + j * KEYS
            pair_ref[2, total + j] = low + j * KEYS
            return carry

        lax.fori_loop(0, steps, add, 0)
        return total + steps

    total = lax.fori_loop(0, TILES, span, jnp.int32(0))
    span_ref[0, TILES] = total
    span_ref[1, TILES] = total
    for u in range(MOST_UNROLL):
        pair_ref[0, total + u] = 0
        pair_ref[1, total + u] = 0
        pair_ref[2, total + u] = -(1 << 20)


def run_groups(labels, received):
    return pl.pallas_call(
        groups_kernel,
        grid=(1,),
        in_specs=[SMEM_SPEC, pl.BlockSpec((BLOCKS, EXTRA, 128), lambda i: (0, 2 * BLOCK // EXTRA, 0))],
        out_specs=[VMEM_SPEC, VMEM_SPEC, SMEM_SPEC, SMEM_SPEC, VMEM_SPEC],
        out_shape=[
            shape((BLOCKS, 128), F32),
            shape((1, 128), F32),
            shape((2, TILES + 1), I32),
            shape((3, MOST_PAIRS), I32),
            shape((TILES, 2, TILE), I32),
        ],
        scratch_shapes=[pltpu.SMEM((IMAGES + 1,), I32)],
        name="row_groups",
    )(labels, received)


def key_mask(span_rows_ref, i, start, step):
    first = span_rows_ref[i, 0:1, :] - start
    count = span_rows_ref[i, 1:2, :]
    row = lax.broadcasted_iota(I32, (step, TILE), 0)
    return (row - first).astype(jnp.uint32) < count.astype(jnp.uint32)


def stats_kernel(
    span_ref, recv_ref, gains_ref, span_rows_ref,
    q_hat_ref, k_hat_ref, q_turned_ref, k_turned_ref, raw_q_ref, raw_k_ref, moments_ref, norm_ref,
    scores,
):
    gains = jnp.concatenate([gains_ref[...], jnp.zeros((6, HEAD_DIM), F32)], 0).T

    def prepare(i, carry):
        rows = tile_at(i)
        outs = ((q_hat_ref, q_turned_ref, raw_q_ref), (k_hat_ref, k_turned_ref, raw_k_ref))
        for n, (hat_ref, turned_ref, raw_ref) in enumerate(outs):
            raw = tile_rows(recv_ref, i * PAIR, n).T
            raw_ref[:, rows] = raw
            values = raw.astype(F32)
            mean = mean_down(values)
            centre = values - mean
            inverse = lax.rsqrt(mean_down(centre * centre) + EPS)
            moments_ref[i, 2 * n : 2 * n + 1, :] = mean
            moments_ref[i, 2 * n + 1 : 2 * n + 2, :] = inverse
            hat = (centre * inverse * gains[:, n : n + 1]).astype(BF16)
            turned_ref[:, rows] = hat
            hat_ref[rows, :] = hat.T
        return carry

    lax.fori_loop(0, TILES, prepare, 0)

    step = STATS_KEYS

    def query_tile(i, carry):
        low, high = span_ref[0, i], span_ref[1, i]
        steps = (high - low + step - 1) // step
        start = jnp.minimum(low, LENGTH - steps * step)
        query = q_turned_ref[:, tile_at(i)]

        def score_tile(j, top):
            at = pl.multiple_of(start + j * step, BLOCK)
            tile = dot(k_hat_ref[pl.ds(at, step), :], query)
            tile = jnp.where(key_mask(span_rows_ref, i, at, step), tile, NEG)
            scores[j] = tile
            return jnp.maximum(top, jnp.max(tile.reshape(step // 8, 8, TILE), 0))

        top = lax.fori_loop(0, steps, score_tile, jnp.full((8, TILE), NEG, F32))
        top = jnp.max(top, 0, keepdims=True) * EXP_SCALE

        def exp_tile(j, total):
            tile = jnp.exp2(scores[j] * EXP_SCALE - top)
            return total + jnp.sum(tile.reshape(step // 8, 8, TILE), 0)

        total = lax.fori_loop(0, steps, exp_tile, jnp.zeros((8, TILE), F32))
        norm_ref[i, 0:1, :] = top
        norm_ref[i, 1:2, :] = 1.0 / jnp.sum(total, 0, keepdims=True)
        return carry

    lax.fori_loop(0, TILES, query_tile, 0)


def run_stats(spans, received, gains, span_rows):
    most = 2 * 1024 // STATS_KEYS + TILE // STATS_KEYS + 2
    return pl.pallas_call(
        stats_kernel,
        in_specs=[SMEM_SPEC] + [VMEM_SPEC] * 3,
        out_specs=[VMEM_SPEC] * 8,
        out_shape=[
            shape((LENGTH, HEAD_DIM), BF16),
            shape((LENGTH, HEAD_DIM), BF16),
            shape((HEAD_DIM, LENGTH), BF16),
            shape((HEAD_DIM, LENGTH), BF16),
            shape((HEAD_DIM, LENGTH), BF16),
            shape((HEAD_DIM, LENGTH), BF16),
            shape((TILES, 4, TILE), F32),
            shape((TILES, 2, TILE), F32),
        ],
        scratch_shapes=[pltpu.VMEM((most, STATS_KEYS, TILE), F32)],
        compiler_params=pltpu.CompilerParams(vmem_limit_bytes=VMEM_LIMIT),
        name="score_stats",
    )(spans, received, gains, span_rows)


def softmax_tile(scores, span_rows_ref, norm_ref, i, mask_at):
    scores = jnp.where(key_mask(span_rows_ref, i, mask_at, KEYS), scores, NEG)
    top, inverse_total = norm_ref[i, 0:1, :], norm_ref[i, 1:2, :]
    return jnp.exp2(scores * EXP_SCALE - top) * inverse_total


def each_pairs(total, unroll, pair_ref, body):
    def some(n, carry):
        pairs = []
        for u in range(unroll):
            p = n * unroll + u
            pairs.append((pair_ref[0, p], pl.multiple_of(pair_ref[1, p], BLOCK), pair_ref[2, p]))
        body(pairs)
        return carry

    lax.fori_loop(0, (total + unroll - 1) // unroll, some, 0)


def forward_kernel(
    span_ref, pair_ref, mixture_ref,
    counts_ref, group_ref, recv_ref, q_turned_ref, k_hat_ref, span_rows_ref, norm_ref,
    send_ref, grad_ref, grad_turned_ref, inner_ref,
    coef_rows, loss_rows, v_turned, out_turned,
):
    def prepare(i, carry):
        v_turned[:, tile_at(i)] = tile_rows(recv_ref, i * PAIR, 0).T
        out_turned[i] = jnp.zeros((HEAD_DIM, TILE), F32)
        return carry

    lax.fori_loop(0, TILES, prepare, 0)

    group = group_ref[...]
    counts = jnp.sum(counts_ref[...], 0, keepdims=True)
    total_mix = mixture_ref[0]
    for g in range(1, GROUPS):
        total_mix = total_mix + mixture_ref[g]
    coef = jnp.zeros((BLOCKS, 128), F32)
    for g in range(GROUPS):
        share = jnp.full((1, 1), mixture_ref[g], F32) / total_mix
        share = share / (counts[:, g : g + 1] * (HEADS * HEAD_DIM))
        coef = jnp.where(group == float(g), share, coef)
    for b in range(BLOCKS):
        tile, at = block_row(b)
        coef_rows[tile, 0:1, at] = coef[b : b + 1, :]

    def add_pairs(pairs):
        tiles = [
            dot(k_hat_ref[pl.ds(at, KEYS), :], q_turned_ref[:, tile_at(i)]) for i, at, _ in pairs
        ]
        tiles = [
            softmax_tile(tile, span_rows_ref, norm_ref, i, mask_at).astype(BF16)
            for tile, (i, _, mask_at) in zip(tiles, pairs)
        ]
        tiles = [dot(v_turned[:, pl.ds(at, KEYS)], tile) for tile, (_, at, _) in zip(tiles, pairs)]
        for tile, (i, _, _) in zip(tiles, pairs):
            out_turned[i] += tile

    each_pairs(span_ref[0, TILES], FORWARD_UNROLL, pair_ref, add_pairs)

    def finish(i, carry):
        rows = tile_at(i)
        head_out = out_turned[i]
        misfit = head_out - tile_rows(recv_ref, i * PAIR, 1).T.astype(F32)
        loss_rows[i, 0:1, :] = 0.5 * jnp.sum(misfit * misfit, 0, keepdims=True)
        grad_out = coef_rows[i, 0:1, :] * misfit
        inner_ref[i, 0:1, :] = jnp.sum(grad_out * head_out, 0, keepdims=True)
        grad_turned = grad_out.astype(BF16)
        grad_turned_ref[:, rows] = grad_turned
        grad_ref[rows, :] = grad_turned.T
        send_ref[pl.ds(i * PAIR, PAIR), 0:BLOCK, :] = head_out.astype(BF16).T.reshape(
            PAIR, BLOCK, HEAD_DIM
        )
        return carry

    lax.fori_loop(0, TILES, finish, 0)

    rows = [block_row(b) for b in range(BLOCKS)]
    losses = jnp.concatenate([loss_rows[tile, 0:1, at] for tile, at in rows], 0)
    loss_row = group_sums(group, losses)
    high = loss_row.astype(BF16)
    left = loss_row - high.astype(F32)
    middle = left.astype(BF16)
    low = (left - middle.astype(F32)).astype(BF16)
    row = lax.broadcasted_iota(I32, (EXTRA, 128), 0)
    pieces = jnp.zeros((EXTRA, 128), F32)
    for n, piece in enumerate((high, middle, low)):
        pieces = jnp.where(row == n, piece.astype(F32), pieces)
    send_ref[:, BLOCK:, :] = jnp.broadcast_to(pieces.astype(BF16)[None], (BLOCKS, EXTRA, 128))


def run_forward(spans, pairs, mixture, counts, group, second, q_turned, k_hat, span_rows, norms):
    return pl.pallas_call(
        forward_kernel,
        in_specs=[SMEM_SPEC] * 3 + [VMEM_SPEC] * 7,
        out_specs=[VMEM_SPEC] * 4,
        out_shape=[
            shape((BLOCKS, BLOCK + EXTRA, 128), BF16),
            shape((LENGTH, HEAD_DIM), BF16),
            shape((HEAD_DIM, LENGTH), BF16),
            shape((TILES, 1, TILE), F32),
        ],
        scratch_shapes=[
            pltpu.VMEM((TILES, 1, TILE), F32),
            pltpu.VMEM((TILES, 1, TILE), F32),
            pltpu.VMEM((HEAD_DIM, LENGTH), BF16),
            pltpu.VMEM((TILES, HEAD_DIM, TILE), F32),
        ],
        compiler_params=pltpu.CompilerParams(vmem_limit_bytes=VMEM_LIMIT),
        name="forward",
    )(spans, pairs, mixture, counts, group, second, q_turned, k_hat, span_rows, norms)


def backward_kernel(
    span_ref, pair_ref,
    recv_ref, gains_ref, q_hat_ref, k_hat_ref, q_turned_ref, k_turned_ref, raw_q_ref, raw_k_ref,
    moments_ref, span_rows_ref, norm_ref, grad_ref, grad_turned_ref, inner_ref,
    send_ref, gain_out_ref,
    grad_q, grad_k, grad_v,
):
    def clear(i, carry):
        grad_q[i] = jnp.zeros((HEAD_DIM, TILE), F32)
        grad_k[tile_at(i), :] = jnp.zeros((TILE, HEAD_DIM), F32)
        grad_v[tile_at(i), :] = jnp.zeros((TILE, HEAD_DIM), F32)
        return carry

    lax.fori_loop(0, TILES, clear, 0)

    def add_pairs(pairs):
        tiles = [
            dot(k_hat_ref[pl.ds(at, KEYS), :], q_turned_ref[:, tile_at(i)]) for i, at, _ in pairs
        ]
        prob_grads = [
            dot(tile_rows(recv_ref, at // BLOCK, 0, KEYS), grad_turned_ref[:, tile_at(i)])
            for i, at, _ in pairs
        ]
        tiles = [
            softmax_tile(tile, span_rows_ref, norm_ref, i, mask_at)
            for tile, (i, _, mask_at) in zip(tiles, pairs)
        ]
        values = [
            dot(tile.astype(BF16), grad_ref[tile_at(i), :]) for tile, (i, _, _) in zip(tiles, pairs)
        ]
        tiles = [
            (tile * (prob - inner_ref[i, 0:1, :]) * SCALE).astype(BF16)
            for tile, prob, (i, _, _) in zip(tiles, prob_grads, pairs)
        ]
        keys = [dot(tile, q_hat_ref[tile_at(i), :]) for tile, (i, _, _) in zip(tiles, pairs)]
        queries = [
            dot(k_turned_ref[:, pl.ds(at, KEYS)], tile) for tile, (_, at, _) in zip(tiles, pairs)
        ]
        for value, key, query, (i, at, _) in zip(values, keys, queries, pairs):
            grad_v[pl.ds(at, KEYS), :] += value
            grad_k[pl.ds(at, KEYS), :] += key
            grad_q[i] += query

    each_pairs(span_ref[0, TILES], BACKWARD_UNROLL, pair_ref, add_pairs)

    gains = jnp.concatenate([gains_ref[...], jnp.zeros((6, HEAD_DIM), F32)], 0).T

    def norm_backward(i, n, grad_hat, raw_ref):
        mean = moments_ref[i, 2 * n : 2 * n + 1, :]
        inverse = moments_ref[i, 2 * n + 1 : 2 * n + 2, :]
        normed = (raw_ref[:, tile_at(i)].astype(F32) - mean) * inverse
        grad_normed = grad_hat * gains[:, n : n + 1]
        inner = mean_down(grad_normed * normed)
        grad_in = inverse * (grad_normed - mean_down(grad_normed) - normed * inner)
        send_ref[pl.ds(i * PAIR, PAIR), n * BLOCK : (n + 1) * BLOCK, :] = grad_in.astype(
            BF16
        ).T.reshape(PAIR, BLOCK, HEAD_DIM)
        grad_gain = grad_hat * normed
        return sum(grad_gain[:, c : c + 128] for c in range(0, TILE, 128))

    def finish(i, gain_sums):
        gain_q, gain_k = gain_sums
        gain_q = gain_q + norm_backward(i, 0, grad_q[i], raw_q_ref)
        gain_k = gain_k + norm_backward(i, 1, grad_k[tile_at(i), :].T, raw_k_ref)
        send_ref[pl.ds(i * PAIR, PAIR), 2 * BLOCK :, :] = (
            grad_v[tile_at(i), :].astype(BF16).reshape(PAIR, BLOCK, HEAD_DIM)
        )
        return gain_q, gain_k

    zero = jnp.zeros((HEAD_DIM, 128), F32)
    gain_q, gain_k = lax.fori_loop(0, TILES, finish, (zero, zero))
    gain_out_ref[0:1, :] = jnp.sum(gain_q.T, 0, keepdims=True)
    gain_out_ref[1:2, :] = jnp.sum(gain_k.T, 0, keepdims=True)


def run_backward(spans, pairs, *arrays):
    return pl.pallas_call(
        backward_kernel,
        in_specs=[SMEM_SPEC] * 2 + [VMEM_SPEC] * len(arrays),
        out_specs=[VMEM_SPEC] * 2,
        out_shape=[shape((BLOCKS, 3 * BLOCK, 128), BF16), shape((2, HEAD_DIM), F32)],
        scratch_shapes=[
            pltpu.VMEM((TILES, HEAD_DIM, TILE), F32),
            pltpu.VMEM((LENGTH, HEAD_DIM), F32),
            pltpu.VMEM((LENGTH, HEAD_DIM), F32),
        ],
        compiler_params=pltpu.CompilerParams(vmem_limit_bytes=VMEM_LIMIT),
        name="backward",
    )(spans, pairs, *arrays)


def over_packs(value):
    moved = [value]
    for shift in range(1, PACKS):
        pairs = [(i, (i + shift) % PACKS) for i in range(PACKS)]
        moved.append(lax.ppermute(value, "pack", pairs))
    return moved


def exchange(slab):
    return lax.all_to_all(slab, "seq", split_axis=0, concat_axis=0, tiled=True)


def on_device(
    query_rows, key_rows, value_rows, target_rows, norm_gains, segment_ids, group_labels, mixture
):
    gains = norm_gains.reshape(2, HEAD_DIM)
    first = exchange(pack_rows((query_rows, key_rows), segment_ids, "pack_first"))
    second = exchange(pack_rows((value_rows, target_rows), None, "pack_second"))

    group, own_counts, spans, pairs, span_rows = run_groups(group_labels, first)
    counts = jnp.concatenate(over_packs(own_counts), 0)
    q_hat, k_hat, q_turned, k_turned, raw_q, raw_k, moments, norms = run_stats(
        spans, first, gains, span_rows
    )
    send, *grads = run_forward(
        spans, pairs, mixture, counts, group, second, q_turned, k_hat, span_rows, norms
    )
    back = exchange(send)
    send, gain_part = run_backward(
        spans, pairs, second, gains, q_hat, k_hat, q_turned, k_turned, raw_q, raw_k,
        moments, span_rows, norms, *grads,
    )
    last = exchange(send)
    (attended,) = unpack_rows(back, 1, "unpack_first")
    losses = jnp.sum(back[:, BLOCK : BLOCK + 3, :GROUPS].astype(F32), (0, 1))
    group_total = sum(over_packs(losses))
    group_loss = group_total / (jnp.sum(counts, 0)[:GROUPS] * (HEADS * HEAD_DIM))
    shares = mixture / jnp.sum(mixture)
    raised = shares * jnp.exp(ETA * group_loss)
    new_mixture = raised / jnp.sum(raised)
    grad_gains = sum(over_packs(gain_part)).reshape(2, 1, HEAD_DIM)
    grad_query, grad_key, grad_value = unpack_rows(last, 3, "unpack_last")
    return (attended, grad_query, grad_key, grad_value, grad_gains, new_mixture)


def solution(mesh):
    rows = P("pack", "seq", None)
    gains = P(None, "seq", None)
    return jax.shard_map(
        on_device,
        mesh=mesh,
        in_specs=(rows, rows, rows, rows, gains, P("pack", "seq"), P("pack", None), P()),
        out_specs=(rows, rows, rows, rows, gains, P()),
        check_vma=False,
    )
```

time: 192 us -> 191 us (level)
  the two profiles are of different devices: /device:TPU:25 before, /device:TPU:1 now
where the time goes in v2:
time: 191 us; the launch traced here: 189 us
  Pallas kernels  60.5 us (32%)
  waiting for transfers between devices  49.9 us (26%)
  starting transfers between devices  44.3 us (23%)
  local copies, waits for them, and re-layouts  28.4 us (15%)
  other arithmetic  4.5 us (2%)
    all_to_all x4, waiting for transfers between devices, exchange(): return lax.all_to_all(slab, 'seq', split_axis=0, concat_axis=0, tiled=True)  49 us
    all_to_all x4, starting transfers between devices, exchange(): return lax.all_to_all(slab, 'seq', split_axis=0, concat_axis=0, tiled=True)  30.6 us
    unnamed x68, local copies, waits for them, and re-layouts  28.4 us
    pallas_call x1, Pallas kernels, run_backward(): pl.pallas_call(backward_kernel, in_specs=[SMEM_SPEC] * 2 + [VMEM_SPEC] *...  20.6 us
    pallas_call x1, Pallas kernels, run_stats(): pl.pallas_call(stats_kernel, in_specs=[SMEM_SPEC] + [VMEM_SPEC] * 3, out_...  15.4 us
    pallas_call x1, Pallas kernels, run_forward(): pl.pallas_call(forward_kernel, in_specs=[SMEM_SPEC] * 3 + [VMEM_SPEC] * 7...  14.7 us
    ppermute x9, starting transfers between devices, over_packs(): moved.append(lax.ppermute(value, 'pack', pairs))  13.8 us
  transfers between devices with their start and end apart: 13, of which 5 were waited for; matrix products, arithmetic and copies ran while one was open for 2% of the time, Pallas kernels for 22%

profile of v2, /device:TPU:1, one launch (start us, length us, event | category | flops | bytes accessed | tf_op | source)
XLA Modules:
  0.0 188.6 jit_solution(9629119549741976492)
XLA Ops:
  0.6 1.2 copy-done.8
  1.9 1.2 copy-done.9
  3.7 1.3 pack_first.1
  5.0 1.4 copy-done.2
  6.4 9.6 %all-to-all-start = ((bf16[32,272,128]{2,1,0:T(8,128)(2,1)}), bf16[32,272,128]{2,1,0:T(8,128)(2,1)S(1)}, u32[]{:S(2)}, u32[]{:S(2)}) async-start(bf16[32,272,128]{2,1,0:T(8,128)(2,1)} %copy-done.2), calls=%async_computation | async-start | bytes 4456448 | tf_op jit(solution)/shard_map/all_to_all | solution.py:510
  17.2 1.2 pack_second.1
  18.5 1.4 copy-done.3
  19.8 25.9 %all-to-all-done.seg_ref.recv_ref = bf16[32,272,128]{2,1,0:T(8,128)(2,1)S(1)} async-done(((bf16[32,272,128]{2,1,0:T(8,128)(2,1)}), bf16[32,272,128]{2,1,0:T(8,128)(2,1)S(1)}, u32[]{:S(2)}, u32[]{:S(2)}) %all-to-all-start) | async-done | bytes 2228256 | tf_op jit(solution)/shard_map/all_to_all | solution.py:510
  45.7 5.3 %all-to-all-start.1 = ((bf16[32,256,128]{2,1,0:T(8,128)(2,1)}), bf16[32,256,128]{2,1,0:T(8,128)(2,1)}, u32[]{:S(2)}, u32[]{:S(2)}) async-start(bf16[32,256,128]{2,1,0:T(8,128)(2,1)} %copy-done.3), calls=%async_computation.1 | async-start | bytes 4194304 | tf_op jit(solution)/shard_map/all_to_all | solution.py:510
  51.0 3.6 %row_groups.1 = (f32[32,128]{1,0:T(8,128)}, f32[1,128]{1,0:T(1,128)}, s32[2,17]{1,0:T(2,128)}, s32[3,164]{1,0:T(4,128)}, s32[16,2,256]{2,1,0:T(2,128)}) custom-call(s32[1,16]{1,0:T(1,128)} %labels_ref.1, bf16[32,272,128]{2,1,0:T(8,128)(2,1)} %copy-done), custom_call_target="tpu_custom_call" | custom-call | tf_op jit(solution)/shard_map/row_groups/pallas_call | solution.py:196
  54.6 1.4 collective-permute-start
  56.0 2.6 %collective-permute-start.1 = (f32[1,128]{1,0:T(1,128)}, f32[1,128]{1,0:T(1,128)S(1)}, u32[]{:S(2)}, u32[]{:S(2)}) collective-permute-start(f32[1,128]{1,0:T(1,128)} %get-tuple-element.30), channel_id=1, source_target_pairs={{0,64},{32,96},{64,0},{96,32},{1,65},{33,97},{65,1},{97,33},{2,66}... | collective-permute-start | bytes 1544 | tf_op jit(solution)/shard_map/ppermute | solution.py:505
  59.7 1.6 copy-done.1
  62.8 15.4 %score_stats.1 = (bf16[4096,128]{1,0:T(8,128)(2,1)S(1)}, bf16[4096,128]{1,0:T(8,128)(2,1)S(1)}, bf16[128,4096]{1,0:T(8,128)(2,1)S(1)}, bf16[128,4096]{1,0:T(8,12...) custom-call(s32[2,17]{1,0:T(2,128)S(1)} %copy-done.28, ...), custom_call_target="tpu_custom_call" | custom-call | tf_op jit(solution)/shard_map/score_stats/pallas_call | solution.py:278
  82.2 14.7 %forward.1 = (bf16[32,144,128]{2,1,0:T(8,128)(2,1)S(1)}, bf16[4096,128]{1,0:T(8,128)(2,1)S(1)}, bf16[128,4096]{1,0:T(8,128)(2,1)S(1)}, f32[16,1,256]{2,1,0:T(1,128)S(1)}) custom-call(s32[2,17]{1,0:T(2,128)S(1)} %copy-done.29, s32[3,164]{1,0:T(4,128)S(1)} %copy-done.27, f32[8]{0:T(128)S(1)} %copy-done.31, f32[4,128]{1,0:T(4,128)S(1)} %pad_maximum_fusion.counts_ref, ...), custom_call_target="tpu_custom_call" | custom-call | tf_op jit(solution)/shard_map/forward/pallas_call | solution.py:389
  100.0 8.3 %all-to-all-start.2 = ((bf16[32,144,128]{2,1,0:T(8,128)(2,1)}), bf16[32,144,128]{2,1,0:T(8,128)(2,1)S(1)}, u32[]{:S(2)}, u32[]{:S(2)}) async-start(bf16[32,144,128]{2,1,0:T(8,128)(2,1)} %copy-done.7), calls=%async_computation.2 | async-start | bytes 2359296 | tf_op jit(solution)/shard_map/all_to_all | solution.py:510
  109.5 1.2 copy-done.15
  110.8 1.2 copy-done.17
  112.0 1.2 copy-done.19
  113.2 1.2 copy-done.21
  114.4 1.2 copy-done.23
  115.7 20.6 %backward.1 = (bf16[32,384,128]{2,1,0:T(8,128)(2,1)S(1)}, f32[2,128]{1,0:T(2,128)S(1)}) custom-call(s32[2,17]{1,0:T(2,128)S(1)} %copy-done.29, s32[3,164]{1,0:T(4,128)S(1)} %copy-done.27, bf16[32,256,128]{2,1,0:T(8,128)(2,1)} %all-to-all-done.1.recv_ref, f32[2,128]{1,0:T(2,128)S(1)} %bitcast.10, bf16[4096,128]{1,0:T(8,128)(2,1)S(1)} %copy-done.13, ...), custom_call_target="tpu_custom_call" | custom-call | tf_op jit(solution)/shard_map/backward/pallas_call | solution.py:486
  136.3 1.6 copy-done.6
  138.9 7.4 %all-to-all-start.3 = ((bf16[32,384,128]{2,1,0:T(8,128)(2,1)}), bf16[32,384,128]{2,1,0:T(8,128)(2,1)S(1)}, u32[]{:S(2)}, u32[]{:S(2)}) async-start(bf16[32,384,128]{2,1,0:T(8,128)(2,1)} %copy-done.6), calls=%async_computation.3 | async-start | bytes 6291456 | tf_op jit(solution)/shard_map/all_to_all | solution.py:510
  147.8 1.3 collective-permute-start.4
  149.1 2.1 %collective-permute-start.5 = (f32[2,128]{1,0:T(2,128)S(1)}, f32[2,128]{1,0:T(2,128)S(1)}, u32[]{:S(2)}, u32[]{:S(2)}) collective-permute-start(f32[2,128]{1,0:T(2,128)S(1)} %get-tuple-element.49), channel_id=1, source_target_pairs={{0,96},{32,0},{64,32},{96,64},{1,97},{33,1},{65,33},{97,65},{2,98}... | collective-permute-start | bytes 3080 | tf_op jit(solution)/shard_map/ppermute | solution.py:505
  154.5 3.3 %collective-permute-start.7 = (f32[8]{0:T(128)S(1)}, f32[8]{0:T(128)S(1)}, u32[]{:S(2)}, u32[]{:S(2)}) collective-permute-start(f32[8]{0:T(128)S(1)} %convert_reduce_fusion), channel_id=1, source_target_pairs={{0,64},{32,96},{64,0},{96,32},{1,65},{33,97},{65,1},{97,33},{2,66}... | collective-permute-start | bytes 104 | tf_op jit(solution)/shard_map/ppermute | solution.py:505
  157.8 1.3 copy-done.5
  159.1 1.2 unpack_first.1
  160.5 1.3 fusion
  162.9 23.2 %all-to-all-done.3.in_ref = bf16[32,384,128]{2,1,0:T(8,128)(2,1)S(1)} async-done(((bf16[32,384,128]{2,1,0:T(8,128)(2,1)}), bf16[32,384,128]{2,1,0:T(8,128)(2,1)S(1)}, u32[]{:S(2)}, u32[]{:S(2)}) %all-to-all-start.3) | async-done | bytes 3145760 | tf_op jit(solution)/shard_map/all_to_all | solution.py:510
  186.1 2.5 %unpack_last.1 = (bf16[1,128,4096]{2,1,0:T(8,128)(2,1)}, bf16[1,128,4096]{2,1,0:T(8,128)(2,1)}, bf16[1,128,4096]{2,1,0:T(8,128)(2,1)}) custom-call(bf16[32,384,128]{2,1,0:T(8,128)(2,1)S(1)} %all-to-all-done.3.in_ref), custom_call_target="tpu_custom_call" | custom-call | tf_op jit(solution)/shard_map/unpack_last/pallas_call | solution.py:103
  (77 shorter events, 19.8 us)
Async XLA Ops:
  0.6 1.2 copy-start.8
  1.9 1.2 copy-start.9
  5.0 1.4 copy-start.2
  6.4 9.6 %copy-start.10 = (bf16[1,128,4096]{2,1,0:T(8,128)(2,1)S(1)}, bf16[1,128,4096]{2,1,0:T(8,128)(2,1)}, u32[]{:S(2)}) copy-start(bf16[1,128,4096]{2,1,0:T(8,128)(2,1)} %refs_0_.3) | copy-start | bytes 3145732
  6.4 39.3 %all-to-all-start = ((bf16[32,272,128]{2,1,0:T(8,128)(2,1)}), bf16[32,272,128]{2,1,0:T(8,128)(2,1)S(1)}, u32[]{:S(2)}, u32[]{:S(2)}) async-start(bf16[32,272,128]{2,1,0:T(8,128)(2,1)} %copy-done.2), calls=%async_computation | async-start | bytes 4456448 | tf_op jit(solution)/shard_map/all_to_all | solution.py:510
  16.0 1.2 copy-start.11
  18.5 1.4 copy-start.3
  45.7 5.3 %copy-start = (bf16[32,272,128]{2,1,0:T(8,128)(2,1)}, bf16[32,272,128]{2,1,0:T(8,128)(2,1)S(1)}, u32[]{:S(2)}) copy-start(bf16[32,272,128]{2,1,0:T(8,128)(2,1)S(1)} %all-to-all-done.seg_ref.recv_ref) | copy-start | bytes 6684676
  45.7 36.5 %all-to-all-start.1 = ((bf16[32,256,128]{2,1,0:T(8,128)(2,1)}), bf16[32,256,128]{2,1,0:T(8,128)(2,1)}, u32[]{:S(2)}, u32[]{:S(2)}) async-start(bf16[32,256,128]{2,1,0:T(8,128)(2,1)} %copy-done.3), calls=%async_computation.1 | async-start | bytes 4194304 | tf_op jit(solution)/shard_map/all_to_all | solution.py:510
  51.0 8.8 %copy-start.30 = (f32[2,1,128]{2,1,0:T(1,128)S(1)}, f32[2,1,128]{2,1,0:T(1,128)}, u32[]{:S(2)}) copy-start(f32[2,1,128]{2,1,0:T(1,128)} %param.12) | copy-start | bytes 3076
  51.0 31.2 %copy-start.31 = (f32[8]{0:T(128)S(1)}, f32[8]{0:T(128)}, u32[]{:S(2)}) copy-start(f32[8]{0:T(128)} %mixture_ref.1) | copy-start | bytes 100
  54.6 27.5 %copy-start.33 = (f32[1,128]{1,0:T(1,128)S(1)}, f32[1,128]{1,0:T(1,128)}, u32[]{:S(2)}) copy-start(f32[1,128]{1,0:T(1,128)} %get-tuple-element.30) | copy-start | bytes 1540
  54.6 27.5 %copy-start.27 = (s32[3,164]{1,0:T(4,128)S(1)}, s32[3,164]{1,0:T(4,128)}, u32[]{:S(2)}) copy-start(s32[3,164]{1,0:T(4,128)} %get-tuple-element.29.pair_ref) | copy-start | bytes 5908
  54.6 27.5 %copy-start.29 = (s32[2,17]{1,0:T(2,128)S(1)}, s32[2,17]{1,0:T(2,128)}, u32[]{:S(2)}) copy-start(s32[2,17]{1,0:T(2,128)} %get-tuple-element.28.span_ref) | copy-start | bytes 412
  54.6 27.5 %collective-permute-start = (f32[1,128]{1,0:T(1,128)}, f32[1,128]{1,0:T(1,128)S(1)}, u32[]{:S(2)}, u32[]{:S(2)}) collective-permute-start(f32[1,128]{1,0:T(1,128)} %get-tuple-element.30), channel_id=1, source_target_pairs={{0,32},{32,64},{64,96},{96,0},{1,33},{33,65},{65,97},{97,1},{2,34}... | collective-permute-start | bytes 1544 | tf_op jit(solution)/shard_map/ppermute | solution.py:505
  56.0 26.1 %collective-permute-start.1 = (f32[1,128]{1,0:T(1,128)}, f32[1,128]{1,0:T(1,128)S(1)}, u32[]{:S(2)}, u32[]{:S(2)}) collective-permute-start(f32[1,128]{1,0:T(1,128)} %get-tuple-element.30), channel_id=1, source_target_pairs={{0,64},{32,96},{64,0},{96,32},{1,65},{33,97},{65,1},{97,33},{2,66}... | collective-permute-start | bytes 1544 | tf_op jit(solution)/shard_map/ppermute | solution.py:505
  58.6 23.5 %collective-permute-start.2 = (f32[1,128]{1,0:T(1,128)}, f32[1,128]{1,0:T(1,128)S(1)}, u32[]{:S(2)}, u32[]{:S(2)}) collective-permute-start(f32[1,128]{1,0:T(1,128)} %get-tuple-element.30), channel_id=1, source_target_pairs={{0,96},{32,0},{64,32},{96,64},{1,97},{33,1},{65,33},{97,65},{2,98}... | collective-permute-start | bytes 1544 | tf_op jit(solution)/shard_map/ppermute | solution.py:505
  59.7 1.6 copy-start.1
  62.8 19.4 %copy-start.25 = (s32[16,2,256]{2,1,0:T(2,128)S(1)}, s32[16,2,256]{2,1,0:T(2,128)}, u32[]{:S(2)}) copy-start(s32[16,2,256]{2,1,0:T(2,128)} %get-tuple-element.32.span_rows_ref) | copy-start | bytes 98308
  62.8 19.4 %copy-start.26 = (f32[32,128]{1,0:T(8,128)S(1)}, f32[32,128]{1,0:T(8,128)}, u32[]{:S(2)}) copy-start(f32[32,128]{1,0:T(8,128)} %get-tuple-element.31.group_ref) | copy-start | bytes 49156
  100.0 37.9 %all-to-all-start.2 = ((bf16[32,144,128]{2,1,0:T(8,128)(2,1)}), bf16[32,144,128]{2,1,0:T(8,128)(2,1)S(1)}, u32[]{:S(2)}, u32[]{:S(2)}) async-start(bf16[32,144,128]{2,1,0:T(8,128)(2,1)} %copy-done.7), calls=%async_computation.2 | async-start | bytes 2359296 | tf_op jit(solution)/shard_map/all_to_all | solution.py:510
  108.3 1.2 copy-start.13
  109.5 1.2 copy-start.15
  136.2 1.6 copy-start.6
  138.9 47.2 %all-to-all-start.3 = ((bf16[32,384,128]{2,1,0:T(8,128)(2,1)}), bf16[32,384,128]{2,1,0:T(8,128)(2,1)S(1)}, u32[]{:S(2)}, u32[]{:S(2)}) async-start(bf16[32,384,128]{2,1,0:T(8,128)(2,1)} %copy-done.6), calls=%async_computation.3 | async-start | bytes 6291456 | tf_op jit(solution)/shard_map/all_to_all | solution.py:510
  146.9 4.3 %collective-permute-start.3 = (f32[2,128]{1,0:T(2,128)S(1)}, f32[2,128]{1,0:T(2,128)S(1)}, u32[]{:S(2)}, u32[]{:S(2)}) collective-permute-start(f32[2,128]{1,0:T(2,128)S(1)} %get-tuple-element.49), channel_id=1, source_target_pairs={{0,32},{32,64},{64,96},{96,0},{1,33},{33,65},{65,97},{97,1},{2,34}... | collective-permute-start | bytes 3080 | tf_op jit(solution)/shard_map/ppermute | solution.py:505
  147.8 3.9 %collective-permute-start.4 = (f32[2,128]{1,0:T(2,128)S(1)}, f32[2,128]{1,0:T(2,128)S(1)}, u32[]{:S(2)}, u32[]{:S(2)}) collective-permute-start(f32[2,128]{1,0:T(2,128)S(1)} %get-tuple-element.49), channel_id=1, source_target_pairs={{0,64},{32,96},{64,0},{96,32},{1,65},{33,97},{65,1},{97,33},{2,66}... | collective-permute-start | bytes 3080 | tf_op jit(solution)/shard_map/ppermute | solution.py:505
  149.1 2.8 %collective-permute-start.5 = (f32[2,128]{1,0:T(2,128)S(1)}, f32[2,128]{1,0:T(2,128)S(1)}, u32[]{:S(2)}, u32[]{:S(2)}) collective-permute-start(f32[2,128]{1,0:T(2,128)S(1)} %get-tuple-element.49), channel_id=1, source_target_pairs={{0,96},{32,0},{64,32},{96,64},{1,97},{33,1},{65,33},{97,65},{2,98}... | collective-permute-start | bytes 3080 | tf_op jit(solution)/shard_map/ppermute | solution.py:505
  153.4 7.0 %collective-permute-start.6 = (f32[8]{0:T(128)S(1)}, f32[8]{0:T(128)S(1)}, u32[]{:S(2)}, u32[]{:S(2)}) collective-permute-start(f32[8]{0:T(128)S(1)} %convert_reduce_fusion), channel_id=1, source_target_pairs={{0,32},{32,64},{64,96},{96,0},{1,33},{33,65},{65,97},{97,1},{2,34}... | collective-permute-start | bytes 104 | tf_op jit(solution)/shard_map/ppermute | solution.py:505
  154.5 5.8 %collective-permute-start.7 = (f32[8]{0:T(128)S(1)}, f32[8]{0:T(128)S(1)}, u32[]{:S(2)}, u32[]{:S(2)}) collective-permute-start(f32[8]{0:T(128)S(1)} %convert_reduce_fusion), channel_id=1, source_target_pairs={{0,64},{32,96},{64,0},{96,32},{1,65},{33,97},{65,1},{97,33},{2,66}... | collective-permute-start | bytes 104 | tf_op jit(solution)/shard_map/ppermute | solution.py:505
  157.8 2.7 %collective-permute-start.8 = (f32[8]{0:T(128)S(1)}, f32[8]{0:T(128)S(1)}, u32[]{:S(2)}, u32[]{:S(2)}) collective-permute-start(f32[8]{0:T(128)S(1)} %convert_reduce_fusion), channel_id=1, source_target_pairs={{0,96},{32,0},{64,32},{96,64},{1,97},{33,1},{65,33},{97,65},{2,98}... | collective-permute-start | bytes 104 | tf_op jit(solution)/shard_map/ppermute | solution.py:505
  157.8 1.3 copy-start.5
  (15 other events, 15.0 us)

commit v3 on v2

v3 whole, which is shorter than its diff:
```python
import functools

import jax
import jax.numpy as jnp
from jax import lax
from jax.experimental import pallas as pl
from jax.experimental.pallas import tpu as pltpu
from jax.sharding import PartitionSpec as P

HEADS = 32
HEAD_DIM = 128
IMAGES = 16
GROUPS = 8
PACKS = 4
LENGTH = 4096

NEG = -1e30
EPS = 1e-06
ETA = 2.0
SCALE = HEAD_DIM ** (-0.5)
EXP_SCALE = SCALE * 1.4426950408889634

BLOCK = 128
BLOCKS = LENGTH // BLOCK
TILE = 256
TILES = LENGTH // TILE
PAIR = TILE // BLOCK
KEYS = 256
UNROLL = 4
MOST_PAIRS = (LENGTH * (1024 // TILE + 2) + TILES * (BLOCK - 1 + KEYS - 1)) // KEYS + UNROLL
SAFE_LOGIT = 70.0
EXTRA = 16
VMEM_LIMIT = 56 * 1024 * 1024

BF16 = jnp.bfloat16
F32 = jnp.float32
I32 = jnp.int32

VMEM_SPEC = pl.BlockSpec(memory_space=pltpu.VMEM)
SMEM_SPEC = pl.BlockSpec(memory_space=pltpu.SMEM)
ANY_SPEC = pl.BlockSpec(memory_space=pl.ANY)


def shape(dims, dtype):
    return jax.ShapeDtypeStruct(dims, dtype)


def head_columns(h):
    return pl.ds(h * HEAD_DIM, HEAD_DIM)


def pack_kernel(count, *refs):
    row_refs, extra_refs, (out_ref, sems) = refs[:count], refs[count:-2], refs[-2:]
    copies = []
    for n, ref in enumerate(row_refs):
        for h in range(HEADS):
            copy = pltpu.make_async_copy(
                ref.at[0, :, head_columns(h)],
                out_ref.at[h, pl.ds(n * BLOCK, BLOCK), :],
                sems.at[n, h],
            )
            copy.start()
            copies.append(copy)
    for extra_ref in extra_refs:
        tile = extra_ref[...].astype(F32)
        left = jnp.zeros((EXTRA - tile.shape[0], 128), F32)
        tile = jnp.concatenate([tile, left], 0).astype(BF16)
        out_ref[:, len(row_refs) * BLOCK :, :] = jnp.broadcast_to(tile[None], (HEADS, EXTRA, 128))
    for copy in copies:
        copy.wait()


def pack_rows(rows, extra, name):
    extras = () if extra is None else (extra,)
    return pl.pallas_call(
        functools.partial(pack_kernel, len(rows)),
        in_specs=[ANY_SPEC] * len(rows) + [VMEM_SPEC] * len(extras),
        out_specs=VMEM_SPEC,
        out_shape=shape((HEADS, len(rows) * BLOCK + EXTRA * len(extras), 128), BF16),
        scratch_shapes=[pltpu.SemaphoreType.DMA((len(rows), HEADS))],
        compiler_params=pltpu.CompilerParams(vmem_limit_bytes=VMEM_LIMIT),
        name=name,
    )(*rows, *extras)


def unpack_kernel(in_ref, *refs):
    *row_refs, sems = refs
    copies = []
    for n, ref in enumerate(row_refs):
        for h in range(HEADS):
            copy = pltpu.make_async_copy(
                in_ref.at[h, pl.ds(n * BLOCK, BLOCK), :],
                ref.at[0, :, head_columns(h)],
                sems.at[n, h],
            )
            copy.start()
            copies.append(copy)
    for copy in copies:
        copy.wait()


def unpack_rows(slab, count, name):
    return pl.pallas_call(
        unpack_kernel,
        in_specs=[VMEM_SPEC],
        out_specs=[ANY_SPEC] * count,
        out_shape=[shape((1, BLOCK, HEADS * HEAD_DIM), BF16)] * count,
        scratch_shapes=[pltpu.SemaphoreType.DMA((count, HEADS))],
        compiler_params=pltpu.CompilerParams(vmem_limit_bytes=VMEM_LIMIT),
        name=name,
    )(slab)


def dot(a, b, contract=((1,), (0,))):
    return lax.dot_general(a, b, (contract, ((), ())), preferred_element_type=F32)


def tile_rows(ref, i, part, size=TILE):
    blocks = size // BLOCK
    return ref[pl.ds(i, blocks), part * BLOCK : (part + 1) * BLOCK, :].reshape(size, HEAD_DIM)


def tile_at(i, size=TILE):
    return pl.ds(pl.multiple_of(i * size, size), size)


def mean_down(values):
    return jnp.sum(values, 0, keepdims=True) * (1.0 / HEAD_DIM)


def block_row(b):
    return b // PAIR, slice((b % PAIR) * BLOCK, (b % PAIR + 1) * BLOCK)


def group_sums(group, values):
    lane = lax.broadcasted_iota(I32, (1, 128), 1)
    sums = jnp.zeros((1, 128), F32)
    for g in range(GROUPS):
        part = jnp.sum(jnp.where(group == float(g), values, 0.0), 0, keepdims=True)
        sums = jnp.where(lane == g, jnp.sum(part, 1, keepdims=True), sums)
    return sums


def key_mask(span_rows_ref, i, start, step):
    first = span_rows_ref[i, 0:1, :] - start
    count = span_rows_ref[i, 1:2, :]
    row = lax.broadcasted_iota(I32, (step, TILE), 0)
    return (row - first).astype(jnp.uint32) < count.astype(jnp.uint32)


def masked(scores, span_rows_ref, i, mask_at):
    return jnp.where(key_mask(span_rows_ref, i, mask_at, KEYS), scores, NEG)


def each_pairs(total, pair_ref, body):
    def some(n, carry):
        pairs = []
        for u in range(UNROLL):
            p = n * UNROLL + u
            at = pl.multiple_of(pair_ref[1, p], BLOCK)
            pairs.append((p, pair_ref[0, p], at, pair_ref[2, p]))
        body(pairs)
        return carry

    lax.fori_loop(0, (total + UNROLL - 1) // UNROLL, some, 0)


def find_pairs(seg_all, starts, pair_ref, span_rows_ref):
    for s in range(IMAGES + 1):
        starts[s] = jnp.sum((seg_all < float(s)).astype(F32)).astype(I32)
    first = jnp.zeros((BLOCKS, 128), I32)
    count = jnp.zeros((BLOCKS, 128), I32)
    for s in range(IMAGES):
        here = seg_all == float(s)
        first = jnp.where(here, starts[s], first)
        count = jnp.where(here, starts[s + 1] - starts[s], count)
    for b in range(BLOCKS):
        tile, at = block_row(b)
        span_rows_ref[tile, 0:1, at] = first[b : b + 1, :]
        span_rows_ref[tile, 1:2, at] = count[b : b + 1, :]

    def span(i, total):
        low, high = jnp.int32(0), jnp.int32(LENGTH)
        for s in range(1, IMAGES):
            low = jnp.where(starts[s] <= i * TILE, starts[s], low)
        for s in range(IMAGES - 1, 0, -1):
            high = jnp.where(starts[s] > i * TILE + TILE - 1, starts[s], high)
        low = (low // BLOCK) * BLOCK
        steps = (high - low + KEYS - 1) // KEYS
        low = jnp.minimum(low, LENGTH - steps * KEYS)

        def add(j, carry):
            pair_ref[0, total + j] = i
            pair_ref[1, total + j] = low + j * KEYS
            pair_ref[2, total + j] = low + j * KEYS
            return carry

        lax.fori_loop(0, steps, add, 0)
        return total + steps

    total = lax.fori_loop(0, TILES, span, jnp.int32(0))
    for u in range(UNROLL):
        pair_ref[0, total + u] = 0
        pair_ref[1, total + u] = 0
        pair_ref[2, total + u] = -(1 << 20)
    return total


def attend_kernel(
    recv_ref, gains_ref,
    pair_ref, total_ref, span_rows_ref,
    q_hat_ref, k_hat_ref, q_turned_ref, k_turned_ref, raw_q_ref, raw_k_ref, moments_ref, norm_ref,
    out_ref,
    starts, v_turned, terms, fold,
):
    total = find_pairs(recv_ref[:, 3 * BLOCK, :].astype(F32), starts, pair_ref, span_rows_ref)
    total_ref[0] = total
    gains = jnp.concatenate([gains_ref[...], jnp.zeros((6, HEAD_DIM), F32)], 0).T

    def prepare(i, most):
        rows = tile_at(i)
        v_turned[:, rows] = tile_rows(recv_ref, i * PAIR, 2).T
        outs = ((q_hat_ref, q_turned_ref, raw_q_ref), (k_hat_ref, k_turned_ref, raw_k_ref))
        sizes = []
        for n, (hat_ref, turned_ref, raw_ref) in enumerate(outs):
            raw = tile_rows(recv_ref, i * PAIR, n).T
            raw_ref[:, rows] = raw
            values = raw.astype(F32)
            mean = mean_down(values)
            centre = values - mean
            inverse = lax.rsqrt(mean_down(centre * centre) + EPS)
            moments_ref[i, 2 * n : 2 * n + 1, :] = mean
            moments_ref[i, 2 * n + 1 : 2 * n + 2, :] = inverse
            hat = centre * inverse * gains[:, n : n + 1]
            sizes.append(jnp.maximum(most[n], mean_down(hat * hat)))
            hat = hat.astype(BF16)
            turned_ref[:, rows] = hat
            hat_ref[rows, :] = hat.T
        out_ref[i] = jnp.zeros((HEAD_DIM, TILE), F32)
        norm_ref[i] = jnp.zeros((2, TILE), F32)
        fold[i] = jnp.zeros((8, TILE), F32)
        return tuple(sizes)

    zero = jnp.zeros((1, TILE), F32)
    most_q, most_k = lax.fori_loop(0, TILES, prepare, (zero, zero))
    bound = jnp.max(most_q) * jnp.max(most_k) * HEAD_DIM

    def scores_of(pairs):
        tiles = [
            dot(k_hat_ref[pl.ds(at, KEYS), :], q_turned_ref[:, tile_at(i)]) for _, i, at, _ in pairs
        ]
        return [
            masked(tile, span_rows_ref, i, mask_at)
            for tile, (_, i, _, mask_at) in zip(tiles, pairs)
        ]

    @pl.when(jnp.logical_not(bound <= SAFE_LOGIT * SAFE_LOGIT))
    def _():
        def clear(i, carry):
            fold[i] = jnp.full((8, TILE), NEG, F32)
            return carry

        lax.fori_loop(0, TILES, clear, 0)

        def top_pairs(pairs):
            for tile, (_, i, _, _) in zip(scores_of(pairs), pairs):
                top = jnp.max(tile.reshape(KEYS // 8, 8, TILE), 0)
                fold[i] = jnp.maximum(fold[i], top)

        each_pairs(total, pair_ref, top_pairs)

        def finish(i, carry):
            norm_ref[i, 0:1, :] = jnp.max(fold[i], 0, keepdims=True) * EXP_SCALE
            fold[i] = jnp.zeros((8, TILE), F32)
            return carry

        lax.fori_loop(0, TILES, finish, 0)

    def exp_pairs(pairs):
        sums = []
        for tile, (p, i, _, _) in zip(scores_of(pairs), pairs):
            tile = jnp.exp2(tile * EXP_SCALE - norm_ref[i, 0:1, :])
            terms[p] = tile
            sums.append(jnp.sum(tile.reshape(KEYS // 8, 8, TILE), 0))
        for part, (_, i, _, _) in zip(sums, pairs):
            fold[i] += part

    each_pairs(total, pair_ref, exp_pairs)

    def invert(i, carry):
        norm_ref[i, 1:2, :] = 1.0 / jnp.sum(fold[i], 0, keepdims=True)
        return carry

    lax.fori_loop(0, TILES, invert, 0)

    def out_pairs(pairs):
        tiles = [(terms[p] * norm_ref[i, 1:2, :]).astype(BF16) for p, i, _, _ in pairs]
        tiles = [
            dot(v_turned[:, pl.ds(at, KEYS)], tile) for tile, (_, _, at, _) in zip(tiles, pairs)
        ]
        for tile, (_, i, _, _) in zip(tiles, pairs):
            out_ref[i] += tile

    each_pairs(total, pair_ref, out_pairs)


def run_attend(received, gains):
    return pl.pallas_call(
        attend_kernel,
        in_specs=[VMEM_SPEC] * 2,
        out_specs=[SMEM_SPEC] * 2 + [VMEM_SPEC] * 10,
        out_shape=[
            shape((3, MOST_PAIRS), I32),
            shape((1,), I32),
            shape((TILES, 2, TILE), I32),
            shape((LENGTH, HEAD_DIM), BF16),
            shape((LENGTH, HEAD_DIM), BF16),
            shape((HEAD_DIM, LENGTH), BF16),
            shape((HEAD_DIM, LENGTH), BF16),
            shape((HEAD_DIM, LENGTH), BF16),
            shape((HEAD_DIM, LENGTH), BF16),
            shape((TILES, 4, TILE), F32),
            shape((TILES, 2, TILE), F32),
            shape((TILES, HEAD_DIM, TILE), F32),
        ],
        scratch_shapes=[
            pltpu.SMEM((IMAGES + 1,), I32),
            pltpu.VMEM((HEAD_DIM, LENGTH), BF16),
            pltpu.VMEM((MOST_PAIRS, KEYS, TILE), F32),
            pltpu.VMEM((TILES, 8, TILE), F32),
        ],
        compiler_params=pltpu.CompilerParams(vmem_limit_bytes=VMEM_LIMIT),
        name="attend",
    )(received, gains)


def loss_kernel(
    labels_ref, mixture_ref,
    recv_ref, out_ref,
    send_ref, grad_ref, grad_turned_ref, inner_ref, counts_ref,
    coef_rows, loss_rows,
):
    seg_all = recv_ref[:, BLOCK, :].astype(F32)
    group = jnp.zeros((BLOCKS, 128), F32)
    for s in range(IMAGES):
        group = jnp.where(seg_all == float(s), labels_ref[0, s].astype(F32), group)
    others = [recv_ref[:, BLOCK + 1 + p, :].astype(F32) for p in range(PACKS)]
    total_mix = mixture_ref[0]
    for g in range(1, GROUPS):
        total_mix = total_mix + mixture_ref[g]
    lane = lax.broadcasted_iota(I32, (1, 128), 1)
    coef = jnp.zeros((BLOCKS, 128), F32)
    count_row = jnp.zeros((1, 128), F32)
    for g in range(GROUPS):
        hits = sum((other == float(g)).astype(F32) for other in others)
        count = jnp.sum(jnp.sum(hits, 0, keepdims=True), 1, keepdims=True)
        share = jnp.full((1, 1), mixture_ref[g], F32) / total_mix
        coef = jnp.where(group == float(g), share / (count * (HEADS * HEAD_DIM)), coef)
        count_row = jnp.where(lane == g, count, count_row)
    counts_ref[...] = count_row
    for b in range(BLOCKS):
        tile, at = block_row(b)
        coef_rows[tile, 0:1, at] = coef[b : b + 1, :]

    def finish(i, carry):
        rows = tile_at(i)
        head_out = out_ref[i]
        misfit = head_out - tile_rows(recv_ref, i * PAIR, 0).T.astype(F32)
        loss_rows[i, 0:1, :] = 0.5 * jnp.sum(misfit * misfit, 0, keepdims=True)
        grad_out = coef_rows[i, 0:1, :] * misfit
        inner_ref[i, 0:1, :] = jnp.sum(grad_out * head_out, 0, keepdims=True)
        grad_turned = grad_out.astype(BF16)
        grad_turned_ref[:, rows] = grad_turned
        grad_ref[rows, :] = grad_turned.T
        send_ref[pl.ds(i * PAIR, PAIR), 0:BLOCK, :] = head_out.astype(BF16).T.reshape(
            PAIR, BLOCK, HEAD_DIM
        )
        return carry

    lax.fori_loop(0, TILES, finish, 0)

    rows = [block_row(b) for b in range(BLOCKS)]
    losses = jnp.concatenate([loss_rows[tile, 0:1, at] for tile, at in rows], 0)
    loss_row = group_sums(group, losses)
    high = loss_row.astype(BF16)
    left = loss_row - high.astype(F32)
    middle = left.astype(BF16)
    low = (left - middle.astype(F32)).astype(BF16)
    row = lax.broadcasted_iota(I32, (EXTRA, 128), 0)
    pieces = jnp.zeros((EXTRA, 128), F32)
    for n, piece in enumerate((high, middle, low)):
        pieces = jnp.where(row == n, piece.astype(F32), pieces)
    send_ref[:, BLOCK:, :] = jnp.broadcast_to(pieces.astype(BF16)[None], (BLOCKS, EXTRA, 128))


def run_loss(labels, mixture, second, head_out):
    return pl.pallas_call(
        loss_kernel,
        in_specs=[SMEM_SPEC] * 2 + [VMEM_SPEC] * 2,
        out_specs=[VMEM_SPEC] * 5,
        out_shape=[
            shape((BLOCKS, BLOCK + EXTRA, 128), BF16),
            shape((LENGTH, HEAD_DIM), BF16),
            shape((HEAD_DIM, LENGTH), BF16),
            shape((TILES, 1, TILE), F32),
            shape((1, 128), F32),
        ],
        scratch_shapes=[pltpu.VMEM((TILES, 1, TILE), F32), pltpu.VMEM((TILES, 1, TILE), F32)],
        compiler_params=pltpu.CompilerParams(vmem_limit_bytes=VMEM_LIMIT),
        name="loss",
    )(labels, mixture, second, head_out)


def backward_kernel(
    pair_ref, total_ref,
    recv_ref, gains_ref, q_hat_ref, k_hat_ref, q_turned_ref, k_turned_ref, raw_q_ref, raw_k_ref,
    moments_ref, span_rows_ref, norm_ref, grad_ref, grad_turned_ref, inner_ref,
    send_ref, gain_out_ref,
    grad_q, grad_k, grad_v,
):
    def clear(i, carry):
        grad_q[i] = jnp.zeros((HEAD_DIM, TILE), F32)
        grad_k[tile_at(i), :] = jnp.zeros((TILE, HEAD_DIM), F32)
        grad_v[tile_at(i), :] = jnp.zeros((TILE, HEAD_DIM), F32)
        return carry

    lax.fori_loop(0, TILES, clear, 0)

    def add_pairs(pairs):
        tiles = [
            dot(k_hat_ref[pl.ds(at, KEYS), :], q_turned_ref[:, tile_at(i)]) for _, i, at, _ in pairs
        ]
        prob_grads = [
            dot(tile_rows(recv_ref, at // BLOCK, 2, KEYS), grad_turned_ref[:, tile_at(i)])
            for _, i, at, _ in pairs
        ]
        tiles = [
            jnp.exp2(
                masked(tile, span_rows_ref, i, mask_at) * EXP_SCALE - norm_ref[i, 0:1, :]
            ) * norm_ref[i, 1:2, :]
            for tile, (_, i, _, mask_at) in zip(tiles, pairs)
        ]
        values = [
            dot(tile.astype(BF16), grad_ref[tile_at(i), :])
            for tile, (_, i, _, _) in zip(tiles, pairs)
        ]
        tiles = [
            (tile * (prob - inner_ref[i, 0:1, :]) * SCALE).astype(BF16)
            for tile, prob, (_, i, _, _) in zip(tiles, prob_grads, pairs)
        ]
        keys = [dot(tile, q_hat_ref[tile_at(i), :]) for tile, (_, i, _, _) in zip(tiles, pairs)]
        queries = [
            dot(k_turned_ref[:, pl.ds(at, KEYS)], tile) for tile, (_, _, at, _) in zip(tiles, pairs)
        ]
        for value, key, query, (_, i, at, _) in zip(values, keys, queries, pairs):
            grad_v[pl.ds(at, KEYS), :] += value
            grad_k[pl.ds(at, KEYS), :] += key
            grad_q[i] += query

    each_pairs(total_ref[0], pair_ref, add_pairs)

    gains = jnp.concatenate([gains_ref[...], jnp.zeros((6, HEAD_DIM), F32)], 0).T

    def norm_backward(i, n, grad_hat, raw_ref):
        mean = moments_ref[i, 2 * n : 2 * n + 1, :]
        inverse = moments_ref[i, 2 * n + 1 : 2 * n + 2, :]
        normed = (raw_ref[:, tile_at(i)].astype(F32) - mean) * inverse
        grad_normed = grad_hat * gains[:, n : n + 1]
        inner = mean_down(grad_normed * normed)
        grad_in = inverse * (grad_normed - mean_down(grad_normed) - normed * inner)
        send_ref[pl.ds(i * PAIR, PAIR), n * BLOCK : (n + 1) * BLOCK, :] = grad_in.astype(
            BF16
        ).T.reshape(PAIR, BLOCK, HEAD_DIM)
        grad_gain = grad_hat * normed
        return sum(grad_gain[:, c : c + 128] for c in range(0, TILE, 128))

    def finish(i, gain_sums):
        gain_q, gain_k = gain_sums
        gain_q = gain_q + norm_backward(i, 0, grad_q[i], raw_q_ref)
        gain_k = gain_k + norm_backward(i, 1, grad_k[tile_at(i), :].T, raw_k_ref)
        send_ref[pl.ds(i * PAIR, PAIR), 2 * BLOCK :, :] = (
            grad_v[tile_at(i), :].astype(BF16).reshape(PAIR, BLOCK, HEAD_DIM)
        )
        return gain_q, gain_k

    zero = jnp.zeros((HEAD_DIM, 128), F32)
    gain_q, gain_k = lax.fori_loop(0, TILES, finish, (zero, zero))
    gain_out_ref[0:1, :] = jnp.sum(gain_q.T, 0, keepdims=True)
    gain_out_ref[1:2, :] = jnp.sum(gain_k.T, 0, keepdims=True)


def run_backward(pairs, total, *arrays):
    return pl.pallas_call(
        backward_kernel,
        in_specs=[SMEM_SPEC] * 2 + [VMEM_SPEC] * len(arrays),
        out_specs=[VMEM_SPEC] * 2,
        out_shape=[shape((BLOCKS, 3 * BLOCK, 128), BF16), shape((2, HEAD_DIM), F32)],
        scratch_shapes=[
            pltpu.VMEM((TILES, HEAD_DIM, TILE), F32),
            pltpu.VMEM((LENGTH, HEAD_DIM), F32),
            pltpu.VMEM((LENGTH, HEAD_DIM), F32),
        ],
        compiler_params=pltpu.CompilerParams(vmem_limit_bytes=VMEM_LIMIT),
        name="backward",
    )(pairs, total, *arrays)


def over_packs(value):
    moved = [value]
    for shift in range(1, PACKS):
        pairs = [(i, (i + shift) % PACKS) for i in range(PACKS)]
        moved.append(lax.ppermute(value, "pack", pairs))
    return moved


def exchange(slab):
    return lax.all_to_all(slab, "seq", split_axis=0, concat_axis=0, tiled=True)


def on_device(
    query_rows, key_rows, value_rows, target_rows, norm_gains, segment_ids, group_labels, mixture
):
    gains = norm_gains.reshape(2, HEAD_DIM)
    first = exchange(pack_rows((query_rows, key_rows, value_rows), segment_ids, "pack_first"))

    image_hot = segment_ids[0][:, None] == jnp.arange(IMAGES, dtype=I32)[None, :]
    labels = jnp.sum(jnp.where(image_hot, group_labels[0][None, :], 0), 1)[None, :]
    extra = jnp.concatenate([segment_ids.astype(F32), *over_packs(labels.astype(F32))], 0)
    second = exchange(pack_rows((target_rows,), extra, "pack_second"))

    pairs, total, span_rows, *hats, moments, norms, head_out = run_attend(first, gains)
    send, *grads, counts = run_loss(group_labels, mixture, second, head_out)
    back = exchange(send)
    send, gain_part = run_backward(
        pairs, total, first, gains, *hats, moments, span_rows, norms, *grads
    )
    last = exchange(send)
    (attended,) = unpack_rows(back, 1, "unpack_first")
    losses = jnp.sum(back[:, BLOCK : BLOCK + 3, :GROUPS].astype(F32), (0, 1))
    group_total = sum(over_packs(losses))
    group_loss = group_total / (counts[0, :GROUPS] * (HEADS * HEAD_DIM))
    shares = mixture / jnp.sum(mixture)
    raised = shares * jnp.exp(ETA * group_loss)
    new_mixture = raised / jnp.sum(raised)
    grad_gains = sum(over_packs(gain_part)).reshape(2, 1, HEAD_DIM)
    grad_query, grad_key, grad_value = unpack_rows(last, 3, "unpack_last")
    return (attended, grad_query, grad_key, grad_value, grad_gains, new_mixture)


def solution(mesh):
    rows = P("pack", "seq", None)
    gains = P(None, "seq", None)
    return jax.shard_map(
        on_device,
        mesh=mesh,
        in_specs=(rows, rows, rows, rows, gains, P("pack", "seq"), P("pack", None), P()),
        out_specs=(rows, rows, rows, rows, gains, P()),
        check_vma=False,
    )
```

time: 191 us -> 188 us (0.984); the launches traced: 189 us -> 188 us
  local copies, waits for them, and re-layouts: 28.4 us -> 3.31 us
  Pallas kernels: 60.5 us -> 79 us
  waiting for transfers between devices: 49.9 us -> 57.6 us
  starting transfers between devices: 44.3 us -> 42.2 us
    unnamed x68 -> x16, local copies, waits for them, and re-layouts: 28.4 us -> 2.7 us
    pallas_call x1, Pallas kernels: 20.6 us -> 27.7 us  [run_backward(): pl.pallas_call(backward_kernel, in_specs=[SMEM_SPEC] * 2 + [VMEM_SPEC] *...]
    all_to_all x4, waiting for transfers between devices: 49 us -> 55.2 us  [exchange(): return lax.all_to_all(slab, 'seq', split_axis=0, concat_axis=0, tiled=True)]
    pallas_call x2, Pallas kernels: 2.51 us -> 8.24 us  [pack_rows(): pl.pallas_call(functools.partial(pack_kernel, len(rows)), in_specs=[ANY_S...]
    pallas_call x2, Pallas kernels: 3.7 us -> 6.86 us  [unpack_rows(): pl.pallas_call(unpack_kernel, in_specs=[VMEM_SPEC], out_specs=[ANY_SPEC]...]
    pallas_call x3 -> x2, Pallas kernels: 33.7 us -> 36.2 us  [the longest x1 29.2 us: run_attend(): pl.pallas_call(attend_kernel, in_specs=[VMEM_SPEC] * 2, out_specs=[SMEM_S...]
  transfers between devices with their start and end apart: 13 -> 13, of which waited for: 5 -> 7; matrix products, arithmetic and copies ran while one was open for 2% -> 3% of each run, Pallas kernels for 22% -> 33%
where the time goes in v3:
time: 188 us
  Pallas kernels  79 us (42%)
  waiting for transfers between devices  57.6 us (31%)
  starting transfers between devices  42.2 us (22%)
  other arithmetic  4.58 us (2%)
  local copies, waits for them, and re-layouts  3.31 us (2%)
    all_to_all x4, waiting for transfers between devices, exchange(): return lax.all_to_all(slab, 'seq', split_axis=0, concat_axis=0, tiled=True)  55.2 us
    all_to_all x4, starting transfers between devices, exchange(): return lax.all_to_all(slab, 'seq', split_axis=0, concat_axis=0, tiled=True)  29.9 us
    pallas_call x1, Pallas kernels, run_attend(): pl.pallas_call(attend_kernel, in_specs=[VMEM_SPEC] * 2, out_specs=[SMEM_S...  29.2 us
    pallas_call x1, Pallas kernels, run_backward(): pl.pallas_call(backward_kernel, in_specs=[SMEM_SPEC] * 2 + [VMEM_SPEC] *...  27.7 us
    ppermute x9, starting transfers between devices, over_packs(): moved.append(lax.ppermute(value, 'pack', pairs))  12.3 us
    pallas_call x2, Pallas kernels, pack_rows(): pl.pallas_call(functools.partial(pack_kernel, len(rows)), in_specs=[ANY_S...  8.24 us
    pallas_call x1, Pallas kernels, run_loss(): pl.pallas_call(loss_kernel, in_specs=[SMEM_SPEC] * 2 + [VMEM_SPEC] * 2, o...  7.07 us
    pallas_call x2, Pallas kernels, unpack_rows(): pl.pallas_call(unpack_kernel, in_specs=[VMEM_SPEC], out_specs=[ANY_SPEC]...  6.86 us
  transfers between devices with their start and end apart: 13, of which 7 were waited for; matrix products, arithmetic and copies ran while one was open for 3% of the time, Pallas kernels for 33%

profile of v3, /device:TPU:1, one launch (start us, length us, event | category | flops | bytes accessed | tf_op | source)
XLA Modules:
  0.0 187.5 jit_solution(14165885998875675847)
XLA Ops:
  0.6 5.1 %pack_first.1 = bf16[32,400,128]{2,1,0:T(8,128)(2,1)} custom-call(bf16[1,128,4096]{2,1,0:T(8,128)(2,1)} %refs_0_.3, bf16[1,128,4096]{2,1,0:T(8,128)(2,1)} %refs_1_.1, bf16[1,128,4096]{2,1,0:T(8,128)(2,1)} %refs_2_.1, s32[1,128]{1,0:T(1,128)} %refs_3_.1), custom_call_target="tpu_custom_call" | custom-call | tf_op jit(solution)/shard_map/pack_first/pallas_call | solution.py:75
  5.7 9.4 %all-to-all-start.1 = ((bf16[32,400,128]{2,1,0:T(8,128)(2,1)}), bf16[32,400,128]{2,1,0:T(8,128)(2,1)S(1)}, u32[]{:S(2)}, u32[]{:S(2)}) async-start(bf16[32,400,128]{2,1,0:T(8,128)(2,1)} %pack_first.1), calls=%async_computation.1 | async-start | bytes 6553600 | tf_op jit(solution)/shard_map/all_to_all | solution.py:517
  15.3 1.4 collective-permute-start
  16.6 2.6 %collective-permute-start.1 = (f32[1,128]{1,0:T(1,128)S(1)}, f32[1,128]{1,0:T(1,128)S(1)}, u32[]{:S(2)}, u32[]{:S(2)}) collective-permute-start(f32[1,128]{1,0:T(1,128)S(1)} %convert_bitcast_fusion), channel_id=1, source_target_pairs={{0,64},{32,96},{64,0},{96,32},{1,65},{33,97},{65,1},{97,33},{2,66}... | collective-permute-start | bytes 1544 | tf_op jit(solution)/shard_map/ppermute | solution.py:512
  19.3 1.1 collective-permute-start.2
  20.3 0.2 collective-permute-done.1
  20.5 1.4 collective-permute-done.2
  21.9 0.6 concatenate.3.refs_1_
  22.6 3.2 %pack_second.1 = bf16[32,144,128]{2,1,0:T(8,128)(2,1)} custom-call(bf16[1,128,4096]{2,1,0:T(8,128)(2,1)} %refs_0_.2, f32[5,128]{1,0:T(8,128)} %concatenate.3.refs_1_), custom_call_target="tpu_custom_call" | custom-call | tf_op jit(solution)/shard_map/pack_second/pallas_call | solution.py:75
  25.8 30.5 %all-to-all-done.1.recv_ref = bf16[32,400,128]{2,1,0:T(8,128)(2,1)S(1)} async-done(((bf16[32,400,128]{2,1,0:T(8,128)(2,1)}), bf16[32,400,128]{2,1,0:T(8,128)(2,1)S(1)}, u32[]{:S(2)}, u32[]{:S(2)}) %all-to-all-start.1) | async-done | bytes 3276832 | tf_op jit(solution)/shard_map/all_to_all | solution.py:517
  56.3 5.7 %all-to-all-start = ((bf16[32,144,128]{2,1,0:T(8,128)(2,1)}), bf16[32,144,128]{2,1,0:T(8,128)(2,1)}, u32[]{:S(2)}, u32[]{:S(2)}) async-start(bf16[32,144,128]{2,1,0:T(8,128)(2,1)} %pack_second.1), calls=%async_computation | async-start | bytes 2359296 | tf_op jit(solution)/shard_map/all_to_all | solution.py:517
  62.0 29.2 %attend.1 = (s32[3,123]{1,0:T(4,128)}, s32[1]{0:T(128)}, s32[16,2,256]{2,1,0:T(2,128)}, bf16[4096,128]{1,0:T(8,128)(2,1)}, bf16[4096,128]{1,0:T(8,128)(2,1)}, /*...) custom-call(bf16[32,400,128]{2,1,0:T(8,128)(2,1)} %copy-done, ...), custom_call_target="tpu_custom_call" | custom-call | tf_op jit(solution)/shard_map/attend/pallas_call | solution.py:308
  91.2 7.1 %loss.1 = (bf16[32,144,128]{2,1,0:T(8,128)(2,1)}, bf16[4096,128]{1,0:T(8,128)(2,1)}, bf16[128,4096]{1,0:T(8,128)(2,1)}, f32[16,1,256]{2,1,0:T(1,128)}, f32[1,128]{1,0:T(1,128)}) custom-call(s32[1,16]{1,0:T(1,128)} %labels_ref.1, f32[8]{0:T(128)} %mixture_ref.1, bf16[32,144,128]{2,1,0:T(8,128)(2,1)} %all-to-all-done.recv_ref, ...), custom_call_target="tpu_custom_call" | custom-call | tf_op jit(solution)/shard_map/loss/pallas_call | solution.py:397
  98.2 7.4 %all-to-all-start.2 = ((bf16[32,144,128]{2,1,0:T(8,128)(2,1)}), bf16[32,144,128]{2,1,0:T(8,128)(2,1)S(1)}, u32[]{:S(2)}, u32[]{:S(2)}) async-start(bf16[32,144,128]{2,1,0:T(8,128)(2,1)} %get-tuple-element.29), calls=%async_computation.2 | async-start | bytes 2359296 | tf_op jit(solution)/shard_map/all_to_all | solution.py:517
  105.6 27.7 %backward.1 = (bf16[32,384,128]{2,1,0:T(8,128)(2,1)}, f32[2,128]{1,0:T(2,128)}) custom-call(s32[3,123]{1,0:T(4,128)} %get-tuple-element.30.pair_ref, s32[1]{0:T(128)} %get-tuple-element.31.total_ref, bf16[32,400,128]{2,1,0:T(8,128)(2,1)} %copy-done, f32[2,128]{1,0:T(2,128)} %bitcast.14, bf16[4096,128]{1,0:T(8,128)(2,1)} %get-tuple-element.32.q_hat_ref, ...), custom_call_target="tpu_custom_call" | custom-call | tf_op jit(solution)/shard_map/backward/pallas_call | solution.py:493
  133.3 1.0 copy-done.2
  134.4 7.4 %all-to-all-start.3 = ((bf16[32,384,128]{2,1,0:T(8,128)(2,1)}), bf16[32,384,128]{2,1,0:T(8,128)(2,1)S(1)}, u32[]{:S(2)}, u32[]{:S(2)}) async-start(bf16[32,384,128]{2,1,0:T(8,128)(2,1)} %get-tuple-element.44), calls=%async_computation.3 | async-start | bytes 6291456 | tf_op jit(solution)/shard_map/all_to_all | solution.py:517
  141.9 1.2 collective-permute-start.4
  143.0 2.0 %collective-permute-start.5 = (f32[2,128]{1,0:T(2,128)S(1)}, f32[2,128]{1,0:T(2,128)S(1)}, u32[]{:S(2)}, u32[]{:S(2)}) collective-permute-start(f32[2,128]{1,0:T(2,128)S(1)} %copy-done.4), channel_id=1, source_target_pairs={{0,96},{32,0},{64,32},{96,64},{1,97},{33,1},{65,33},{97,65},{2,98}... | collective-permute-start | bytes 3080 | tf_op jit(solution)/shard_map/ppermute | solution.py:512
  145.0 0.6 reduce_sum.37
  145.9 0.5 collective-permute-done.5
  146.4 0.6 add_add_fusion
  146.9 0.9 convert_reduce_fusion
  147.8 1.5 collective-permute-start.6
  149.3 2.3 %collective-permute-start.7 = (f32[8]{0:T(128)S(1)}, f32[8]{0:T(128)S(1)}, u32[]{:S(2)}, u32[]{:S(2)}) collective-permute-start(f32[8]{0:T(128)S(1)} %convert_reduce_fusion), channel_id=1, source_target_pairs={{0,64},{32,96},{64,0},{96,32},{1,65},{33,97},{65,1},{97,33},{2,66}... | collective-permute-start | bytes 104 | tf_op jit(solution)/shard_map/ppermute | solution.py:512
  151.6 0.2 collective-permute-start.8
  151.8 2.5 %unpack_first.1 = bf16[1,128,4096]{2,1,0:T(8,128)(2,1)} custom-call(bf16[32,144,128]{2,1,0:T(8,128)(2,1)} %copy-done.2), custom_call_target="tpu_custom_call" | custom-call | tf_op jit(solution)/shard_map/unpack_first/pallas_call | solution.py:103
  154.4 1.3 fusion
  155.6 1.2 broadcast_divide_fusion
  156.8 24.7 %all-to-all-done.3.in_ref = bf16[32,384,128]{2,1,0:T(8,128)(2,1)S(1)} async-done(((bf16[32,384,128]{2,1,0:T(8,128)(2,1)}), bf16[32,384,128]{2,1,0:T(8,128)(2,1)S(1)}, u32[]{:S(2)}, u32[]{:S(2)}) %all-to-all-start.3) | async-done | bytes 3145760 | tf_op jit(solution)/shard_map/all_to_all | solution.py:517
  181.5 1.6 copy-done.1
  183.2 4.4 %unpack_last.1 = (bf16[1,128,4096]{2,1,0:T(8,128)(2,1)}, bf16[1,128,4096]{2,1,0:T(8,128)(2,1)}, bf16[1,128,4096]{2,1,0:T(8,128)(2,1)}) custom-call(bf16[32,384,128]{2,1,0:T(8,128)(2,1)} %copy-done.1), custom_call_target="tpu_custom_call" | custom-call | tf_op jit(solution)/shard_map/unpack_last/pallas_call | solution.py:103
  (26 shorter events, 0.5 us)
Async XLA Ops:
  5.7 9.5 %copy-start.5 = (s32[1,128]{1,0:T(1,128)S(1)}, s32[1,128]{1,0:T(1,128)}, u32[]{:S(2)}) copy-start(s32[1,128]{1,0:T(1,128)} %refs_3_.1) | copy-start | bytes 1540
  5.7 9.5 %copy-start.6 = (s32[1,16]{1,0:T(1,128)S(1)}, s32[1,16]{1,0:T(1,128)}, u32[]{:S(2)}) copy-start(s32[1,16]{1,0:T(1,128)} %labels_ref.1) | copy-start | bytes 196
  5.7 50.5 %all-to-all-start.1 = ((bf16[32,400,128]{2,1,0:T(8,128)(2,1)}), bf16[32,400,128]{2,1,0:T(8,128)(2,1)S(1)}, u32[]{:S(2)}, u32[]{:S(2)}) async-start(bf16[32,400,128]{2,1,0:T(8,128)(2,1)} %pack_first.1), calls=%async_computation.1 | async-start | bytes 6553600 | tf_op jit(solution)/shard_map/all_to_all | solution.py:517
  15.3 5.1 %collective-permute-start = (f32[1,128]{1,0:T(1,128)S(1)}, f32[1,128]{1,0:T(1,128)S(1)}, u32[]{:S(2)}, u32[]{:S(2)}) collective-permute-start(f32[1,128]{1,0:T(1,128)S(1)} %convert_bitcast_fusion), channel_id=1, source_target_pairs={{0,32},{32,64},{64,96},{96,0},{1,33},{33,65},{65,97},{97,1},{2,34}... | collective-permute-start | bytes 1544 | tf_op jit(solution)/shard_map/ppermute | solution.py:512
  16.6 3.9 %collective-permute-start.1 = (f32[1,128]{1,0:T(1,128)S(1)}, f32[1,128]{1,0:T(1,128)S(1)}, u32[]{:S(2)}, u32[]{:S(2)}) collective-permute-start(f32[1,128]{1,0:T(1,128)S(1)} %convert_bitcast_fusion), channel_id=1, source_target_pairs={{0,64},{32,96},{64,0},{96,32},{1,65},{33,97},{65,1},{97,33},{2,66}... | collective-permute-start | bytes 1544 | tf_op jit(solution)/shard_map/ppermute | solution.py:512
  19.3 2.7 %collective-permute-start.2 = (f32[1,128]{1,0:T(1,128)S(1)}, f32[1,128]{1,0:T(1,128)S(1)}, u32[]{:S(2)}, u32[]{:S(2)}) collective-permute-start(f32[1,128]{1,0:T(1,128)S(1)} %convert_bitcast_fusion), channel_id=1, source_target_pairs={{0,96},{32,0},{64,32},{96,64},{1,97},{33,1},{65,33},{97,65},{2,98}... | collective-permute-start | bytes 1544 | tf_op jit(solution)/shard_map/ppermute | solution.py:512
  56.3 5.7 %copy-start = (bf16[32,400,128]{2,1,0:T(8,128)(2,1)}, bf16[32,400,128]{2,1,0:T(8,128)(2,1)S(1)}, u32[]{:S(2)}) copy-start(bf16[32,400,128]{2,1,0:T(8,128)(2,1)S(1)} %all-to-all-done.1.recv_ref) | copy-start | bytes 9830404
  56.3 34.9 %all-to-all-start = ((bf16[32,144,128]{2,1,0:T(8,128)(2,1)}), bf16[32,144,128]{2,1,0:T(8,128)(2,1)}, u32[]{:S(2)}, u32[]{:S(2)}) async-start(bf16[32,144,128]{2,1,0:T(8,128)(2,1)} %pack_second.1), calls=%async_computation | async-start | bytes 2359296 | tf_op jit(solution)/shard_map/all_to_all | solution.py:517
  98.2 35.1 %all-to-all-start.2 = ((bf16[32,144,128]{2,1,0:T(8,128)(2,1)}), bf16[32,144,128]{2,1,0:T(8,128)(2,1)S(1)}, u32[]{:S(2)}, u32[]{:S(2)}) async-start(bf16[32,144,128]{2,1,0:T(8,128)(2,1)} %get-tuple-element.29), calls=%async_computation.2 | async-start | bytes 2359296 | tf_op jit(solution)/shard_map/all_to_all | solution.py:517
  133.3 1.1 copy-start.2
  133.3 8.5 %copy-start.4 = (f32[2,128]{1,0:T(2,128)S(1)}, f32[2,128]{1,0:T(2,128)}, u32[]{:S(2)}) copy-start(f32[2,128]{1,0:T(2,128)} %get-tuple-element.48) | copy-start | bytes 3076
  133.3 11.7 %copy-start.3 = (f32[8]{0:T(128)S(1)}, f32[8]{0:T(128)}, u32[]{:S(2)}) copy-start(f32[8]{0:T(128)} %mixture_ref.1) | copy-start | bytes 100
  134.4 47.2 %all-to-all-start.3 = ((bf16[32,384,128]{2,1,0:T(8,128)(2,1)}), bf16[32,384,128]{2,1,0:T(8,128)(2,1)S(1)}, u32[]{:S(2)}, u32[]{:S(2)}) async-start(bf16[32,384,128]{2,1,0:T(8,128)(2,1)} %get-tuple-element.44), calls=%async_computation.3 | async-start | bytes 6291456 | tf_op jit(solution)/shard_map/all_to_all | solution.py:517
  141.8 12.6 %copy-start.7 = (f32[1,128]{1,0:T(1,128)S(1)}, f32[1,128]{1,0:T(1,128)}, u32[]{:S(2)}) copy-start(f32[1,128]{1,0:T(1,128)} %get-tuple-element.49) | copy-start | bytes 1540
  141.8 4.0 %collective-permute-start.3 = (f32[2,128]{1,0:T(2,128)S(1)}, f32[2,128]{1,0:T(2,128)S(1)}, u32[]{:S(2)}, u32[]{:S(2)}) collective-permute-start(f32[2,128]{1,0:T(2,128)S(1)} %copy-done.4), channel_id=1, source_target_pairs={{0,32},{32,64},{64,96},{96,0},{1,33},{33,65},{65,97},{97,1},{2,34}... | collective-permute-start | bytes 3080 | tf_op jit(solution)/shard_map/ppermute | solution.py:512
  141.9 4.0 %collective-permute-start.4 = (f32[2,128]{1,0:T(2,128)S(1)}, f32[2,128]{1,0:T(2,128)S(1)}, u32[]{:S(2)}, u32[]{:S(2)}) collective-permute-start(f32[2,128]{1,0:T(2,128)S(1)} %copy-done.4), channel_id=1, source_target_pairs={{0,64},{32,96},{64,0},{96,32},{1,65},{33,97},{65,1},{97,33},{2,66}... | collective-permute-start | bytes 3080 | tf_op jit(solution)/shard_map/ppermute | solution.py:512
  143.0 3.3 %collective-permute-start.5 = (f32[2,128]{1,0:T(2,128)S(1)}, f32[2,128]{1,0:T(2,128)S(1)}, u32[]{:S(2)}, u32[]{:S(2)}) collective-permute-start(f32[2,128]{1,0:T(2,128)S(1)} %copy-done.4), channel_id=1, source_target_pairs={{0,96},{32,0},{64,32},{96,64},{1,97},{33,1},{65,33},{97,65},{2,98}... | collective-permute-start | bytes 3080 | tf_op jit(solution)/shard_map/ppermute | solution.py:512
  147.8 6.5 %collective-permute-start.6 = (f32[8]{0:T(128)S(1)}, f32[8]{0:T(128)S(1)}, u32[]{:S(2)}, u32[]{:S(2)}) collective-permute-start(f32[8]{0:T(128)S(1)} %convert_reduce_fusion), channel_id=1, source_target_pairs={{0,32},{32,64},{64,96},{96,0},{1,33},{33,65},{65,97},{97,1},{2,34}... | collective-permute-start | bytes 104 | tf_op jit(solution)/shard_map/ppermute | solution.py:512
  149.3 5.0 %collective-permute-start.7 = (f32[8]{0:T(128)S(1)}, f32[8]{0:T(128)S(1)}, u32[]{:S(2)}, u32[]{:S(2)}) collective-permute-start(f32[8]{0:T(128)S(1)} %convert_reduce_fusion), channel_id=1, source_target_pairs={{0,64},{32,96},{64,0},{96,32},{1,65},{33,97},{65,1},{97,33},{2,66}... | collective-permute-start | bytes 104 | tf_op jit(solution)/shard_map/ppermute | solution.py:512
  151.6 2.7 %collective-permute-start.8 = (f32[8]{0:T(128)S(1)}, f32[8]{0:T(128)S(1)}, u32[]{:S(2)}, u32[]{:S(2)}) collective-permute-start(f32[8]{0:T(128)S(1)} %convert_reduce_fusion), channel_id=1, source_target_pairs={{0,96},{32,0},{64,32},{96,64},{1,97},{33,1},{65,33},{97,65},{2,98}... | collective-permute-start | bytes 104 | tf_op jit(solution)/shard_map/ppermute | solution.py:512
  181.5 1.6 copy-start.1

commit v4 on v3

--- a/solution.py
+++ b/solution.py
@@ -26,8 +26,11 @@
 TILES = LENGTH // TILE
 PAIR = TILE // BLOCK
 KEYS = 256
-UNROLL = 4
-MOST_PAIRS = (LENGTH * (1024 // TILE + 2) + TILES * (BLOCK - 1 + KEYS - 1)) // KEYS + UNROLL
+UNROLL = 6
+MOST_PAIRS = (LENGTH * (1024 // TILE + 1) + TILES * (BLOCK - 1 + KEYS - 1)) // KEYS
+MOST_STEPS = MOST_PAIRS // UNROLL + 1
+MOST_PAIRS = MOST_STEPS * UNROLL
+RING = 4
 SAFE_LOGIT = 70.0
 EXTRA = 16
 VMEM_LIMIT = 56 * 1024 * 1024
@@ -152,6 +155,10 @@
     return jnp.where(key_mask(span_rows_ref, i, mask_at, KEYS), scores, NEG)
 
 
+def pair_steps(total):
+    return (total + UNROLL - 1) // UNROLL
+
+
 def each_pairs(total, pair_ref, body):
     def some(n, carry):
         pairs = []
@@ -159,10 +166,15 @@
             p = n * UNROLL + u
             at = pl.multiple_of(pair_ref[1, p], BLOCK)
             pairs.append((p, pair_ref[0, p], at, pair_ref[2, p]))
-        body(pairs)
+        body(n, pairs)
         return carry
 
-    lax.fori_loop(0, (total + UNROLL - 1) // UNROLL, some, 0)
+    lax.fori_loop(0, pair_steps(total), some, 0)
+
+
+def softmax_tile(scores, span_rows_ref, norm_ref, i, mask_at):
+    scores = masked(scores, span_rows_ref, i, mask_at)
+    return jnp.exp2(scores * EXP_SCALE - norm_ref[i, 0:1, :]) * norm_ref[i, 1:2, :]
 
 
 def find_pairs(seg_all, starts, pair_ref, span_rows_ref):
@@ -206,26 +218,62 @@
     return total
 
 
+def each_tile(what):
+    def one(i, carry):
+        what(i)
+        return carry
+
+    lax.fori_loop(0, TILES, one, 0)
+
+
+def tile_blocks(i):
+    return pl.ds(i * PAIR, PAIR)
+
+
 def attend_kernel(
-    recv_ref, gains_ref,
-    pair_ref, total_ref, span_rows_ref,
-    q_hat_ref, k_hat_ref, q_turned_ref, k_turned_ref, raw_q_ref, raw_k_ref, moments_ref, norm_ref,
-    out_ref,
-    starts, v_turned, terms, fold,
+    all_ref, gains_ref,
+    pair_ref, total_ref, span_rows_ref, *refs,
 ):
-    total = find_pairs(recv_ref[:, 3 * BLOCK, :].astype(F32), starts, pair_ref, span_rows_ref)
+    hat_outs, probs_out, refs = refs[:2], refs[2], refs[3:]
+    (moments_ref, norm_ref, out_ref), refs = refs[:3], refs[3:]
+    hats, refs = refs[:2], refs[2:]
+    q_turned_ref, k_hat_ref = hats
+    recv_ref, extra_ref, starts, v_turned, terms, fold, probs, sums = refs[:8]
+    in_sems, extra_sem, out_sems, prob_sems = refs[8:]
+
+    def arrival(i):
+        return pltpu.make_async_copy(
+            all_ref.at[tile_blocks(i), pl.ds(0, 3 * BLOCK), :],
+            recv_ref.at[tile_blocks(i)],
+            in_sems.at[i],
+        )
+
+    def leaving(i, n):
+        rows = tile_at(i)
+        source, target = (
+            (q_turned_ref.at[:, rows], hat_outs[0].at[:, rows]),
+            (k_hat_ref.at[rows, :], hat_outs[1].at[rows, :]),
+            (sums.at[i], out_ref.at[i]),
+        )[n]
+        return pltpu.make_async_copy(source, target, out_sems.at[n, i])
+
+    extra = pltpu.make_async_copy(
+        all_ref.at[:, pl.ds(3 * BLOCK, EXTRA), :], extra_ref, extra_sem.at[0]
+    )
+    extra.start()
+    each_tile(lambda i: arrival(i).start())
+    extra.wait()
+    total = find_pairs(extra_ref[:, 0, :].astype(F32), starts, pair_ref, span_rows_ref)
     total_ref[0] = total
     gains = jnp.concatenate([gains_ref[...], jnp.zeros((6, HEAD_DIM), F32)], 0).T
 
     def prepare(i, most):
+        arrival(i).wait()
         rows = tile_at(i)
         v_turned[:, rows] = tile_rows(recv_ref, i * PAIR, 2).T
-        outs = ((q_hat_ref, q_turned_ref, raw_q_ref), (k_hat_ref, k_turned_ref, raw_k_ref))
         sizes = []
-        for n, (hat_ref, turned_ref, raw_ref) in enumerate(outs):
-            raw = tile_rows(recv_ref, i * PAIR, n).T
-            raw_ref[:, rows] = raw
-            values = raw.astype(F32)
+        for n in range(2):
+            values = tile_rows(recv_ref, i * PAIR, n).T.astype(F32)
             mean = mean_down(values)
             centre = values - mean
             inverse = lax.rsqrt(mean_down(centre * centre) + EPS)
@@ -233,16 +281,19 @@
             moments_ref[i, 2 * n + 1 : 2 * n + 2, :] = inverse
             hat = centre * inverse * gains[:, n : n + 1]
             sizes.append(jnp.maximum(most[n], mean_down(hat * hat)))
-            hat = hat.astype(BF16)
-            turned_ref[:, rows] = hat
-            hat_ref[rows, :] = hat.T
-        out_ref[i] = jnp.zeros((HEAD_DIM, TILE), F32)
+            if n == 0:
+                q_turned_ref[:, rows] = hat.astype(BF16)
+            else:
+                k_hat_ref[rows, :] = hat.astype(BF16).T
+        for n in range(2):
+            leaving(i, n).start()
+        sums[i] = jnp.zeros((HEAD_DIM, TILE), F32)
         norm_ref[i] = jnp.zeros((2, TILE), F32)
         fold[i] = jnp.zeros((8, TILE), F32)
         return tuple(sizes)
 
     zero = jnp.zeros((1, TILE), F32)
-    most_q, most_k = lax.fori_loop(0, TILES, prepare, (zero, zero))
+    most_q, most_k = lax.fori_loop(0, TILES, prepare, (zero, zero), unroll=TILES)
     bound = jnp.max(most_q) * jnp.max(most_k) * HEAD_DIM
 
     def scores_of(pairs):
@@ -262,7 +313,7 @@
 
         lax.fori_loop(0, TILES, clear, 0)
 
-        def top_pairs(pairs):
+        def top_pairs(n, pairs):
             for tile, (_, i, _, _) in zip(scores_of(pairs), pairs):
                 top = jnp.max(tile.reshape(KEYS // 8, 8, TILE), 0)
                 fold[i] = jnp.maximum(fold[i], top)
@@ -276,7 +327,7 @@
 
         lax.fori_loop(0, TILES, finish, 0)
 
-    def exp_pairs(pairs):
+    def exp_pairs(n, pairs):
         sums = []
         for tile, (p, i, _, _) in zip(scores_of(pairs), pairs):
             tile = jnp.exp2(tile * EXP_SCALE - norm_ref[i, 0:1, :])
@@ -293,41 +344,70 @@
 
     lax.fori_loop(0, TILES, invert, 0)
 
-    def out_pairs(pairs):
+    def give_probs(n):
+        slot = lax.rem(n, RING)
+        return pltpu.make_async_copy(probs.at[slot], probs_out.at[n], prob_sems.at[slot])
+
+    def out_pairs(n, pairs):
+        slot = lax.rem(n, RING)
+
+        @pl.when(n >= RING)
+        def _():
+            give_probs(n - RING).wait()
+
         tiles = [(terms[p] * norm_ref[i, 1:2, :]).astype(BF16) for p, i, _, _ in pairs]
+        for u, tile in enumerate(tiles):
+            probs[slot, u] = tile
+        give_probs(n).start()
         tiles = [
             dot(v_turned[:, pl.ds(at, KEYS)], tile) for tile, (_, _, at, _) in zip(tiles, pairs)
         ]
         for tile, (_, i, _, _) in zip(tiles, pairs):
-            out_ref[i] += tile
+            sums[i] += tile
 
     each_pairs(total, pair_ref, out_pairs)
+    each_tile(lambda i: leaving(i, 2).start())
+    steps = pair_steps(total)
+
+    def end(n, carry):
+        give_probs(n).wait()
+        return carry
+
+    lax.fori_loop(jnp.maximum(steps - RING, 0), steps, end, 0)
+    for n in range(3):
+        each_tile(lambda i, n=n: leaving(i, n).wait())
 
 
 def run_attend(received, gains):
+    hats = [((HEAD_DIM, LENGTH), BF16), ((LENGTH, HEAD_DIM), BF16)]
     return pl.pallas_call(
         attend_kernel,
-        in_specs=[VMEM_SPEC] * 2,
-        out_specs=[SMEM_SPEC] * 2 + [VMEM_SPEC] * 10,
+        in_specs=[ANY_SPEC, VMEM_SPEC],
+        out_specs=[SMEM_SPEC] * 2 + [VMEM_SPEC] + [ANY_SPEC] * 3 + [VMEM_SPEC] * 2 + [ANY_SPEC],
         out_shape=[
             shape((3, MOST_PAIRS), I32),
             shape((1,), I32),
             shape((TILES, 2, TILE), I32),
-            shape((LENGTH, HEAD_DIM), BF16),
-            shape((LENGTH, HEAD_DIM), BF16),
-            shape((HEAD_DIM, LENGTH), BF16),
-            shape((HEAD_DIM, LENGTH), BF16),
-            shape((HEAD_DIM, LENGTH), BF16),
-            shape((HEAD_DIM, LENGTH), BF16),
+            *[shape(*hat) for hat in hats],
+            shape((MOST_STEPS, UNROLL, KEYS, TILE), BF16),
             shape((TILES, 4, TILE), F32),
             shape((TILES, 2, TILE), F32),
             shape((TILES, HEAD_DIM, TILE), F32),
         ],
         scratch_shapes=[
+            *[pltpu.VMEM(*hat) for hat in hats],
+            pltpu.VMEM((BLOCKS, 3 * BLOCK, 128), BF16),
+            pltpu.VMEM((BLOCKS, EXTRA, 128), BF16),
             pltpu.SMEM((IMAGES + 1,), I32),
             pltpu.VMEM((HEAD_DIM, LENGTH), BF16),
             pltpu.VMEM((MOST_PAIRS, KEYS, TILE), F32),
             pltpu.VMEM((TILES, 8, TILE), F32),
+            pltpu.VMEM((RING, UNROLL, KEYS, TILE), BF16),
+            pltpu.VMEM((TILES, HEAD_DIM, TILE), F32),
+            pltpu.SemaphoreType.DMA((TILES,)),
+            pltpu.SemaphoreType.DMA((1,)),
+            pltpu.SemaphoreType.DMA((3, TILES)),
+            pltpu.SemaphoreType.DMA((RING,)),
         ],
         compiler_params=pltpu.CompilerParams(vmem_limit_bytes=VMEM_LIMIT),
         name="attend",
@@ -335,16 +415,50 @@
 
 
 def loss_kernel(
-    labels_ref, mixture_ref,
-    recv_ref, out_ref,
-    send_ref, grad_ref, grad_turned_ref, inner_ref, counts_ref,
-    coef_rows, loss_rows,
+    labels_ref, mixture_ref, pair_ref, total_ref,
+    all_ref, out_in, probs_in,
+    send_out, grad_turned_out, inner_ref, counts_ref,
+    coef_rows, loss_rows, grad_low, grad_v, probs, recv_ref, extra_ref, out_ref, first_ref, value_ref,
+    grad_turned_ref, sems, in_sems, extra_sem, out_sems,
 ):
-    seg_all = recv_ref[:, BLOCK, :].astype(F32)
+    def arrival(i, n):
+        source, target = (
+            (all_ref.at[tile_blocks(i), pl.ds(0, BLOCK), :], recv_ref.at[tile_blocks(i)]),
+            (out_in.at[i], out_ref.at[i]),
+        )[n]
+        return pltpu.make_async_copy(source, target, in_sems.at[n, i])
+
+    def leaving(i, n):
+        rows = tile_at(i)
+        blocks = tile_blocks(i)
+        source, target = (
+            (first_ref.at[blocks], send_out.at[blocks, pl.ds(0, BLOCK), :]),
+            (grad_turned_ref.at[:, rows], grad_turned_out.at[:, rows]),
+            (value_ref.at[blocks], send_out.at[blocks, pl.ds(BLOCK, BLOCK + EXTRA), :]),
+        )[n]
+        return pltpu.make_async_copy(source, target, out_sems.at[n, i])
+
+    def take_probs(n):
+        return pltpu.make_async_copy(probs_in.at[n], probs.at[n], sems.at[n])
+
+    def start_probs(n, carry):
+        take_probs(n).start()
+        return carry
+
+    extra = pltpu.make_async_copy(
+        all_ref.at[:, pl.ds(BLOCK, EXTRA), :], extra_ref, extra_sem.at[0]
+    )
+    extra.start()
+    for n in range(2):
+        each_tile(lambda i, n=n: arrival(i, n).start())
+    lax.fori_loop(0, pair_steps(total_ref[0]), start_probs, 0)
+
+    extra.wait()
+    seg_all = extra_ref[:, 0, :].astype(F32)
     group = jnp.zeros((BLOCKS, 128), F32)
     for s in range(IMAGES):
         group = jnp.where(seg_all == float(s), labels_ref[0, s].astype(F32), group)
-    others = [recv_ref[:, BLOCK + 1 + p, :].astype(F32) for p in range(PACKS)]
+    others = [extra_ref[:, 1 + p, :].astype(F32) for p in range(PACKS)]
     total_mix = mixture_ref[0]
     for g in range(1, GROUPS):
         total_mix = total_mix + mixture_ref[g]
@@ -363,6 +477,8 @@
         coef_rows[tile, 0:1, at] = coef[b : b + 1, :]
 
     def finish(i, carry):
+        for n in range(2):
+            arrival(i, n).wait()
         rows = tile_at(i)
         head_out = out_ref[i]
         misfit = head_out - tile_rows(recv_ref, i * PAIR, 0).T.astype(F32)
@@ -371,13 +487,14 @@
         inner_ref[i, 0:1, :] = jnp.sum(grad_out * head_out, 0, keepdims=True)
         grad_turned = grad_out.astype(BF16)
         grad_turned_ref[:, rows] = grad_turned
-        grad_ref[rows, :] = grad_turned.T
-        send_ref[pl.ds(i * PAIR, PAIR), 0:BLOCK, :] = head_out.astype(BF16).T.reshape(
-            PAIR, BLOCK, HEAD_DIM
-        )
+        grad_low[rows, :] = grad_turned.T
+        grad_v[rows, :] = jnp.zeros((TILE, HEAD_DIM), F32)
+        first_ref[tile_blocks(i)] = head_out.astype(BF16).T.reshape(PAIR, BLOCK, HEAD_DIM)
+        for n in range(2):
+            leaving(i, n).start()
         return carry
 
-    lax.fori_loop(0, TILES, finish, 0)
+    lax.fori_loop(0, TILES, finish, 0, unroll=TILES)
 
     rows = [block_row(b) for b in range(BLOCKS)]
     losses = jnp.concatenate([loss_rows[tile, 0:1, at] for tile, at in rows], 0)
@@ -390,59 +507,112 @@
     pieces = jnp.zeros((EXTRA, 128), F32)
     for n, piece in enumerate((high, middle, low)):
         pieces = jnp.where(row == n, piece.astype(F32), pieces)
-    send_ref[:, BLOCK:, :] = jnp.broadcast_to(pieces.astype(BF16)[None], (BLOCKS, EXTRA, 128))
-
-
-def run_loss(labels, mixture, second, head_out):
+    value_ref[:, BLOCK:, :] = jnp.broadcast_to(pieces.astype(BF16)[None], (BLOCKS, EXTRA, 128))
+
+    def add_pairs(n, pairs):
+        take_probs(n).wait()
+        tiles = [dot(probs[n, u], grad_low[tile_at(pair[1]), :]) for u, pair in enumerate(pairs)]
+        for tile, (_, _, at, _) in zip(tiles, pairs):
+            grad_v[pl.ds(at, KEYS), :] += tile
+
+    each_pairs(total_ref[0], pair_ref, add_pairs)
+
+    def give(i, carry):
+        value_ref[pl.ds(i * PAIR, PAIR), 0:BLOCK, :] = (
+            grad_v[tile_at(i), :].astype(BF16).reshape(PAIR, BLOCK, HEAD_DIM)
+        )
+        leaving(i, 2).start()
+        return carry
+
+    lax.fori_loop(0, TILES, give, 0, unroll=TILES)
+    for n in range(3):
+        each_tile(lambda i, n=n: leaving(i, n).wait())
+
+
+def run_loss(labels, mixture, pairs, total, second, head_out, probs):
     return pl.pallas_call(
         loss_kernel,
-        in_specs=[SMEM_SPEC] * 2 + [VMEM_SPEC] * 2,
-        out_specs=[VMEM_SPEC] * 5,
+        in_specs=[SMEM_SPEC] * 4 + [ANY_SPEC] * 3,
+        out_specs=[ANY_SPEC] * 2 + [VMEM_SPEC] * 2,
         out_shape=[
-            shape((BLOCKS, BLOCK + EXTRA, 128), BF16),
-            shape((LENGTH, HEAD_DIM), BF16),
+            shape((BLOCKS, 2 * BLOCK + EXTRA, 128), BF16),
             shape((HEAD_DIM, LENGTH), BF16),
             shape((TILES, 1, TILE), F32),
             shape((1, 128), F32),
         ],
-        scratch_shapes=[pltpu.VMEM((TILES, 1, TILE), F32), pltpu.VMEM((TILES, 1, TILE), F32)],
+        scratch_shapes=[
+            pltpu.VMEM((TILES, 1, TILE), F32),
+            pltpu.VMEM((TILES, 1, TILE), F32),
+            pltpu.VMEM((LENGTH, HEAD_DIM), BF16),
+            pltpu.VMEM((LENGTH, HEAD_DIM), F32),
+            pltpu.VMEM((MOST_STEPS, UNROLL, KEYS, TILE), BF16),
+            pltpu.VMEM((BLOCKS, BLOCK, 128), BF16),
+            pltpu.VMEM((BLOCKS, EXTRA, 128), BF16),
+            pltpu.VMEM((TILES, HEAD_DIM, TILE), F32),
+            pltpu.VMEM((BLOCKS, BLOCK, 128), BF16),
+            pltpu.VMEM((BLOCKS, BLOCK + EXTRA, 128), BF16),
+            pltpu.VMEM((HEAD_DIM, LENGTH), BF16),
+            pltpu.SemaphoreType.DMA((MOST_STEPS,)),
+            pltpu.SemaphoreType.DMA((2, TILES)),
+            pltpu.SemaphoreType.DMA((1,)),
+            pltpu.SemaphoreType.DMA((3, TILES)),
+        ],
         compiler_params=pltpu.CompilerParams(vmem_limit_bytes=VMEM_LIMIT),
-        name="loss",
-    )(labels, mixture, second, head_out)
+        name="loss_and_grad_value",
+    )(labels, mixture, pairs, total, second, head_out, probs)
 
 
 def backward_kernel(
     pair_ref, total_ref,
-    recv_ref, gains_ref, q_hat_ref, k_hat_ref, q_turned_ref, k_turned_ref, raw_q_ref, raw_k_ref,
-    moments_ref, span_rows_ref, norm_ref, grad_ref, grad_turned_ref, inner_ref,
-    send_ref, gain_out_ref,
-    grad_q, grad_k, grad_v,
+    all_ref, q_turned_in, k_hat_in, grad_turned_in,
+    gains_ref, moments_ref, span_rows_ref, norm_ref, inner_ref,
+    send_out, gain_out_ref,
+    grad_q, grad_k, q_hat_ref, k_turned_ref, value_ref, raw_ref, q_turned_ref, k_hat_ref,
+    grad_turned_ref, send_ref, in_sems, out_sems,
 ):
+    def arrival(i, n):
+        rows = tile_at(i)
+        blocks = tile_blocks(i)
+        source, target = (
+            (q_turned_in.at[:, rows], q_turned_ref.at[:, rows]),
+            (k_hat_in.at[rows, :], k_hat_ref.at[rows, :]),
+            (all_ref.at[blocks, pl.ds(2 * BLOCK, BLOCK), :], value_ref.at[blocks]),
+            (grad_turned_in.at[:, rows], grad_turned_ref.at[:, rows]),
+            (all_ref.at[blocks, pl.ds(0, 2 * BLOCK), :], raw_ref.at[blocks]),
+        )[n]
+        return pltpu.make_async_copy(source, target, in_sems.at[n, i])
+
+    def leaving(i):
+        blocks = tile_blocks(i)
+        return pltpu.make_async_copy(send_ref.at[blocks], send_out.at[blocks], out_sems.at[i])
+
+    for n in range(5):
+        each_tile(lambda i, n=n: arrival(i, n).start())
+
     def clear(i, carry):
+        for n in range(2):
+            arrival(i, n).wait()
+        q_hat_ref[tile_at(i), :] = q_turned_ref[:, tile_at(i)].T
+        k_turned_ref[:, tile_at(i)] = k_hat_ref[tile_at(i), :].T
         grad_q[i] = jnp.zeros((HEAD_DIM, TILE), F32)
         grad_k[tile_at(i), :] = jnp.zeros((TILE, HEAD_DIM), F32)
-        grad_v[tile_at(i), :] = jnp.zeros((TILE, HEAD_DIM), F32)
         return carry
 
-    lax.fori_loop(0, TILES, clear, 0)
-
-    def add_pairs(pairs):
+    lax.fori_loop(0, TILES, clear, 0, unroll=TILES)
+    for n in (2, 3):
+        each_tile(lambda i, n=n: arrival(i, n).wait())
+
+    def add_pairs(n, pairs):
         tiles = [
             dot(k_hat_ref[pl.ds(at, KEYS), :], q_turned_ref[:, tile_at(i)]) for _, i, at, _ in pairs
         ]
         prob_grads = [
-            dot(tile_rows(recv_ref, at // BLOCK, 2, KEYS), grad_turned_ref[:, tile_at(i)])
+            dot(tile_rows(value_ref, at // BLOCK, 0, KEYS), grad_turned_ref[:, tile_at(i)])
             for _, i, at, _ in pairs
         ]
         tiles = [
-            jnp.exp2(
-                masked(tile, span_rows_ref, i, mask_at) * EXP_SCALE - norm_ref[i, 0:1, :]
-            ) * norm_ref[i, 1:2, :]
+            softmax_tile(tile, span_rows_ref, norm_ref, i, mask_at)
             for tile, (_, i, _, mask_at) in zip(tiles, pairs)
-        ]
-        values = [
-            dot(tile.astype(BF16), grad_ref[tile_at(i), :])
-            for tile, (_, i, _, _) in zip(tiles, pairs)
         ]
         tiles = [
             (tile * (prob - inner_ref[i, 0:1, :]) * SCALE).astype(BF16)
@@ -452,8 +622,7 @@
         queries = [
             dot(k_turned_ref[:, pl.ds(at, KEYS)], tile) for tile, (_, _, at, _) in zip(tiles, pairs)
         ]
-        for value, key, query, (_, i, at, _) in zip(values, keys, queries, pairs):
-            grad_v[pl.ds(at, KEYS), :] += value
+        for key, query, (_, i, at, _) in zip(keys, queries, pairs):
             grad_k[pl.ds(at, KEYS), :] += key
             grad_q[i] += query
 
@@ -461,10 +630,10 @@
 
     gains = jnp.concatenate([gains_ref[...], jnp.zeros((6, HEAD_DIM), F32)], 0).T
 
-    def norm_backward(i, n, grad_hat, raw_ref):
+    def norm_backward(i, n, grad_hat):
         mean = moments_ref[i, 2 * n : 2 * n + 1, :]
         inverse = moments_ref[i, 2 * n + 1 : 2 * n + 2, :]
-        normed = (raw_ref[:, tile_at(i)].astype(F32) - mean) * inverse
+        normed = (tile_rows(raw_ref, i * PAIR, n).T.astype(F32) - mean) * inverse
         grad_normed = grad_hat * gains[:, n : n + 1]
         inner = mean_down(grad_normed * normed)
         grad_in = inverse * (grad_normed - mean_down(grad_normed) - normed * inner)
@@ -475,34 +644,43 @@
         return sum(grad_gain[:, c : c + 128] for c in range(0, TILE, 128))
 
     def finish(i, gain_sums):
+        arrival(i, 4).wait()
         gain_q, gain_k = gain_sums
-        gain_q = gain_q + norm_backward(i, 0, grad_q[i], raw_q_ref)
-        gain_k = gain_k + norm_backward(i, 1, grad_k[tile_at(i), :].T, raw_k_ref)
-        send_ref[pl.ds(i * PAIR, PAIR), 2 * BLOCK :, :] = (
-            grad_v[tile_at(i), :].astype(BF16).reshape(PAIR, BLOCK, HEAD_DIM)
-        )
+        gain_q = gain_q + norm_backward(i, 0, grad_q[i])
+        gain_k = gain_k + norm_backward(i, 1, grad_k[tile_at(i), :].T)
+        leaving(i).start()
         return gain_q, gain_k
 
     zero = jnp.zeros((HEAD_DIM, 128), F32)
-    gain_q, gain_k = lax.fori_loop(0, TILES, finish, (zero, zero))
+    gain_q, gain_k = lax.fori_loop(0, TILES, finish, (zero, zero), unroll=TILES)
     gain_out_ref[0:1, :] = jnp.sum(gain_q.T, 0, keepdims=True)
     gain_out_ref[1:2, :] = jnp.sum(gain_k.T, 0, keepdims=True)
-
-
-def run_backward(pairs, total, *arrays):
+    each_tile(lambda i: leaving(i).wait())
+
+
+def run_backward(pairs, total, received, q_turned, k_hat, grad_turned, *arrays):
     return pl.pallas_call(
         backward_kernel,
-        in_specs=[SMEM_SPEC] * 2 + [VMEM_SPEC] * len(arrays),
-        out_specs=[VMEM_SPEC] * 2,
-        out_shape=[shape((BLOCKS, 3 * BLOCK, 128), BF16), shape((2, HEAD_DIM), F32)],
+        in_specs=[SMEM_SPEC] * 2 + [ANY_SPEC] * 4 + [VMEM_SPEC] * len(arrays),
+        out_specs=[ANY_SPEC, VMEM_SPEC],
+        out_shape=[shape((BLOCKS, 2 * BLOCK, 128), BF16), shape((2, HEAD_DIM), F32)],
         scratch_shapes=[
             pltpu.VMEM((TILES, HEAD_DIM, TILE), F32),
             pltpu.VMEM((LENGTH, HEAD_DIM), F32),
-            pltpu.VMEM((LENGTH, HEAD_DIM), F32),
+            pltpu.VMEM((LENGTH, HEAD_DIM), BF16),
+            pltpu.VMEM((HEAD_DIM, LENGTH), BF16),
+            pltpu.VMEM((BLOCKS, BLOCK, 128), BF16),
+            pltpu.VMEM((BLOCKS, 2 * BLOCK, 128), BF16),
+            pltpu.VMEM((HEAD_DIM, LENGTH), BF16),
+            pltpu.VMEM((LENGTH, HEAD_DIM), BF16),
+            pltpu.VMEM((HEAD_DIM, LENGTH), BF16),
+            pltpu.VMEM((BLOCKS, 2 * BLOCK, 128), BF16),
+            pltpu.SemaphoreType.DMA((5, TILES)),
+            pltpu.SemaphoreType.DMA((TILES,)),
         ],
         compiler_params=pltpu.CompilerParams(vmem_limit_bytes=VMEM_LIMIT),
         name="backward",
-    )(pairs, total, *arrays)
+    )(pairs, total, received, q_turned, k_hat, grad_turned, *arrays)
 
 
 def over_packs(value):
@@ -528,22 +706,24 @@
     extra = jnp.concatenate([segment_ids.astype(F32), *over_packs(labels.astype(F32))], 0)
     second = exchange(pack_rows((target_rows,), extra, "pack_second"))
 
-    pairs, total, span_rows, *hats, moments, norms, head_out = run_attend(first, gains)
-    send, *grads, counts = run_loss(group_labels, mixture, second, head_out)
+    pairs, total, span_rows, *hats, probs, moments, norms, head_out = run_attend(first, gains)
+    send, grad_turned, inner, counts = run_loss(
+        group_labels, mixture, pairs, total, second, head_out, probs
+    )
     back = exchange(send)
     send, gain_part = run_backward(
-        pairs, total, first, gains, *hats, moments, span_rows, norms, *grads
+        pairs, total, first, *hats, grad_turned, gains, moments, span_rows, norms, inner
     )
     last = exchange(send)
-    (attended,) = unpack_rows(back, 1, "unpack_first")
-    losses = jnp.sum(back[:, BLOCK : BLOCK + 3, :GROUPS].astype(F32), (0, 1))
+    attended, grad_value = unpack_rows(back, 2, "unpack_first")
+    losses = jnp.sum(back[:, 2 * BLOCK : 2 * BLOCK + 3, :GROUPS].astype(F32), (0, 1))
     group_total = sum(over_packs(losses))
     group_loss = group_total / (counts[0, :GROUPS] * (HEADS * HEAD_DIM))
     shares = mixture / jnp.sum(mixture)
     raised = shares * jnp.exp(ETA * group_loss)
     new_mixture = raised / jnp.sum(raised)
     grad_gains = sum(over_packs(gain_part)).reshape(2, 1, HEAD_DIM)
-    grad_query, grad_key, grad_value = unpack_rows(last, 3, "unpack_last")
+    grad_query, grad_key = unpack_rows(last, 2, "unpack_last")
     return (attended, grad_query, grad_key, grad_value, grad_gains, new_mixture)
 
 

time: 188 us -> 205 us (1.090)
  blocking collectives: 0 us -> 35.6 us
  waiting for transfers between devices: 57.6 us -> 43.5 us
  starting transfers between devices: 42.2 us -> 51.6 us
  Pallas kernels: 79 us -> 70.1 us
  local copies, waits for them, and re-layouts: 3.31 us -> 0.64 us
    all_to_all x0 -> x1, blocking collectives: none -> 35.6 us  [exchange(): return lax.all_to_all(slab, 'seq', split_axis=0, concat_axis=0, tiled=True)]
    ppermute x9, starting transfers between devices: 12.3 us -> 32.4 us  [over_packs(): moved.append(lax.ppermute(value, 'pack', pairs))]
    all_to_all x4 -> x3, waiting for transfers between devices: 55.2 us -> 41.7 us  [exchange(): return lax.all_to_all(slab, 'seq', split_axis=0, concat_axis=0, tiled=True)]
    all_to_all x4 -> x3, starting transfers between devices: 29.9 us -> 19.2 us  [exchange(): return lax.all_to_all(slab, 'seq', split_axis=0, concat_axis=0, tiled=True)]
    pallas_call x3, Pallas kernels: 63.9 us -> 54.9 us  [the longest x1 22 us: run_attend(): pl.pallas_call(attend_kernel, in_specs=[ANY_SPEC, VMEM_SPEC], out_specs=[...]
    unnamed x16 -> x14, local copies, waits for them, and re-layouts: 2.7 us -> 0.03 us
  transfers between devices with their start and end apart: 13 -> 12, of which waited for: 7 -> 5; matrix products, arithmetic and copies ran while one was open for 3% -> 1% of each run, Pallas kernels for 33% -> 16%
where the time goes in v4:
time: 205 us; the launch traced here: 206 us
  Pallas kernels  70.1 us (34%)
  starting transfers between devices  51.6 us (25%)
  waiting for transfers between devices  43.5 us (21%)
  blocking collectives  35.6 us (17%)
  other arithmetic  3.75 us (2%)
    all_to_all x3, waiting for transfers between devices, exchange(): return lax.all_to_all(slab, 'seq', split_axis=0, concat_axis=0, tiled=True)  41.7 us
    all_to_all x1, blocking collectives, exchange(): return lax.all_to_all(slab, 'seq', split_axis=0, concat_axis=0, tiled=True)  35.6 us
    ppermute x9, starting transfers between devices, over_packs(): moved.append(lax.ppermute(value, 'pack', pairs))  32.4 us
    pallas_call x1, Pallas kernels, run_attend(): pl.pallas_call(attend_kernel, in_specs=[ANY_SPEC, VMEM_SPEC], out_specs=[...  22 us
    pallas_call x1, Pallas kernels, run_backward(): pl.pallas_call(backward_kernel, in_specs=[SMEM_SPEC] * 2 + [ANY_SPEC] * 4...  20.9 us
    all_to_all x3, starting transfers between devices, exchange(): return lax.all_to_all(slab, 'seq', split_axis=0, concat_axis=0, tiled=True)  19.2 us
    pallas_call x1, Pallas kernels, run_loss(): pl.pallas_call(loss_kernel, in_specs=[SMEM_SPEC] * 4 + [ANY_SPEC] * 3, ou...  12 us
    pallas_call x2, Pallas kernels, pack_rows(): pl.pallas_call(functools.partial(pack_kernel, len(rows)), in_specs=[ANY_S...  8.29 us
  transfers between devices with their start and end apart: 12, of which 5 were waited for; matrix products, arithmetic and copies ran while one was open for 1% of the time, Pallas kernels for 16%

profile of v4, /device:TPU:1, one launch (start us, length us, event | category | flops | bytes accessed | tf_op | source)
XLA Modules:
  0.0 206.1 jit_solution(15904167401756692713)
XLA Ops:
  0.6 5.1 %pack_first.1 = bf16[32,400,128]{2,1,0:T(8,128)(2,1)} custom-call(bf16[1,128,4096]{2,1,0:T(8,128)(2,1)} %refs_0_.2, bf16[1,128,4096]{2,1,0:T(8,128)(2,1)} %refs_1_.1, bf16[1,128,4096]{2,1,0:T(8,128)(2,1)} %refs_2_.1, s32[1,128]{1,0:T(1,128)} %refs_3_.1), custom_call_target="tpu_custom_call" | custom-call | tf_op jit(solution)/shard_map/pack_first/pallas_call | solution.py:78
  5.7 9.4 %all-to-all-start = ((bf16[32,400,128]{2,1,0:T(8,128)(2,1)}), bf16[32,400,128]{2,1,0:T(8,128)(2,1)S(1)}, u32[]{:S(2)}, u32[]{:S(2)}) async-start(bf16[32,400,128]{2,1,0:T(8,128)(2,1)} %pack_first.1), calls=%async_computation | async-start | bytes 6553600 | tf_op jit(solution)/shard_map/all_to_all | solution.py:695
  15.2 0.1 select_reduce_fusion
  15.3 1.4 collective-permute-start
  16.7 2.6 %collective-permute-start.1 = (f32[1,128]{1,0:T(1,128)S(1)}, f32[1,128]{1,0:T(1,128)S(1)}, u32[]{:S(2)}, u32[]{:S(2)}) collective-permute-start(f32[1,128]{1,0:T(1,128)S(1)} %convert_bitcast_fusion), channel_id=1, source_target_pairs={{0,64},{32,96},{64,0},{96,32},{1,65},{33,97},{65,1},{97,33},{2,66}... | collective-permute-start | bytes 1544 | tf_op jit(solution)/shard_map/ppermute | solution.py:690
  19.3 1.1 collective-permute-start.2
  20.3 0.2 collective-permute-done.1
  20.5 1.4 collective-permute-done.2
  22.0 0.6 concatenate.3.refs_1_
  22.6 3.2 %pack_second.1 = bf16[32,144,128]{2,1,0:T(8,128)(2,1)} custom-call(bf16[1,128,4096]{2,1,0:T(8,128)(2,1)} %refs_0_.3, f32[5,128]{1,0:T(8,128)} %concatenate.3.refs_1_), custom_call_target="tpu_custom_call" | custom-call | tf_op jit(solution)/shard_map/pack_second/pallas_call | solution.py:78
  25.8 30.5 %all-to-all-done.all_ref = bf16[32,400,128]{2,1,0:T(8,128)(2,1)S(1)} async-done(((bf16[32,400,128]{2,1,0:T(8,128)(2,1)}), bf16[32,400,128]{2,1,0:T(8,128)(2,1)S(1)}, u32[]{:S(2)}, u32[]{:S(2)}) %all-to-all-start) | async-done | bytes 3276832 | tf_op jit(solution)/shard_map/all_to_all | solution.py:695
  56.3 5.7 %all-to-all-start.1 = ((bf16[32,144,128]{2,1,0:T(8,128)(2,1)}), bf16[32,144,128]{2,1,0:T(8,128)(2,1)}, u32[]{:S(2)}, u32[]{:S(2)}) async-start(bf16[32,144,128]{2,1,0:T(8,128)(2,1)} %pack_second.1), calls=%async_computation.1 | async-start | bytes 2359296 | tf_op jit(solution)/shard_map/all_to_all | solution.py:695
  62.0 22.0 %attend.1 = (s32[3,108]{1,0:T(4,128)}, s32[1]{0:T(128)}, s32[16,2,256]{2,1,0:T(2,128)}, bf16[128,4096]{1,0:T(8,128)(2,1)}, bf16[4096,128]{1,0:T(8,128)(2,1)}, /*...) custom-call(bf16[32,400,128]{2,1,0:T(8,128)(2,1)} %copy-done, ...), custom_call_target="tpu_custom_call" | custom-call | tf_op jit(solution)/shard_map/attend/pallas_call | solution.py:383
  84.1 12.0 %loss_and_grad_value.1 = (bf16[32,272,128]{2,1,0:T(8,128)(2,1)}, bf16[128,4096]{1,0:T(8,128)(2,1)}, f32[16,1,256]{2,1,0:T(1,128)}, f32[1,128]{1,0:T(1,128)}) custom-call(s32[1,16]{1,0:T(1,128)} %labels_ref.1, f32[8]{0:T(128)} %mixture_ref.1, s32[3,108]{1,0:T(4,128)} %get-tuple-element.25.pair_ref, s32[1]{0:T(128)} %get-tuple-element.26.total_ref, ...), custom_call_target="tpu_custom_call" | custom-call | tf_op jit(solution)/shard_map/loss_and_grad_value/pallas_call | solution.py:533
  96.1 20.9 %backward.1 = (bf16[32,256,128]{2,1,0:T(8,128)(2,1)}, f32[2,128]{1,0:T(2,128)}) custom-call(s32[3,108]{1,0:T(4,128)} %get-tuple-element.25.pair_ref, s32[1]{0:T(128)} %get-tuple-element.26.total_ref, bf16[32,400,128]{2,1,0:T(8,128)(2,1)} %copy-done, bf16[128,4096]{1,0:T(8,128)(2,1)} %get-tuple-element.31.q_turned_in, ...), custom_call_target="tpu_custom_call" | custom-call | tf_op jit(solution)/shard_map/backward/pallas_call | solution.py:662
  117.0 35.6 %all_to_all.20.in_ref = bf16[32,256,128]{2,1,0:T(8,128)(2,1)} all-to-all(bf16[32,256,128]{2,1,0:T(8,128)(2,1)} %get-tuple-element.38), channel_id=1, replica_groups=mesh['pack'=4,'seq'=32] {'seq'}, dimensions={0} | all-to-all | bytes 4194304 | tf_op jit(solution)/shard_map/all_to_all | solution.py:695
  152.6 4.1 %all-to-all-start.2 = ((bf16[32,272,128]{2,1,0:T(8,128)(2,1)}), bf16[32,272,128]{2,1,0:T(8,128)(2,1)S(1)}, u32[]{:S(2)}, u32[]{:S(2)}) async-start(bf16[32,272,128]{2,1,0:T(8,128)(2,1)} %get-tuple-element.29), calls=%async_computation.2 | async-start | bytes 4456448 | tf_op jit(solution)/shard_map/all_to_all | solution.py:695
  156.7 4.1 %collective-permute-start.3 = (f32[2,128]{1,0:T(2,128)S(1)}, f32[2,128]{1,0:T(2,128)S(1)}, u32[]{:S(2)}, u32[]{:S(2)}) collective-permute-start(f32[2,128]{1,0:T(2,128)S(1)} %copy-done.3), channel_id=1, source_target_pairs={{0,32},{32,64},{64,96},{96,0},{1,33},{33,65},{65,97},{97,1},{2,34}... | collective-permute-start | bytes 3080 | tf_op jit(solution)/shard_map/ppermute | solution.py:690
  160.9 7.5 %collective-permute-start.4 = (f32[2,128]{1,0:T(2,128)S(1)}, f32[2,128]{1,0:T(2,128)S(1)}, u32[]{:S(2)}, u32[]{:S(2)}) collective-permute-start(f32[2,128]{1,0:T(2,128)S(1)} %copy-done.3), channel_id=1, source_target_pairs={{0,64},{32,96},{64,0},{96,32},{1,65},{33,97},{65,1},{97,33},{2,66}... | collective-permute-start | bytes 3080 | tf_op jit(solution)/shard_map/ppermute | solution.py:690
  168.4 2.0 collective-permute-start.5
  170.4 0.6 reduce_sum.37
  171.0 0.1 collective-permute-done.5
  171.1 0.6 add_add_fusion
  171.7 3.4 %unpack_last.1 = (bf16[1,128,4096]{2,1,0:T(8,128)(2,1)}, bf16[1,128,4096]{2,1,0:T(8,128)(2,1)}) custom-call(bf16[32,256,128]{2,1,0:T(8,128)(2,1)} %all_to_all.20.in_ref), custom_call_target="tpu_custom_call" | custom-call | tf_op jit(solution)/shard_map/unpack_last/pallas_call | solution.py:106
  175.2 11.3 %all-to-all-done.2.in_ref = bf16[32,272,128]{2,1,0:T(8,128)(2,1)S(1)} async-done(((bf16[32,272,128]{2,1,0:T(8,128)(2,1)}), bf16[32,272,128]{2,1,0:T(8,128)(2,1)S(1)}, u32[]{:S(2)}, u32[]{:S(2)}) %all-to-all-start.2) | async-done | bytes 2228256 | tf_op jit(solution)/shard_map/all_to_all | solution.py:695
  186.4 0.1 convert_reduce_fusion
  186.5 4.1 %collective-permute-start.6 = (f32[8]{0:T(128)S(1)}, f32[8]{0:T(128)S(1)}, u32[]{:S(2)}, u32[]{:S(2)}) collective-permute-start(f32[8]{0:T(128)S(1)} %convert_reduce_fusion), channel_id=1, source_target_pairs={{0,32},{32,64},{64,96},{96,0},{1,33},{33,65},{65,97},{97,1},{2,34}... | collective-permute-start | bytes 104 | tf_op jit(solution)/shard_map/ppermute | solution.py:690
  190.6 7.5 %collective-permute-start.7 = (f32[8]{0:T(128)S(1)}, f32[8]{0:T(128)S(1)}, u32[]{:S(2)}, u32[]{:S(2)}) collective-permute-start(f32[8]{0:T(128)S(1)} %convert_reduce_fusion), channel_id=1, source_target_pairs={{0,64},{32,96},{64,0},{96,32},{1,65},{33,97},{65,1},{97,33},{2,66}... | collective-permute-start | bytes 104 | tf_op jit(solution)/shard_map/ppermute | solution.py:690
  198.2 2.0 collective-permute-start.8
  200.1 3.5 %unpack_first.1 = (bf16[1,128,4096]{2,1,0:T(8,128)(2,1)}, bf16[1,128,4096]{2,1,0:T(8,128)(2,1)}) custom-call(bf16[32,272,128]{2,1,0:T(8,128)(2,1)} %copy-done.1), custom_call_target="tpu_custom_call" | custom-call | tf_op jit(solution)/shard_map/unpack_first/pallas_call | solution.py:106
  203.7 1.3 fusion
  205.0 1.2 broadcast_divide_fusion
  (23 shorter events, 0.1 us)
Async XLA Ops:
  5.7 9.5 %copy-start.4 = (s32[1,128]{1,0:T(1,128)S(1)}, s32[1,128]{1,0:T(1,128)}, u32[]{:S(2)}) copy-start(s32[1,128]{1,0:T(1,128)} %refs_3_.1) | copy-start | bytes 1540
  5.7 9.5 %copy-start.5 = (s32[1,16]{1,0:T(1,128)S(1)}, s32[1,16]{1,0:T(1,128)}, u32[]{:S(2)}) copy-start(s32[1,16]{1,0:T(1,128)} %labels_ref.1) | copy-start | bytes 196
  5.7 50.5 %all-to-all-start = ((bf16[32,400,128]{2,1,0:T(8,128)(2,1)}), bf16[32,400,128]{2,1,0:T(8,128)(2,1)S(1)}, u32[]{:S(2)}, u32[]{:S(2)}) async-start(bf16[32,400,128]{2,1,0:T(8,128)(2,1)} %pack_first.1), calls=%async_computation | async-start | bytes 6553600 | tf_op jit(solution)/shard_map/all_to_all | solution.py:695
  15.3 5.1 %collective-permute-start = (f32[1,128]{1,0:T(1,128)S(1)}, f32[1,128]{1,0:T(1,128)S(1)}, u32[]{:S(2)}, u32[]{:S(2)}) collective-permute-start(f32[1,128]{1,0:T(1,128)S(1)} %convert_bitcast_fusion), channel_id=1, source_target_pairs={{0,32},{32,64},{64,96},{96,0},{1,33},{33,65},{65,97},{97,1},{2,34}... | collective-permute-start | bytes 1544 | tf_op jit(solution)/shard_map/ppermute | solution.py:690
  16.7 3.9 %collective-permute-start.1 = (f32[1,128]{1,0:T(1,128)S(1)}, f32[1,128]{1,0:T(1,128)S(1)}, u32[]{:S(2)}, u32[]{:S(2)}) collective-permute-start(f32[1,128]{1,0:T(1,128)S(1)} %convert_bitcast_fusion), channel_id=1, source_target_pairs={{0,64},{32,96},{64,0},{96,32},{1,65},{33,97},{65,1},{97,33},{2,66}... | collective-permute-start | bytes 1544 | tf_op jit(solution)/shard_map/ppermute | solution.py:690
  19.3 2.7 %collective-permute-start.2 = (f32[1,128]{1,0:T(1,128)S(1)}, f32[1,128]{1,0:T(1,128)S(1)}, u32[]{:S(2)}, u32[]{:S(2)}) collective-permute-start(f32[1,128]{1,0:T(1,128)S(1)} %convert_bitcast_fusion), channel_id=1, source_target_pairs={{0,96},{32,0},{64,32},{96,64},{1,97},{33,1},{65,33},{97,65},{2,98}... | collective-permute-start | bytes 1544 | tf_op jit(solution)/shard_map/ppermute | solution.py:690
  56.3 5.7 %copy-start = (bf16[32,400,128]{2,1,0:T(8,128)(2,1)}, bf16[32,400,128]{2,1,0:T(8,128)(2,1)S(1)}, u32[]{:S(2)}) copy-start(bf16[32,400,128]{2,1,0:T(8,128)(2,1)S(1)} %all-to-all-done.all_ref) | copy-start | bytes 9830404
  56.3 27.8 %all-to-all-start.1 = ((bf16[32,144,128]{2,1,0:T(8,128)(2,1)}), bf16[32,144,128]{2,1,0:T(8,128)(2,1)}, u32[]{:S(2)}, u32[]{:S(2)}) async-start(bf16[32,144,128]{2,1,0:T(8,128)(2,1)} %pack_second.1), calls=%async_computation.1 | async-start | bytes 2359296 | tf_op jit(solution)/shard_map/all_to_all | solution.py:695
  152.6 4.1 %copy-start.3 = (f32[2,128]{1,0:T(2,128)S(1)}, f32[2,128]{1,0:T(2,128)}, u32[]{:S(2)}) copy-start(f32[2,128]{1,0:T(2,128)} %get-tuple-element.42) | copy-start | bytes 3076
  152.6 17.8 %copy-start.2 = (f32[8]{0:T(128)S(1)}, f32[8]{0:T(128)}, u32[]{:S(2)}) copy-start(f32[8]{0:T(128)} %mixture_ref.1) | copy-start | bytes 100
  152.6 33.8 %all-to-all-start.2 = ((bf16[32,272,128]{2,1,0:T(8,128)(2,1)}), bf16[32,272,128]{2,1,0:T(8,128)(2,1)S(1)}, u32[]{:S(2)}, u32[]{:S(2)}) async-start(bf16[32,272,128]{2,1,0:T(8,128)(2,1)} %get-tuple-element.29), calls=%async_computation.2 | async-start | bytes 4456448 | tf_op jit(solution)/shard_map/all_to_all | solution.py:695
  156.7 46.9 %copy-start.6 = (f32[1,128]{1,0:T(1,128)S(1)}, f32[1,128]{1,0:T(1,128)}, u32[]{:S(2)}) copy-start(f32[1,128]{1,0:T(1,128)} %get-tuple-element.43) | copy-start | bytes 1540
  156.7 14.3 %collective-permute-start.3 = (f32[2,128]{1,0:T(2,128)S(1)}, f32[2,128]{1,0:T(2,128)S(1)}, u32[]{:S(2)}, u32[]{:S(2)}) collective-permute-start(f32[2,128]{1,0:T(2,128)S(1)} %copy-done.3), channel_id=1, source_target_pairs={{0,32},{32,64},{64,96},{96,0},{1,33},{33,65},{65,97},{97,1},{2,34}... | collective-permute-start | bytes 3080 | tf_op jit(solution)/shard_map/ppermute | solution.py:690
  160.9 10.1 %collective-permute-start.4 = (f32[2,128]{1,0:T(2,128)S(1)}, f32[2,128]{1,0:T(2,128)S(1)}, u32[]{:S(2)}, u32[]{:S(2)}) collective-permute-start(f32[2,128]{1,0:T(2,128)S(1)} %copy-done.3), channel_id=1, source_target_pairs={{0,64},{32,96},{64,0},{96,32},{1,65},{33,97},{65,1},{97,33},{2,66}... | collective-permute-start | bytes 3080 | tf_op jit(solution)/shard_map/ppermute | solution.py:690
  168.4 2.7 %collective-permute-start.5 = (f32[2,128]{1,0:T(2,128)S(1)}, f32[2,128]{1,0:T(2,128)S(1)}, u32[]{:S(2)}, u32[]{:S(2)}) collective-permute-start(f32[2,128]{1,0:T(2,128)S(1)} %copy-done.3), channel_id=1, source_target_pairs={{0,96},{32,0},{64,32},{96,64},{1,97},{33,1},{65,33},{97,65},{2,98}... | collective-permute-start | bytes 3080 | tf_op jit(solution)/shard_map/ppermute | solution.py:690
  186.4 13.7 %copy-start.1 = (bf16[32,272,128]{2,1,0:T(8,128)(2,1)}, bf16[32,272,128]{2,1,0:T(8,128)(2,1)S(1)}, u32[]{:S(2)}) copy-start(bf16[32,272,128]{2,1,0:T(8,128)(2,1)S(1)} %all-to-all-done.2.in_ref) | copy-start | bytes 6684676
  186.5 17.1 %collective-permute-start.6 = (f32[8]{0:T(128)S(1)}, f32[8]{0:T(128)S(1)}, u32[]{:S(2)}, u32[]{:S(2)}) collective-permute-start(f32[8]{0:T(128)S(1)} %convert_reduce_fusion), channel_id=1, source_target_pairs={{0,32},{32,64},{64,96},{96,0},{1,33},{33,65},{65,97},{97,1},{2,34}... | collective-permute-start | bytes 104 | tf_op jit(solution)/shard_map/ppermute | solution.py:690
  190.6 13.0 %collective-permute-start.7 = (f32[8]{0:T(128)S(1)}, f32[8]{0:T(128)S(1)}, u32[]{:S(2)}, u32[]{:S(2)}) collective-permute-start(f32[8]{0:T(128)S(1)} %convert_reduce_fusion), channel_id=1, source_target_pairs={{0,64},{32,96},{64,0},{96,32},{1,65},{33,97},{65,1},{97,33},{2,66}... | collective-permute-start | bytes 104 | tf_op jit(solution)/shard_map/ppermute | solution.py:690
  198.2 5.5 %collective-permute-start.8 = (f32[8]{0:T(128)S(1)}, f32[8]{0:T(128)S(1)}, u32[]{:S(2)}, u32[]{:S(2)}) collective-permute-start(f32[8]{0:T(128)S(1)} %convert_reduce_fusion), channel_id=1, source_target_pairs={{0,96},{32,0},{64,32},{96,64},{1,97},{33,1},{65,33},{97,65},{2,98}... | collective-permute-start | bytes 104 | tf_op jit(solution)/shard_map/ppermute | solution.py:690

commit v5 on v4

--- a/solution.py
+++ b/solution.py
@@ -38,6 +38,8 @@
 BF16 = jnp.bfloat16
 F32 = jnp.float32
 I32 = jnp.int32
+
+WORK = pl.CostEstimate(flops=1 << 33, bytes_accessed=1 << 25, transcendentals=1 << 22)
 
 VMEM_SPEC = pl.BlockSpec(memory_space=pltpu.VMEM)
 SMEM_SPEC = pl.BlockSpec(memory_space=pltpu.SMEM)
@@ -410,6 +412,7 @@
             pltpu.SemaphoreType.DMA((RING,)),
         ],
         compiler_params=pltpu.CompilerParams(vmem_limit_bytes=VMEM_LIMIT),
+        cost_estimate=WORK,
         name="attend",
     )(received, gains)
 
@@ -679,6 +682,7 @@
             pltpu.SemaphoreType.DMA((TILES,)),
         ],
         compiler_params=pltpu.CompilerParams(vmem_limit_bytes=VMEM_LIMIT),
+        cost_estimate=WORK,
         name="backward",
     )(pairs, total, received, q_turned, k_hat, grad_turned, *arrays)
 
@@ -714,6 +718,7 @@
     send, gain_part = run_backward(
         pairs, total, first, *hats, grad_turned, gains, moments, span_rows, norms, inner
     )
+    back, send = lax.optimization_barrier((back, send))
     last = exchange(send)
     attended, grad_value = unpack_rows(back, 2, "unpack_first")
     losses = jnp.sum(back[:, 2 * BLOCK : 2 * BLOCK + 3, :GROUPS].astype(F32), (0, 1))

time: 205 us -> 177 us (0.86)
  blocking collectives: 35.6 us -> 0 us
  starting transfers between devices: 51.6 us -> 40.6 us
  waiting for transfers between devices: 43.5 us -> 52.2 us
  Pallas kernels: 70.1 us -> 75.6 us
  local copies, waits for them, and re-layouts: 0.64 us -> 3.32 us
    all_to_all x1 -> x0, blocking collectives: 35.6 us -> none  [exchange(): return lax.all_to_all(slab, 'seq', split_axis=0, concat_axis=0, tiled=True)]
    ppermute x9, starting transfers between devices: 32.4 us -> 12.6 us  [over_packs(): moved.append(lax.ppermute(value, 'pack', pairs))]
    all_to_all x3 -> x4, starting transfers between devices: 19.2 us -> 27.9 us  [exchange(): return lax.all_to_all(slab, 'seq', split_axis=0, concat_axis=0, tiled=True)]
    all_to_all x3 -> x4, waiting for transfers between devices: 41.7 us -> 48.4 us  [exchange(): return lax.all_to_all(slab, 'seq', split_axis=0, concat_axis=0, tiled=True)]
    unnamed x14 -> x16, local copies, waits for them, and re-layouts: 0.03 us -> 2.71 us
    pallas_call x1, Pallas kernels: 22 us -> 24.7 us  [run_attend(): pl.pallas_call(attend_kernel, in_specs=[ANY_SPEC, VMEM_SPEC], out_specs=[...]
    pallas_call x1, Pallas kernels: 20.9 us -> 23.2 us  [run_backward(): pl.pallas_call(backward_kernel, in_specs=[SMEM_SPEC] * 2 + [ANY_SPEC] * 4...]
    ppermute x9, waiting for transfers between devices: 1.75 us -> 3.83 us  [over_packs(): moved.append(lax.ppermute(value, 'pack', pairs))]
  transfers between devices with their start and end apart: 12 -> 13, of which waited for: 5 -> 7; matrix products, arithmetic and copies ran while one was open for 1% -> 2% of each run, Pallas kernels for 16% -> 31%
where the time goes in v5:
time: 177 us; the launch traced here: 176 us
  Pallas kernels  75.6 us (43%)
  waiting for transfers between devices  52.2 us (29%)
  starting transfers between devices  40.6 us (23%)
  other arithmetic  3.74 us (2%)
  local copies, waits for them, and re-layouts  3.32 us (2%)
    all_to_all x4, waiting for transfers between devices, exchange(): return lax.all_to_all(slab, 'seq', split_axis=0, concat_axis=0, tiled=True)  48.4 us
    all_to_all x4, starting transfers between devices, exchange(): return lax.all_to_all(slab, 'seq', split_axis=0, concat_axis=0, tiled=True)  27.9 us
    pallas_call x1, Pallas kernels, run_attend(): pl.pallas_call(attend_kernel, in_specs=[ANY_SPEC, VMEM_SPEC], out_specs=[...  24.7 us
    pallas_call x1, Pallas kernels, run_backward(): pl.pallas_call(backward_kernel, in_specs=[SMEM_SPEC] * 2 + [ANY_SPEC] * 4...  23.2 us
    ppermute x9, starting transfers between devices, over_packs(): moved.append(lax.ppermute(value, 'pack', pairs))  12.6 us
    pallas_call x1, Pallas kernels, run_loss(): pl.pallas_call(loss_kernel, in_specs=[SMEM_SPEC] * 4 + [ANY_SPEC] * 3, ou...  12.5 us
    pallas_call x2, Pallas kernels, pack_rows(): pl.pallas_call(functools.partial(pack_kernel, len(rows)), in_specs=[ANY_S...  8.27 us
    pallas_call x2, Pallas kernels, unpack_rows(): pl.pallas_call(unpack_kernel, in_specs=[VMEM_SPEC], out_specs=[ANY_SPEC]...  6.92 us
  transfers between devices with their start and end apart: 13, of which 7 were waited for; matrix products, arithmetic and copies ran while one was open for 2% of the time, Pallas kernels for 31%

profile of v5, /device:TPU:1, one launch (start us, length us, event | category | flops | bytes accessed | tf_op | source)
XLA Modules:
  0.0 176.4 jit_solution(1739064002582823010)
XLA Ops:
  0.6 5.1 %pack_first.1 = bf16[32,400,128]{2,1,0:T(8,128)(2,1)} custom-call(bf16[1,128,4096]{2,1,0:T(8,128)(2,1)} %refs_0_.2, bf16[1,128,4096]{2,1,0:T(8,128)(2,1)} %refs_1_.1, bf16[1,128,4096]{2,1,0:T(8,128)(2,1)} %refs_2_.1, s32[1,128]{1,0:T(1,128)} %refs_3_.1), custom_call_target="tpu_custom_call" | custom-call | tf_op jit(solution)/shard_map/pack_first/pallas_call | solution.py:80
  5.7 9.4 %all-to-all-start = ((bf16[32,400,128]{2,1,0:T(8,128)(2,1)}), bf16[32,400,128]{2,1,0:T(8,128)(2,1)S(1)}, u32[]{:S(2)}, u32[]{:S(2)}) async-start(bf16[32,400,128]{2,1,0:T(8,128)(2,1)} %pack_first.1), calls=%async_computation | async-start | bytes 6553600 | tf_op jit(solution)/shard_map/all_to_all | solution.py:699
  15.3 1.4 collective-permute-start
  16.6 2.6 %collective-permute-start.1 = (f32[1,128]{1,0:T(1,128)S(1)}, f32[1,128]{1,0:T(1,128)S(1)}, u32[]{:S(2)}, u32[]{:S(2)}) collective-permute-start(f32[1,128]{1,0:T(1,128)S(1)} %convert_bitcast_fusion), channel_id=1, source_target_pairs={{0,64},{32,96},{64,0},{96,32},{1,65},{33,97},{65,1},{97,33},{2,66}... | collective-permute-start | bytes 1544 | tf_op jit(solution)/shard_map/ppermute | solution.py:694
  19.3 1.1 collective-permute-start.2
  20.3 0.2 collective-permute-done.1
  20.5 1.4 collective-permute-done.2
  22.0 0.6 concatenate.3.refs_1_
  22.6 3.2 %pack_second.1 = bf16[32,144,128]{2,1,0:T(8,128)(2,1)} custom-call(bf16[1,128,4096]{2,1,0:T(8,128)(2,1)} %refs_0_.3, f32[5,128]{1,0:T(8,128)} %concatenate.3.refs_1_), custom_call_target="tpu_custom_call" | custom-call | tf_op jit(solution)/shard_map/pack_second/pallas_call | solution.py:80
  25.8 30.5 %all-to-all-done.all_ref = bf16[32,400,128]{2,1,0:T(8,128)(2,1)S(1)} async-done(((bf16[32,400,128]{2,1,0:T(8,128)(2,1)}), bf16[32,400,128]{2,1,0:T(8,128)(2,1)S(1)}, u32[]{:S(2)}, u32[]{:S(2)}) %all-to-all-start) | async-done | bytes 3276832 | tf_op jit(solution)/shard_map/all_to_all | solution.py:699
  56.3 1.6 copy-done.2
  57.9 5.7 %all-to-all-start.1 = ((bf16[32,144,128]{2,1,0:T(8,128)(2,1)}), bf16[32,144,128]{2,1,0:T(8,128)(2,1)S(1)}, u32[]{:S(2)}, u32[]{:S(2)}) async-start(bf16[32,144,128]{2,1,0:T(8,128)(2,1)} %pack_second.1), calls=%async_computation.1 | async-start | bytes 2359296 | tf_op jit(solution)/shard_map/all_to_all | solution.py:699
  63.6 24.7 %attend.1 = (s32[3,108]{1,0:T(4,128)}, s32[1]{0:T(128)}, s32[16,2,256]{2,1,0:T(2,128)}, bf16[128,4096]{1,0:T(8,128)(2,1)}, bf16[4096,128]{1,0:T(8,128)(2,1)}, /*...) custom-call(bf16[32,400,128]{2,1,0:T(8,128)(2,1)} %copy-done.2, ...), custom_call_target="tpu_custom_call" | custom-call | flops 8589934592 | bytes 33554432 | tf_op jit(solution)/shard_map/attend/pallas_call | solution.py:385
  88.3 1.0 copy-done.1
  89.3 12.5 %loss_and_grad_value.1 = (bf16[32,272,128]{2,1,0:T(8,128)(2,1)}, bf16[128,4096]{1,0:T(8,128)(2,1)}, f32[16,1,256]{2,1,0:T(1,128)}, f32[1,128]{1,0:T(1,128)}) custom-call(s32[1,16]{1,0:T(1,128)} %labels_ref.1, f32[8]{0:T(128)} %mixture_ref.1, s32[3,108]{1,0:T(4,128)} %get-tuple-element.27.pair_ref, s32[1]{0:T(128)} %get-tuple-element.28.total_ref, ...), custom_call_target="tpu_custom_call" | custom-call | tf_op jit(solution)/shard_map/loss_and_grad_value/pallas_call | solution.py:536
  101.9 7.4 %all-to-all-start.2 = ((bf16[32,272,128]{2,1,0:T(8,128)(2,1)}), bf16[32,272,128]{2,1,0:T(8,128)(2,1)S(1)}, u32[]{:S(2)}, u32[]{:S(2)}) async-start(bf16[32,272,128]{2,1,0:T(8,128)(2,1)} %get-tuple-element.31), calls=%async_computation.2 | async-start | bytes 4456448 | tf_op jit(solution)/shard_map/all_to_all | solution.py:699
  109.3 23.2 %backward.1 = (bf16[32,256,128]{2,1,0:T(8,128)(2,1)}, f32[2,128]{1,0:T(2,128)}) custom-call(s32[3,108]{1,0:T(4,128)} %get-tuple-element.27.pair_ref, s32[1]{0:T(128)} %get-tuple-element.28.total_ref, bf16[32,400,128]{2,1,0:T(8,128)(2,1)} %copy-done.2, bf16[128,4096]{1,0:T(8,128)(2,1)} %get-tuple-element.32.q_turned_in, ...), custom_call_target="tpu_custom_call" | custom-call | flops 8589934592 | bytes 33554432 | tf_op jit(solution)/shard_map/backward/pallas_call | solution.py:665
  132.5 6.5 %all-to-all-done.2.in_ref = bf16[32,272,128]{2,1,0:T(8,128)(2,1)S(1)} async-done(((bf16[32,272,128]{2,1,0:T(8,128)(2,1)}), bf16[32,272,128]{2,1,0:T(8,128)(2,1)S(1)}, u32[]{:S(2)}, u32[]{:S(2)}) %all-to-all-start.2) | async-done | bytes 2228256 | tf_op jit(solution)/shard_map/all_to_all | solution.py:699
  139.0 5.4 %all-to-all-start.3 = ((bf16[32,256,128]{2,1,0:T(8,128)(2,1)}), bf16[32,256,128]{2,1,0:T(8,128)(2,1)}, u32[]{:S(2)}, u32[]{:S(2)}) async-start(bf16[32,256,128]{2,1,0:T(8,128)(2,1)} %get-tuple-element.42), calls=%async_computation.3 | async-start | bytes 4194304 | tf_op jit(solution)/shard_map/all_to_all | solution.py:699
  144.4 1.3 collective-permute-start.3
  145.8 2.6 %collective-permute-start.4 = (f32[2,128]{1,0:T(2,128)S(1)}, f32[2,128]{1,0:T(2,128)S(1)}, u32[]{:S(2)}, u32[]{:S(2)}) collective-permute-start(f32[2,128]{1,0:T(2,128)S(1)} %copy-done.4), channel_id=1, source_target_pairs={{0,64},{32,96},{64,0},{96,32},{1,65},{33,97},{65,1},{97,33},{2,66}... | collective-permute-start | bytes 3080 | tf_op jit(solution)/shard_map/ppermute | solution.py:694
  148.4 0.6 reduce_sum.37
  149.0 1.1 collective-permute-done.4
  150.1 1.1 collective-permute-done.5
  151.2 0.6 add_add_fusion
  151.9 2.4 %collective-permute-start.7 = (f32[8]{0:T(128)S(1)}, f32[8]{0:T(128)S(1)}, u32[]{:S(2)}, u32[]{:S(2)}) collective-permute-start(f32[8]{0:T(128)S(1)} %convert_reduce_fusion), channel_id=1, source_target_pairs={{0,64},{32,96},{64,0},{96,32},{1,65},{33,97},{65,1},{97,33},{2,66}... | collective-permute-start | bytes 104 | tf_op jit(solution)/shard_map/ppermute | solution.py:694
  154.3 1.2 collective-permute-start.8
  155.5 3.5 %unpack_first.1 = (bf16[1,128,4096]{2,1,0:T(8,128)(2,1)}, bf16[1,128,4096]{2,1,0:T(8,128)(2,1)}) custom-call(bf16[32,272,128]{2,1,0:T(8,128)(2,1)} %copy-done), custom_call_target="tpu_custom_call" | custom-call | tf_op jit(solution)/shard_map/unpack_first/pallas_call | solution.py:108
  159.0 1.3 fusion
  160.3 1.2 broadcast_divide_fusion
  161.4 11.4 %all-to-all-done.3.in_ref = bf16[32,256,128]{2,1,0:T(8,128)(2,1)} async-done(((bf16[32,256,128]{2,1,0:T(8,128)(2,1)}), bf16[32,256,128]{2,1,0:T(8,128)(2,1)}, u32[]{:S(2)}, u32[]{:S(2)}) %all-to-all-start.3) | async-done | bytes 2097184 | tf_op jit(solution)/shard_map/all_to_all | solution.py:699
  172.8 3.4 %unpack_last.1 = (bf16[1,128,4096]{2,1,0:T(8,128)(2,1)}, bf16[1,128,4096]{2,1,0:T(8,128)(2,1)}) custom-call(bf16[32,256,128]{2,1,0:T(8,128)(2,1)} %all-to-all-done.3.in_ref), custom_call_target="tpu_custom_call" | custom-call | tf_op jit(solution)/shard_map/unpack_last/pallas_call | solution.py:108
  (26 shorter events, 0.3 us)
Async XLA Ops:
  5.7 9.5 %copy-start.5 = (s32[1,128]{1,0:T(1,128)S(1)}, s32[1,128]{1,0:T(1,128)}, u32[]{:S(2)}) copy-start(s32[1,128]{1,0:T(1,128)} %refs_3_.1) | copy-start | bytes 1540
  5.7 9.5 %copy-start.6 = (s32[1,16]{1,0:T(1,128)S(1)}, s32[1,16]{1,0:T(1,128)}, u32[]{:S(2)}) copy-start(s32[1,16]{1,0:T(1,128)} %labels_ref.1) | copy-start | bytes 196
  5.7 50.5 %all-to-all-start = ((bf16[32,400,128]{2,1,0:T(8,128)(2,1)}), bf16[32,400,128]{2,1,0:T(8,128)(2,1)S(1)}, u32[]{:S(2)}, u32[]{:S(2)}) async-start(bf16[32,400,128]{2,1,0:T(8,128)(2,1)} %pack_first.1), calls=%async_computation | async-start | bytes 6553600 | tf_op jit(solution)/shard_map/all_to_all | solution.py:699
  15.3 5.1 %collective-permute-start = (f32[1,128]{1,0:T(1,128)S(1)}, f32[1,128]{1,0:T(1,128)S(1)}, u32[]{:S(2)}, u32[]{:S(2)}) collective-permute-start(f32[1,128]{1,0:T(1,128)S(1)} %convert_bitcast_fusion), channel_id=1, source_target_pairs={{0,32},{32,64},{64,96},{96,0},{1,33},{33,65},{65,97},{97,1},{2,34}... | collective-permute-start | bytes 1544 | tf_op jit(solution)/shard_map/ppermute | solution.py:694
  16.6 3.9 %collective-permute-start.1 = (f32[1,128]{1,0:T(1,128)S(1)}, f32[1,128]{1,0:T(1,128)S(1)}, u32[]{:S(2)}, u32[]{:S(2)}) collective-permute-start(f32[1,128]{1,0:T(1,128)S(1)} %convert_bitcast_fusion), channel_id=1, source_target_pairs={{0,64},{32,96},{64,0},{96,32},{1,65},{33,97},{65,1},{97,33},{2,66}... | collective-permute-start | bytes 1544 | tf_op jit(solution)/shard_map/ppermute | solution.py:694
  19.3 2.7 %collective-permute-start.2 = (f32[1,128]{1,0:T(1,128)S(1)}, f32[1,128]{1,0:T(1,128)S(1)}, u32[]{:S(2)}, u32[]{:S(2)}) collective-permute-start(f32[1,128]{1,0:T(1,128)S(1)} %convert_bitcast_fusion), channel_id=1, source_target_pairs={{0,96},{32,0},{64,32},{96,64},{1,97},{33,1},{65,33},{97,65},{2,98}... | collective-permute-start | bytes 1544 | tf_op jit(solution)/shard_map/ppermute | solution.py:694
  56.3 1.7 copy-start.2
  57.9 30.4 %all-to-all-start.1 = ((bf16[32,144,128]{2,1,0:T(8,128)(2,1)}), bf16[32,144,128]{2,1,0:T(8,128)(2,1)S(1)}, u32[]{:S(2)}, u32[]{:S(2)}) async-start(bf16[32,144,128]{2,1,0:T(8,128)(2,1)} %pack_second.1), calls=%async_computation.1 | async-start | bytes 2359296 | tf_op jit(solution)/shard_map/all_to_all | solution.py:699
  88.3 1.0 copy-start.1
  101.9 37.1 %all-to-all-start.2 = ((bf16[32,272,128]{2,1,0:T(8,128)(2,1)}), bf16[32,272,128]{2,1,0:T(8,128)(2,1)S(1)}, u32[]{:S(2)}, u32[]{:S(2)}) async-start(bf16[32,272,128]{2,1,0:T(8,128)(2,1)} %get-tuple-element.31), calls=%async_computation.2 | async-start | bytes 4456448 | tf_op jit(solution)/shard_map/all_to_all | solution.py:699
  132.5 11.9 %copy-start.4 = (f32[2,128]{1,0:T(2,128)S(1)}, f32[2,128]{1,0:T(2,128)}, u32[]{:S(2)}) copy-start(f32[2,128]{1,0:T(2,128)} %get-tuple-element.46) | copy-start | bytes 3076
  132.5 15.9 %copy-start.3 = (f32[8]{0:T(128)S(1)}, f32[8]{0:T(128)}, u32[]{:S(2)}) copy-start(f32[8]{0:T(128)} %mixture_ref.1) | copy-start | bytes 100
  139.0 16.4 %copy-start = (bf16[32,272,128]{2,1,0:T(8,128)(2,1)}, bf16[32,272,128]{2,1,0:T(8,128)(2,1)S(1)}, u32[]{:S(2)}) copy-start(bf16[32,272,128]{2,1,0:T(8,128)(2,1)S(1)} %all-to-all-done.2.in_ref) | copy-start | bytes 6684676
  139.0 20.0 %copy-start.7 = (f32[1,128]{1,0:T(1,128)S(1)}, f32[1,128]{1,0:T(1,128)}, u32[]{:S(2)}) copy-start(f32[1,128]{1,0:T(1,128)} %get-tuple-element.47) | copy-start | bytes 1540
  139.0 33.8 %all-to-all-start.3 = ((bf16[32,256,128]{2,1,0:T(8,128)(2,1)}), bf16[32,256,128]{2,1,0:T(8,128)(2,1)}, u32[]{:S(2)}, u32[]{:S(2)}) async-start(bf16[32,256,128]{2,1,0:T(8,128)(2,1)} %get-tuple-element.42), calls=%async_computation.3 | async-start | bytes 4194304 | tf_op jit(solution)/shard_map/all_to_all | solution.py:699
  144.4 4.6 %collective-permute-start.3 = (f32[2,128]{1,0:T(2,128)S(1)}, f32[2,128]{1,0:T(2,128)S(1)}, u32[]{:S(2)}, u32[]{:S(2)}) collective-permute-start(f32[2,128]{1,0:T(2,128)S(1)} %copy-done.4), channel_id=1, source_target_pairs={{0,32},{32,64},{64,96},{96,0},{1,33},{33,65},{65,97},{97,1},{2,34}... | collective-permute-start | bytes 3080 | tf_op jit(solution)/shard_map/ppermute | solution.py:694
  145.8 4.3 %collective-permute-start.4 = (f32[2,128]{1,0:T(2,128)S(1)}, f32[2,128]{1,0:T(2,128)S(1)}, u32[]{:S(2)}, u32[]{:S(2)}) collective-permute-start(f32[2,128]{1,0:T(2,128)S(1)} %copy-done.4), channel_id=1, source_target_pairs={{0,64},{32,96},{64,0},{96,32},{1,65},{33,97},{65,1},{97,33},{2,66}... | collective-permute-start | bytes 3080 | tf_op jit(solution)/shard_map/ppermute | solution.py:694
  148.4 2.8 %collective-permute-start.5 = (f32[2,128]{1,0:T(2,128)S(1)}, f32[2,128]{1,0:T(2,128)S(1)}, u32[]{:S(2)}, u32[]{:S(2)}) collective-permute-start(f32[2,128]{1,0:T(2,128)S(1)} %copy-done.4), channel_id=1, source_target_pairs={{0,96},{32,0},{64,32},{96,64},{1,97},{33,1},{65,33},{97,65},{2,98}... | collective-permute-start | bytes 3080 | tf_op jit(solution)/shard_map/ppermute | solution.py:694
  151.8 7.1 %collective-permute-start.6 = (f32[8]{0:T(128)S(1)}, f32[8]{0:T(128)S(1)}, u32[]{:S(2)}, u32[]{:S(2)}) collective-permute-start(f32[8]{0:T(128)S(1)} %convert_reduce_fusion), channel_id=1, source_target_pairs={{0,32},{32,64},{64,96},{96,0},{1,33},{33,65},{65,97},{97,1},{2,34}... | collective-permute-start | bytes 104 | tf_op jit(solution)/shard_map/ppermute | solution.py:694
  151.9 7.1 %collective-permute-start.7 = (f32[8]{0:T(128)S(1)}, f32[8]{0:T(128)S(1)}, u32[]{:S(2)}, u32[]{:S(2)}) collective-permute-start(f32[8]{0:T(128)S(1)} %convert_reduce_fusion), channel_id=1, source_target_pairs={{0,64},{32,96},{64,0},{96,32},{1,65},{33,97},{65,1},{97,33},{2,66}... | collective-permute-start | bytes 104 | tf_op jit(solution)/shard_map/ppermute | solution.py:694
  154.3 4.7 %collective-permute-start.8 = (f32[8]{0:T(128)S(1)}, f32[8]{0:T(128)S(1)}, u32[]{:S(2)}, u32[]{:S(2)}) collective-permute-start(f32[8]{0:T(128)S(1)} %convert_reduce_fusion), channel_id=1, source_target_pairs={{0,96},{32,0},{64,32},{96,64},{1,97},{33,1},{65,33},{97,65},{2,98}... | collective-permute-start | bytes 104 | tf_op jit(solution)/shard_map/ppermute | solution.py:694

commit v6 on v5

--- a/solution.py
+++ b/solution.py
@@ -33,7 +33,9 @@
 RING = 4
 SAFE_LOGIT = 70.0
 EXTRA = 16
-VMEM_LIMIT = 56 * 1024 * 1024
+CHUNK = 4
+CHUNKS = HEADS // CHUNK
+VMEM_LIMIT = 63 * 1024 * 1024
 
 BF16 = jnp.bfloat16
 F32 = jnp.float32
@@ -43,7 +45,7 @@
 
 VMEM_SPEC = pl.BlockSpec(memory_space=pltpu.VMEM)
 SMEM_SPEC = pl.BlockSpec(memory_space=pltpu.SMEM)
-ANY_SPEC = pl.BlockSpec(memory_space=pl.ANY)
+HBM_SPEC = pl.BlockSpec(memory_space=pltpu.HBM)
 
 
 def shape(dims, dtype):
@@ -55,62 +57,98 @@
 
 
 def pack_kernel(count, *refs):
-    row_refs, extra_refs, (out_ref, sems) = refs[:count], refs[count:-2], refs[-2:]
-    copies = []
-    for n, ref in enumerate(row_refs):
-        for h in range(HEADS):
-            copy = pltpu.make_async_copy(
-                ref.at[0, :, head_columns(h)],
-                out_ref.at[h, pl.ds(n * BLOCK, BLOCK), :],
-                sems.at[n, h],
-            )
-            copy.start()
-            copies.append(copy)
-    for extra_ref in extra_refs:
-        tile = extra_ref[...].astype(F32)
-        left = jnp.zeros((EXTRA - tile.shape[0], 128), F32)
-        tile = jnp.concatenate([tile, left], 0).astype(BF16)
-        out_ref[:, len(row_refs) * BLOCK :, :] = jnp.broadcast_to(tile[None], (HEADS, EXTRA, 128))
-    for copy in copies:
-        copy.wait()
+    row_refs, (extra_ref, out_ref, rows, slab, in_sems, out_sems) = refs[:count], refs[count:]
+
+    def arrival(c, n):
+        columns = pl.ds(c * CHUNK * HEAD_DIM, CHUNK * HEAD_DIM)
+        return pltpu.make_async_copy(
+            row_refs[n].at[0, :, columns], rows.at[n, :, columns], in_sems.at[n, c]
+        )
+
+    def leaving(c):
+        heads = pl.ds(c * CHUNK, CHUNK)
+        return pltpu.make_async_copy(slab.at[heads], out_ref.at[heads], out_sems.at[c])
+
+    for c in range(CHUNKS):
+        for n in range(count):
+            arrival(c, n).start()
+    extra = extra_ref[...].astype(F32)
+    extra = jnp.concatenate([extra, jnp.zeros((EXTRA - extra.shape[0], 128), F32)], 0)
+    slab[:, count * BLOCK :, :] = jnp.broadcast_to(extra.astype(BF16)[None], (HEADS, EXTRA, 128))
+    for c in range(CHUNKS):
+        for n in range(count):
+            arrival(c, n).wait()
+            for h in range(c * CHUNK, (c + 1) * CHUNK):
+                block = rows[n, :, h * HEAD_DIM : (h + 1) * HEAD_DIM]
+                slab[h, n * BLOCK : (n + 1) * BLOCK, :] = block.T
+        leaving(c).start()
+    for c in range(CHUNKS):
+        leaving(c).wait()
 
 
 def pack_rows(rows, extra, name):
-    extras = () if extra is None else (extra,)
+    count = len(rows)
+    slab = (HEADS, count * BLOCK + EXTRA, 128)
     return pl.pallas_call(
-        functools.partial(pack_kernel, len(rows)),
-        in_specs=[ANY_SPEC] * len(rows) + [VMEM_SPEC] * len(extras),
-        out_specs=VMEM_SPEC,
-        out_shape=shape((HEADS, len(rows) * BLOCK + EXTRA * len(extras), 128), BF16),
-        scratch_shapes=[pltpu.SemaphoreType.DMA((len(rows), HEADS))],
+        functools.partial(pack_kernel, count),
+        in_specs=[HBM_SPEC] * count + [VMEM_SPEC],
+        out_specs=HBM_SPEC,
+        out_shape=shape(slab, BF16),
+        scratch_shapes=[
+            pltpu.VMEM((count, BLOCK, HEADS * HEAD_DIM), BF16),
+            pltpu.VMEM(slab, BF16),
+            pltpu.SemaphoreType.DMA((count, CHUNKS)),
+            pltpu.SemaphoreType.DMA((CHUNKS,)),
+        ],
         compiler_params=pltpu.CompilerParams(vmem_limit_bytes=VMEM_LIMIT),
         name=name,
-    )(*rows, *extras)
-
-
-def unpack_kernel(in_ref, *refs):
-    *row_refs, sems = refs
-    copies = []
-    for n, ref in enumerate(row_refs):
-        for h in range(HEADS):
-            copy = pltpu.make_async_copy(
-                in_ref.at[h, pl.ds(n * BLOCK, BLOCK), :],
-                ref.at[0, :, head_columns(h)],
-                sems.at[n, h],
-            )
-            copy.start()
-            copies.append(copy)
-    for copy in copies:
-        copy.wait()
-
-
-def unpack_rows(slab, count, name):
+    )(*rows, extra)
+
+
+def unpack_kernel(turned, in_ref, *refs):
+    *row_refs, slab, rows, in_sems, out_sems = refs
+    lines = len(row_refs) * BLOCK
+
+    def arrival(c):
+        heads = pl.ds(c * CHUNK, CHUNK)
+        return pltpu.make_async_copy(
+            in_ref.at[heads, pl.ds(0, lines), :], slab.at[heads], in_sems.at[c]
+        )
+
+    def leaving(h, n):
+        columns = head_columns(h)
+        source = slab.at[h, pl.ds(n * BLOCK, BLOCK), :]
+        if n in turned:
+            source = rows.at[:, columns]
+        return pltpu.make_async_copy(source, row_refs[n].at[0, :, columns], out_sems.at[n, h])
+
+    for c in range(CHUNKS):
+        arrival(c).start()
+    for c in range(CHUNKS):
+        arrival(c).wait()
+        for h in range(c * CHUNK, (c + 1) * CHUNK):
+            for n in range(len(row_refs)):
+                if n in turned:
+                    block = slab[h, n * BLOCK : (n + 1) * BLOCK, :]
+                    rows[:, h * HEAD_DIM : (h + 1) * HEAD_DIM] = block.T
+                leaving(h, n).start()
+    for h in range(HEADS):
+        for n in range(len(row_refs)):
+            leaving(h, n).wait()
+
+
+def unpack_rows(slab, count, turned, name):
     return pl.pallas_call(
-        unpack_kernel,
-        in_specs=[VMEM_SPEC],
-        out_specs=[ANY_SPEC] * count,
+        functools.partial(unpack_kernel, turned),
+        in_specs=[HBM_SPEC],
+        out_specs=[HBM_SPEC] * count,
         out_shape=[shape((1, BLOCK, HEADS * HEAD_DIM), BF16)] * count,
-        scratch_shapes=[pltpu.SemaphoreType.DMA((count, HEADS))],
+        scratch_shapes=[
+            pltpu.VMEM((HEADS, count * BLOCK, 128), BF16),
+            pltpu.VMEM((BLOCK, HEADS * HEAD_DIM), BF16),
+            pltpu.SemaphoreType.DMA((CHUNKS,)),
+            pltpu.SemaphoreType.DMA((count, HEADS)),
+        ],
         compiler_params=pltpu.CompilerParams(vmem_limit_bytes=VMEM_LIMIT),
         name=name,
     )(slab)
@@ -120,9 +158,9 @@
     return lax.dot_general(a, b, (contract, ((), ())), preferred_element_type=F32)
 
 
-def tile_rows(ref, i, part, size=TILE):
-    blocks = size // BLOCK
-    return ref[pl.ds(i, blocks), part * BLOCK : (part + 1) * BLOCK, :].reshape(size, HEAD_DIM)
+def tile_turned(ref, block, part):
+    lines = slice(part * BLOCK, (part + 1) * BLOCK)
+    return jnp.concatenate([ref[block + b, lines, :] for b in range(PAIR)], 1)
 
 
 def tile_at(i, size=TILE):
@@ -240,8 +278,8 @@
     (moments_ref, norm_ref, out_ref), refs = refs[:3], refs[3:]
     hats, refs = refs[:2], refs[2:]
     q_turned_ref, k_hat_ref = hats
-    recv_ref, extra_ref, starts, v_turned, terms, fold, probs, sums = refs[:8]
-    in_sems, extra_sem, out_sems, prob_sems = refs[8:]
+    recv_ref, extra_ref, starts, terms, fold, probs, sums = refs[:7]
+    in_sems, extra_sem, out_sems, prob_sems = refs[7:]
 
     def arrival(i):
         return pltpu.make_async_copy(
@@ -272,10 +310,9 @@
     def prepare(i, most):
         arrival(i).wait()
         rows = tile_at(i)
-        v_turned[:, rows] = tile_rows(recv_ref, i * PAIR, 2).T
         sizes = []
         for n in range(2):
-            values = tile_rows(recv_ref, i * PAIR, n).T.astype(F32)
+            values = tile_turned(recv_ref, i * PAIR, n).astype(F32)
             mean = mean_down(values)
             centre = values - mean
             inverse = lax.rsqrt(mean_down(centre * centre) + EPS)
@@ -362,7 +399,8 @@
             probs[slot, u] = tile
         give_probs(n).start()
         tiles = [
-            dot(v_turned[:, pl.ds(at, KEYS)], tile) for tile, (_, _, at, _) in zip(tiles, pairs)
+            dot(tile_turned(recv_ref, at // BLOCK, 2), tile)
+            for tile, (_, _, at, _) in zip(tiles, pairs)
         ]
         for tile, (_, i, _, _) in zip(tiles, pairs):
             sums[i] += tile
@@ -384,8 +422,8 @@
     hats = [((HEAD_DIM, LENGTH), BF16), ((LENGTH, HEAD_DIM), BF16)]
     return pl.pallas_call(
         attend_kernel,
-        in_specs=[ANY_SPEC, VMEM_SPEC],
-        out_specs=[SMEM_SPEC] * 2 + [VMEM_SPEC] + [ANY_SPEC] * 3 + [VMEM_SPEC] * 2 + [ANY_SPEC],
+        in_specs=[HBM_SPEC, VMEM_SPEC],
+        out_specs=[SMEM_SPEC] * 2 + [VMEM_SPEC] + [HBM_SPEC] * 3 + [VMEM_SPEC] * 2 + [HBM_SPEC],
         out_shape=[
             shape((3, MOST_PAIRS), I32),
             shape((1,), I32),
@@ -401,7 +439,6 @@
             pltpu.VMEM((BLOCKS, 3 * BLOCK, 128), BF16),
             pltpu.VMEM((BLOCKS, EXTRA, 128), BF16),
             pltpu.SMEM((IMAGES + 1,), I32),
-            pltpu.VMEM((HEAD_DIM, LENGTH), BF16),
             pltpu.VMEM((MOST_PAIRS, KEYS, TILE), F32),
             pltpu.VMEM((TILES, 8, TILE), F32),
             pltpu.VMEM((RING, UNROLL, KEYS, TILE), BF16),
@@ -484,7 +521,7 @@
             arrival(i, n).wait()
         rows = tile_at(i)
         head_out = out_ref[i]
-        misfit = head_out - tile_rows(recv_ref, i * PAIR, 0).T.astype(F32)
+        misfit = head_out - tile_turned(recv_ref, i * PAIR, 0).astype(F32)
         loss_rows[i, 0:1, :] = 0.5 * jnp.sum(misfit * misfit, 0, keepdims=True)
         grad_out = coef_rows[i, 0:1, :] * misfit
         inner_ref[i, 0:1, :] = jnp.sum(grad_out * head_out, 0, keepdims=True)
@@ -492,7 +529,9 @@
         grad_turned_ref[:, rows] = grad_turned
         grad_low[rows, :] = grad_turned.T
         grad_v[rows, :] = jnp.zeros((TILE, HEAD_DIM), F32)
-        first_ref[tile_blocks(i)] = head_out.astype(BF16).T.reshape(PAIR, BLOCK, HEAD_DIM)
+        low = head_out.astype(BF16)
+        for b in range(PAIR):
+            first_ref[i * PAIR + b] = low[:, b * BLOCK : (b + 1) * BLOCK]
         for n in range(2):
             leaving(i, n).start()
         return carry
@@ -535,8 +574,8 @@
 def run_loss(labels, mixture, pairs, total, second, head_out, probs):
     return pl.pallas_call(
         loss_kernel,
-        in_specs=[SMEM_SPEC] * 4 + [ANY_SPEC] * 3,
-        out_specs=[ANY_SPEC] * 2 + [VMEM_SPEC] * 2,
+        in_specs=[SMEM_SPEC] * 4 + [HBM_SPEC] * 3,
+        out_specs=[HBM_SPEC] * 2 + [VMEM_SPEC] * 2,
         out_shape=[
             shape((BLOCKS, 2 * BLOCK + EXTRA, 128), BF16),
             shape((HEAD_DIM, LENGTH), BF16),
@@ -579,9 +618,8 @@
         source, target = (
             (q_turned_in.at[:, rows], q_turned_ref.at[:, rows]),
             (k_hat_in.at[rows, :], k_hat_ref.at[rows, :]),
-            (all_ref.at[blocks, pl.ds(2 * BLOCK, BLOCK), :], value_ref.at[blocks]),
+            (all_ref.at[blocks, pl.ds(0, 3 * BLOCK), :], raw_ref.at[blocks]),
             (grad_turned_in.at[:, rows], grad_turned_ref.at[:, rows]),
-            (all_ref.at[blocks, pl.ds(0, 2 * BLOCK), :], raw_ref.at[blocks]),
         )[n]
         return pltpu.make_async_copy(source, target, in_sems.at[n, i])
 
@@ -589,7 +627,7 @@
         blocks = tile_blocks(i)
         return pltpu.make_async_copy(send_ref.at[blocks], send_out.at[blocks], out_sems.at[i])
 
-    for n in range(5):
+    for n in range(4):
         each_tile(lambda i, n=n: arrival(i, n).start())
 
     def clear(i, carry):
@@ -597,20 +635,21 @@
             arrival(i, n).wait()
         q_hat_ref[tile_at(i), :] = q_turned_ref[:, tile_at(i)].T
         k_turned_ref[:, tile_at(i)] = k_hat_ref[tile_at(i), :].T
+        arrival(i, 2).wait()
+        value_ref[tile_at(i), :] = tile_turned(raw_ref, i * PAIR, 2).T
         grad_q[i] = jnp.zeros((HEAD_DIM, TILE), F32)
         grad_k[tile_at(i), :] = jnp.zeros((TILE, HEAD_DIM), F32)
         return carry
 
     lax.fori_loop(0, TILES, clear, 0, unroll=TILES)
-    for n in (2, 3):
-        each_tile(lambda i, n=n: arrival(i, n).wait())
+    each_tile(lambda i: arrival(i, 3).wait())
 
     def add_pairs(n, pairs):
         tiles = [
             dot(k_hat_ref[pl.ds(at, KEYS), :], q_turned_ref[:, tile_at(i)]) for _, i, at, _ in pairs
         ]
         prob_grads = [
-            dot(tile_rows(value_ref, at // BLOCK, 0, KEYS), grad_turned_ref[:, tile_at(i)])
+            dot(value_ref[pl.ds(at, KEYS), :], grad_turned_ref[:, tile_at(i)])
             for _, i, at, _ in pairs
         ]
         tiles = [
@@ -636,7 +675,7 @@
     def norm_backward(i, n, grad_hat):
         mean = moments_ref[i, 2 * n : 2 * n + 1, :]
         inverse = moments_ref[i, 2 * n + 1 : 2 * n + 2, :]
-        normed = (tile_rows(raw_ref, i * PAIR, n).T.astype(F32) - mean) * inverse
+        normed = (tile_turned(raw_ref, i * PAIR, n).astype(F32) - mean) * inverse
         grad_normed = grad_hat * gains[:, n : n + 1]
         inner = mean_down(grad_normed * normed)
         grad_in = inverse * (grad_normed - mean_down(grad_normed) - normed * inner)
@@ -647,7 +686,6 @@
         return sum(grad_gain[:, c : c + 128] for c in range(0, TILE, 128))
 
     def finish(i, gain_sums):
-        arrival(i, 4).wait()
         gain_q, gain_k = gain_sums
         gain_q = gain_q + norm_backward(i, 0, grad_q[i])
         gain_k = gain_k + norm_backward(i, 1, grad_k[tile_at(i), :].T)
@@ -664,21 +702,21 @@
 def run_backward(pairs, total, received, q_turned, k_hat, grad_turned, *arrays):
     return pl.pallas_call(
         backward_kernel,
-        in_specs=[SMEM_SPEC] * 2 + [ANY_SPEC] * 4 + [VMEM_SPEC] * len(arrays),
-        out_specs=[ANY_SPEC, VMEM_SPEC],
+        in_specs=[SMEM_SPEC] * 2 + [HBM_SPEC] * 4 + [VMEM_SPEC] * len(arrays),
+        out_specs=[HBM_SPEC, VMEM_SPEC],
         out_shape=[shape((BLOCKS, 2 * BLOCK, 128), BF16), shape((2, HEAD_DIM), F32)],
         scratch_shapes=[
             pltpu.VMEM((TILES, HEAD_DIM, TILE), F32),
             pltpu.VMEM((LENGTH, HEAD_DIM), F32),
             pltpu.VMEM((LENGTH, HEAD_DIM), BF16),
             pltpu.VMEM((HEAD_DIM, LENGTH), BF16),
-            pltpu.VMEM((BLOCKS, BLOCK, 128), BF16),
-            pltpu.VMEM((BLOCKS, 2 * BLOCK, 128), BF16),
+            pltpu.VMEM((LENGTH, HEAD_DIM), BF16),
+            pltpu.VMEM((BLOCKS, 3 * BLOCK, 128), BF16),
             pltpu.VMEM((HEAD_DIM, LENGTH), BF16),
             pltpu.VMEM((LENGTH, HEAD_DIM), BF16),
             pltpu.VMEM((HEAD_DIM, LENGTH), BF16),
             pltpu.VMEM((BLOCKS, 2 * BLOCK, 128), BF16),
-            pltpu.SemaphoreType.DMA((5, TILES)),
+            pltpu.SemaphoreType.DMA((4, TILES)),
             pltpu.SemaphoreType.DMA((TILES,)),
         ],
         compiler_params=pltpu.CompilerParams(vmem_limit_bytes=VMEM_LIMIT),
@@ -720,7 +758,7 @@
     )
     back, send = lax.optimization_barrier((back, send))
     last = exchange(send)
-    attended, grad_value = unpack_rows(back, 2, "unpack_first")
+    attended, grad_value = unpack_rows(back, 2, (0,), "unpack_first")
     losses = jnp.sum(back[:, 2 * BLOCK : 2 * BLOCK + 3, :GROUPS].astype(F32), (0, 1))
     group_total = sum(over_packs(losses))
     group_loss = group_total / (counts[0, :GROUPS] * (HEADS * HEAD_DIM))
@@ -728,7 +766,7 @@
     raised = shares * jnp.exp(ETA * group_loss)
     new_mixture = raised / jnp.sum(raised)
     grad_gains = sum(over_packs(gain_part)).reshape(2, 1, HEAD_DIM)
-    grad_query, grad_key = unpack_rows(last, 2, "unpack_last")
+    grad_query, grad_key = unpack_rows(last, 2, (), "unpack_last")
     return (attended, grad_query, grad_key, grad_value, grad_gains, new_mixture)
 
 

time: 177 us -> 172 us (0.972)
  Pallas kernels: 75.6 us -> 71.9 us
  local copies, waits for them, and re-layouts: 3.32 us -> 0.64 us
  waiting for transfers between devices: 52.2 us -> 50 us
  starting transfers between devices: 40.6 us -> 42.6 us
    pallas_call x7, Pallas kernels: 75.6 us -> 71.9 us  [the longest x1 23.3 us: run_backward(): pl.pallas_call(backward_kernel, in_specs=[SMEM_SPEC] * 2 + [HBM_SPEC] * 4...]
    unnamed x16 -> x10, local copies, waits for them, and re-layouts: 2.71 us -> 0.03 us
    ppermute x9, starting transfers between devices: 12.6 us -> 14.5 us  [over_packs(): moved.append(lax.ppermute(value, 'pack', pairs))]
    ppermute x9, waiting for transfers between devices: 3.83 us -> 1.96 us  [over_packs(): moved.append(lax.ppermute(value, 'pack', pairs))]
  transfers between devices with their start and end apart: 13 -> 13, of which waited for: 7 -> 6; matrix products, arithmetic and copies ran while one was open for 2% -> 3% of each run, Pallas kernels for 31% -> 31%
where the time goes in v6:
time: 172 us; the launch traced here: 171 us
  Pallas kernels  71.9 us (42%)
  waiting for transfers between devices  50 us (29%)
  starting transfers between devices  42.6 us (25%)
  other arithmetic  4.58 us (3%)
    all_to_all x4, waiting for transfers between devices, exchange(): return lax.all_to_all(slab, 'seq', split_axis=0, concat_axis=0, tiled=True)  48.1 us
    all_to_all x4, starting transfers between devices, exchange(): return lax.all_to_all(slab, 'seq', split_axis=0, concat_axis=0, tiled=True)  28 us
    pallas_call x1, Pallas kernels, run_backward(): pl.pallas_call(backward_kernel, in_specs=[SMEM_SPEC] * 2 + [HBM_SPEC] * 4...  23.3 us
    pallas_call x1, Pallas kernels, run_attend(): pl.pallas_call(attend_kernel, in_specs=[HBM_SPEC, VMEM_SPEC], out_specs=[...  23.3 us
    ppermute x9, starting transfers between devices, over_packs(): moved.append(lax.ppermute(value, 'pack', pairs))  14.5 us
    pallas_call x1, Pallas kernels, run_loss(): pl.pallas_call(loss_kernel, in_specs=[SMEM_SPEC] * 4 + [HBM_SPEC] * 3, ou...  11.5 us
    pallas_call x2, Pallas kernels, pack_rows(): pl.pallas_call(functools.partial(pack_kernel, count), in_specs=[HBM_SPEC]...  7.89 us
    pallas_call x2, Pallas kernels, unpack_rows(): pl.pallas_call(functools.partial(unpack_kernel, turned), in_specs=[HBM_SP...  5.91 us
  transfers between devices with their start and end apart: 13, of which 6 were waited for; matrix products, arithmetic and copies ran while one was open for 3% of the time, Pallas kernels for 31%

profile of v6, /device:TPU:1, one launch (start us, length us, event | category | flops | bytes accessed | tf_op | source)
XLA Modules:
  0.0 170.7 jit_solution(6773379942305394678)
XLA Ops:
  0.6 4.8 %pack_first.1 = bf16[32,400,128]{2,1,0:T(8,128)(2,1)} custom-call(bf16[1,128,4096]{2,1,0:T(8,128)(2,1)} %refs_0_.2, bf16[1,128,4096]{2,1,0:T(8,128)(2,1)} %refs_1_.1, bf16[1,128,4096]{2,1,0:T(8,128)(2,1)} %refs_2_.1, s32[1,128]{1,0:T(1,128)} %refs_3_.1), custom_call_target="tpu_custom_call" | custom-call | tf_op jit(solution)/shard_map/pack_first/pallas_call | solution.py:92
  5.4 9.5 %all-to-all-start = ((bf16[32,400,128]{2,1,0:T(8,128)(2,1)}), bf16[32,400,128]{2,1,0:T(8,128)(2,1)}, u32[]{:S(2)}, u32[]{:S(2)}) async-start(bf16[32,400,128]{2,1,0:T(8,128)(2,1)} %pack_first.1), calls=%async_computation | async-start | bytes 6553600 | tf_op jit(solution)/shard_map/all_to_all | solution.py:737
  15.0 0.1 select_reduce_fusion
  15.1 1.4 collective-permute-start
  16.4 2.6 %collective-permute-start.1 = (f32[1,128]{1,0:T(1,128)S(1)}, f32[1,128]{1,0:T(1,128)S(1)}, u32[]{:S(2)}, u32[]{:S(2)}) collective-permute-start(f32[1,128]{1,0:T(1,128)S(1)} %convert_bitcast_fusion), channel_id=1, source_target_pairs={{0,64},{32,96},{64,0},{96,32},{1,65},{33,97},{65,1},{97,33},{2,66}... | collective-permute-start | bytes 1544 | tf_op jit(solution)/shard_map/ppermute | solution.py:732
  19.0 1.1 collective-permute-start.2
  20.1 0.2 collective-permute-done.1
  20.3 1.5 collective-permute-done.2
  21.8 0.6 concatenate.3.refs_1_
  22.4 3.1 %pack_second.1 = bf16[32,144,128]{2,1,0:T(8,128)(2,1)} custom-call(bf16[1,128,4096]{2,1,0:T(8,128)(2,1)} %refs_0_.3, f32[5,128]{1,0:T(8,128)} %concatenate.3.refs_1_), custom_call_target="tpu_custom_call" | custom-call | tf_op jit(solution)/shard_map/pack_second/pallas_call | solution.py:92
  25.6 30.5 %all-to-all-done.all_ref = bf16[32,400,128]{2,1,0:T(8,128)(2,1)} async-done(((bf16[32,400,128]{2,1,0:T(8,128)(2,1)}), bf16[32,400,128]{2,1,0:T(8,128)(2,1)}, u32[]{:S(2)}, u32[]{:S(2)}) %all-to-all-start) | async-done | bytes 3276832 | tf_op jit(solution)/shard_map/all_to_all | solution.py:737
  56.1 5.7 %all-to-all-start.1 = ((bf16[32,144,128]{2,1,0:T(8,128)(2,1)}), bf16[32,144,128]{2,1,0:T(8,128)(2,1)}, u32[]{:S(2)}, u32[]{:S(2)}) async-start(bf16[32,144,128]{2,1,0:T(8,128)(2,1)} %pack_second.1), calls=%async_computation.1 | async-start | bytes 2359296 | tf_op jit(solution)/shard_map/all_to_all | solution.py:737
  61.8 23.3 %attend.1 = (s32[3,108]{1,0:T(4,128)}, s32[1]{0:T(128)}, s32[16,2,256]{2,1,0:T(2,128)}, bf16[128,4096]{1,0:T(8,128)(2,1)}, bf16[4096,128]{1,0:T(8,128)(2,1)}, /*...) custom-call(bf16[32,400,128]{2,1,0:T(8,128)(2,1)} %all-to-all-done.all, ...), custom_call_target="tpu_custom_call" | custom-call | flops 8589934592 | bytes 33554432 | tf_op jit(solution)/shard_map/attend/pallas_call | solution.py:423
  85.1 11.5 %loss_and_grad_value.1 = (bf16[32,272,128]{2,1,0:T(8,128)(2,1)}, bf16[128,4096]{1,0:T(8,128)(2,1)}, f32[16,1,256]{2,1,0:T(1,128)}, f32[1,128]{1,0:T(1,128)}) custom-call(s32[1,16]{1,0:T(1,128)} %labels_ref.1, f32[8]{0:T(128)} %mixture_ref.1, s32[3,108]{1,0:T(4,128)} %get-tuple-element.27.pair_ref, s32[1]{0:T(128)} %get-tuple-element.28.total_ref, ...), custom_call_target="tpu_custom_call" | custom-call | tf_op jit(solution)/shard_map/loss_and_grad_value/pallas_call | solution.py:575
  96.6 7.5 %all-to-all-start.2 = ((bf16[32,272,128]{2,1,0:T(8,128)(2,1)}), bf16[32,272,128]{2,1,0:T(8,128)(2,1)}, u32[]{:S(2)}, u32[]{:S(2)}) async-start(bf16[32,272,128]{2,1,0:T(8,128)(2,1)} %get-tuple-element.31), calls=%async_computation.2 | async-start | bytes 4456448 | tf_op jit(solution)/shard_map/all_to_all | solution.py:737
  104.1 23.3 %backward.1 = (bf16[32,256,128]{2,1,0:T(8,128)(2,1)}, f32[2,128]{1,0:T(2,128)}) custom-call(s32[3,108]{1,0:T(4,128)} %get-tuple-element.27.pair_ref, s32[1]{0:T(128)} %get-tuple-element.28.total_ref, bf16[32,400,128]{2,1,0:T(8,128)(2,1)} %all-to-all-done.all_ref, bf16[128,4096]{1,0:T(8,128)(2,1)} %get-tuple-element.32.q_turned_in, ...), custom_call_target="tpu_custom_call" | custom-call | flops 8589934592 | bytes 33554432 | tf_op jit(solution)/shard_map/backward/pallas_call | solution.py:703
  127.4 6.4 %all-to-all-done.2.in_ref = bf16[32,272,128]{2,1,0:T(8,128)(2,1)} async-done(((bf16[32,272,128]{2,1,0:T(8,128)(2,1)}), bf16[32,272,128]{2,1,0:T(8,128)(2,1)}, u32[]{:S(2)}, u32[]{:S(2)}) %all-to-all-start.2) | async-done | bytes 2228256 | tf_op jit(solution)/shard_map/all_to_all | solution.py:737
  133.8 5.4 %all-to-all-start.3 = ((bf16[32,256,128]{2,1,0:T(8,128)(2,1)}), bf16[32,256,128]{2,1,0:T(8,128)(2,1)}, u32[]{:S(2)}, u32[]{:S(2)}) async-start(bf16[32,256,128]{2,1,0:T(8,128)(2,1)} %get-tuple-element.42), calls=%async_computation.3 | async-start | bytes 4194304 | tf_op jit(solution)/shard_map/all_to_all | solution.py:737
  139.2 1.4 collective-permute-start.3
  140.6 1.7 %collective-permute-start.4 = (f32[2,128]{1,0:T(2,128)S(1)}, f32[2,128]{1,0:T(2,128)S(1)}, u32[]{:S(2)}, u32[]{:S(2)}) collective-permute-start(f32[2,128]{1,0:T(2,128)S(1)} %copy-done.1), channel_id=1, source_target_pairs={{0,64},{32,96},{64,0},{96,32},{1,65},{33,97},{65,1},{97,33},{2,66}... | collective-permute-start | bytes 3080 | tf_op jit(solution)/shard_map/ppermute | solution.py:732
  142.3 2.0 %collective-permute-start.5 = (f32[2,128]{1,0:T(2,128)S(1)}, f32[2,128]{1,0:T(2,128)S(1)}, u32[]{:S(2)}, u32[]{:S(2)}) collective-permute-start(f32[2,128]{1,0:T(2,128)S(1)} %copy-done.1), channel_id=1, source_target_pairs={{0,96},{32,0},{64,32},{96,64},{1,97},{33,1},{65,33},{97,65},{2,98}... | collective-permute-start | bytes 3080 | tf_op jit(solution)/shard_map/ppermute | solution.py:732
  144.3 0.6 reduce_sum.37
  145.0 0.2 collective-permute-done.5
  145.2 0.6 add_add_fusion
  145.7 0.9 convert_reduce_fusion
  146.6 1.2 collective-permute-start.6
  147.8 3.3 %collective-permute-start.7 = (f32[8]{0:T(128)S(1)}, f32[8]{0:T(128)S(1)}, u32[]{:S(2)}, u32[]{:S(2)}) collective-permute-start(f32[8]{0:T(128)S(1)} %convert_reduce_fusion), channel_id=1, source_target_pairs={{0,64},{32,96},{64,0},{96,32},{1,65},{33,97},{65,1},{97,33},{2,66}... | collective-permute-start | bytes 104 | tf_op jit(solution)/shard_map/ppermute | solution.py:732
  151.1 3.0 %unpack_first.1 = (bf16[1,128,4096]{2,1,0:T(8,128)(2,1)}, bf16[1,128,4096]{2,1,0:T(8,128)(2,1)}) custom-call(bf16[32,272,128]{2,1,0:T(8,128)(2,1)} %all-to-all-done.2.in_ref), custom_call_target="tpu_custom_call" | custom-call | tf_op jit(solution)/shard_map/unpack_first/pallas_call | solution.py:141
  154.1 1.3 fusion
  155.4 1.2 broadcast_divide_fusion
  156.6 11.1 %all-to-all-done.3.in_ref = bf16[32,256,128]{2,1,0:T(8,128)(2,1)} async-done(((bf16[32,256,128]{2,1,0:T(8,128)(2,1)}), bf16[32,256,128]{2,1,0:T(8,128)(2,1)}, u32[]{:S(2)}, u32[]{:S(2)}) %all-to-all-start.3) | async-done | bytes 2097184 | tf_op jit(solution)/shard_map/all_to_all | solution.py:737
  167.7 2.9 %unpack_last.1 = (bf16[1,128,4096]{2,1,0:T(8,128)(2,1)}, bf16[1,128,4096]{2,1,0:T(8,128)(2,1)}) custom-call(bf16[32,256,128]{2,1,0:T(8,128)(2,1)} %all-to-all-done.3.in_ref), custom_call_target="tpu_custom_call" | custom-call | tf_op jit(solution)/shard_map/unpack_last/pallas_call | solution.py:141
  (20 shorter events, 0.1 us)
Async XLA Ops:
  5.4 9.5 %copy-start.2 = (s32[1,128]{1,0:T(1,128)S(1)}, s32[1,128]{1,0:T(1,128)}, u32[]{:S(2)}) copy-start(s32[1,128]{1,0:T(1,128)} %refs_3_.1) | copy-start | bytes 1540
  5.4 9.5 %copy-start.3 = (s32[1,16]{1,0:T(1,128)S(1)}, s32[1,16]{1,0:T(1,128)}, u32[]{:S(2)}) copy-start(s32[1,16]{1,0:T(1,128)} %labels_ref.1) | copy-start | bytes 196
  5.4 50.6 %all-to-all-start = ((bf16[32,400,128]{2,1,0:T(8,128)(2,1)}), bf16[32,400,128]{2,1,0:T(8,128)(2,1)}, u32[]{:S(2)}, u32[]{:S(2)}) async-start(bf16[32,400,128]{2,1,0:T(8,128)(2,1)} %pack_first.1), calls=%async_computation | async-start | bytes 6553600 | tf_op jit(solution)/shard_map/all_to_all | solution.py:737
  15.1 5.1 %collective-permute-start = (f32[1,128]{1,0:T(1,128)S(1)}, f32[1,128]{1,0:T(1,128)S(1)}, u32[]{:S(2)}, u32[]{:S(2)}) collective-permute-start(f32[1,128]{1,0:T(1,128)S(1)} %convert_bitcast_fusion), channel_id=1, source_target_pairs={{0,32},{32,64},{64,96},{96,0},{1,33},{33,65},{65,97},{97,1},{2,34}... | collective-permute-start | bytes 1544 | tf_op jit(solution)/shard_map/ppermute | solution.py:732
  16.4 3.9 %collective-permute-start.1 = (f32[1,128]{1,0:T(1,128)S(1)}, f32[1,128]{1,0:T(1,128)S(1)}, u32[]{:S(2)}, u32[]{:S(2)}) collective-permute-start(f32[1,128]{1,0:T(1,128)S(1)} %convert_bitcast_fusion), channel_id=1, source_target_pairs={{0,64},{32,96},{64,0},{96,32},{1,65},{33,97},{65,1},{97,33},{2,66}... | collective-permute-start | bytes 1544 | tf_op jit(solution)/shard_map/ppermute | solution.py:732
  19.0 2.8 %collective-permute-start.2 = (f32[1,128]{1,0:T(1,128)S(1)}, f32[1,128]{1,0:T(1,128)S(1)}, u32[]{:S(2)}, u32[]{:S(2)}) collective-permute-start(f32[1,128]{1,0:T(1,128)S(1)} %convert_bitcast_fusion), channel_id=1, source_target_pairs={{0,96},{32,0},{64,32},{96,64},{1,97},{33,1},{65,33},{97,65},{2,98}... | collective-permute-start | bytes 1544 | tf_op jit(solution)/shard_map/ppermute | solution.py:732
  56.1 29.0 %all-to-all-start.1 = ((bf16[32,144,128]{2,1,0:T(8,128)(2,1)}), bf16[32,144,128]{2,1,0:T(8,128)(2,1)}, u32[]{:S(2)}, u32[]{:S(2)}) async-start(bf16[32,144,128]{2,1,0:T(8,128)(2,1)} %pack_second.1), calls=%async_computation.1 | async-start | bytes 2359296 | tf_op jit(solution)/shard_map/all_to_all | solution.py:737
  96.6 37.2 %all-to-all-start.2 = ((bf16[32,272,128]{2,1,0:T(8,128)(2,1)}), bf16[32,272,128]{2,1,0:T(8,128)(2,1)}, u32[]{:S(2)}, u32[]{:S(2)}) async-start(bf16[32,272,128]{2,1,0:T(8,128)(2,1)} %get-tuple-element.31), calls=%async_computation.2 | async-start | bytes 4456448 | tf_op jit(solution)/shard_map/all_to_all | solution.py:737
  127.4 11.9 %copy-start.1 = (f32[2,128]{1,0:T(2,128)S(1)}, f32[2,128]{1,0:T(2,128)}, u32[]{:S(2)}) copy-start(f32[2,128]{1,0:T(2,128)} %get-tuple-element.46) | copy-start | bytes 3076
  127.4 16.9 %copy-start = (f32[8]{0:T(128)S(1)}, f32[8]{0:T(128)}, u32[]{:S(2)}) copy-start(f32[8]{0:T(128)} %mixture_ref.1) | copy-start | bytes 100
  133.8 20.3 %copy-start.4 = (f32[1,128]{1,0:T(1,128)S(1)}, f32[1,128]{1,0:T(1,128)}, u32[]{:S(2)}) copy-start(f32[1,128]{1,0:T(1,128)} %get-tuple-element.47) | copy-start | bytes 1540
  133.8 33.8 %all-to-all-start.3 = ((bf16[32,256,128]{2,1,0:T(8,128)(2,1)}), bf16[32,256,128]{2,1,0:T(8,128)(2,1)}, u32[]{:S(2)}, u32[]{:S(2)}) async-start(bf16[32,256,128]{2,1,0:T(8,128)(2,1)} %get-tuple-element.42), calls=%async_computation.3 | async-start | bytes 4194304 | tf_op jit(solution)/shard_map/all_to_all | solution.py:737
  139.2 5.7 %collective-permute-start.3 = (f32[2,128]{1,0:T(2,128)S(1)}, f32[2,128]{1,0:T(2,128)S(1)}, u32[]{:S(2)}, u32[]{:S(2)}) collective-permute-start(f32[2,128]{1,0:T(2,128)S(1)} %copy-done.1), channel_id=1, source_target_pairs={{0,32},{32,64},{64,96},{96,0},{1,33},{33,65},{65,97},{97,1},{2,34}... | collective-permute-start | bytes 3080 | tf_op jit(solution)/shard_map/ppermute | solution.py:732
  140.6 4.3 %collective-permute-start.4 = (f32[2,128]{1,0:T(2,128)S(1)}, f32[2,128]{1,0:T(2,128)S(1)}, u32[]{:S(2)}, u32[]{:S(2)}) collective-permute-start(f32[2,128]{1,0:T(2,128)S(1)} %copy-done.1), channel_id=1, source_target_pairs={{0,64},{32,96},{64,0},{96,32},{1,65},{33,97},{65,1},{97,33},{2,66}... | collective-permute-start | bytes 3080 | tf_op jit(solution)/shard_map/ppermute | solution.py:732
  142.3 2.8 %collective-permute-start.5 = (f32[2,128]{1,0:T(2,128)S(1)}, f32[2,128]{1,0:T(2,128)S(1)}, u32[]{:S(2)}, u32[]{:S(2)}) collective-permute-start(f32[2,128]{1,0:T(2,128)S(1)} %copy-done.1), channel_id=1, source_target_pairs={{0,96},{32,0},{64,32},{96,64},{1,97},{33,1},{65,33},{97,65},{2,98}... | collective-permute-start | bytes 3080 | tf_op jit(solution)/shard_map/ppermute | solution.py:732
  146.6 7.5 %collective-permute-start.6 = (f32[8]{0:T(128)S(1)}, f32[8]{0:T(128)S(1)}, u32[]{:S(2)}, u32[]{:S(2)}) collective-permute-start(f32[8]{0:T(128)S(1)} %convert_reduce_fusion), channel_id=1, source_target_pairs={{0,32},{32,64},{64,96},{96,0},{1,33},{33,65},{65,97},{97,1},{2,34}... | collective-permute-start | bytes 104 | tf_op jit(solution)/shard_map/ppermute | solution.py:732
  147.8 6.3 %collective-permute-start.7 = (f32[8]{0:T(128)S(1)}, f32[8]{0:T(128)S(1)}, u32[]{:S(2)}, u32[]{:S(2)}) collective-permute-start(f32[8]{0:T(128)S(1)} %convert_reduce_fusion), channel_id=1, source_target_pairs={{0,64},{32,96},{64,0},{96,32},{1,65},{33,97},{65,1},{97,33},{2,66}... | collective-permute-start | bytes 104 | tf_op jit(solution)/shard_map/ppermute | solution.py:732
  151.1 3.1 %collective-permute-start.8 = (f32[8]{0:T(128)S(1)}, f32[8]{0:T(128)S(1)}, u32[]{:S(2)}, u32[]{:S(2)}) collective-permute-start(f32[8]{0:T(128)S(1)} %convert_reduce_fusion), channel_id=1, source_target_pairs={{0,96},{32,0},{64,32},{96,64},{1,97},{33,1},{65,33},{97,65},{2,98}... | collective-permute-start | bytes 104 | tf_op jit(solution)/shard_map/ppermute | solution.py:732

commit v7 on v6

--- a/solution.py
+++ b/solution.py
@@ -26,7 +26,7 @@
 TILES = LENGTH // TILE
 PAIR = TILE // BLOCK
 KEYS = 256
-UNROLL = 6
+UNROLL = 8
 MOST_PAIRS = (LENGTH * (1024 // TILE + 1) + TILES * (BLOCK - 1 + KEYS - 1)) // KEYS
 MOST_STEPS = MOST_PAIRS // UNROLL + 1
 MOST_PAIRS = MOST_STEPS * UNROLL
@@ -276,8 +276,7 @@
 ):
     hat_outs, probs_out, refs = refs[:2], refs[2], refs[3:]
     (moments_ref, norm_ref, out_ref), refs = refs[:3], refs[3:]
-    hats, refs = refs[:2], refs[2:]
-    q_turned_ref, k_hat_ref = hats
+    (q_turned_ref, k_hat_ref), refs = refs[:2], refs[2:]
     recv_ref, extra_ref, starts, terms, fold, probs, sums = refs[:7]
     in_sems, extra_sem, out_sems, prob_sems = refs[7:]
 
@@ -291,8 +290,8 @@
     def leaving(i, n):
         rows = tile_at(i)
         source, target = (
-            (q_turned_ref.at[:, rows], hat_outs[0].at[:, rows]),
-            (k_hat_ref.at[rows, :], hat_outs[1].at[rows, :]),
+            (q_turned_ref.at[pl.ds(0, HEAD_DIM), rows], hat_outs[0].at[:, rows]),
+            (k_hat_ref.at[rows, pl.ds(0, HEAD_DIM)], hat_outs[1].at[rows, :]),
             (sums.at[i], out_ref.at[i]),
         )[n]
         return pltpu.make_async_copy(source, target, out_sems.at[n, i])
@@ -306,6 +305,16 @@
     total = find_pairs(extra_ref[:, 0, :].astype(F32), starts, pair_ref, span_rows_ref)
     total_ref[0] = total
     gains = jnp.concatenate([gains_ref[...], jnp.zeros((6, HEAD_DIM), F32)], 0).T
+
+    lane = lax.broadcasted_iota(I32, (1, HEAD_DIM), 1)
+    seg_from = jnp.full((1, HEAD_DIM), LENGTH, I32)
+    seg_to = jnp.full((1, HEAD_DIM), LENGTH, I32)
+    for s in range(IMAGES):
+        seg_from = jnp.where(lane == s, starts[s], seg_from)
+        seg_to = jnp.where(lane == s, starts[s + 1], seg_to)
+    k_hat_ref[LENGTH:, :HEAD_DIM] = jnp.zeros((KEYS, HEAD_DIM), BF16)
+    nobody = jnp.where(lane == IMAGES, 1.0, 0.0)
+    k_hat_ref[LENGTH:, HEAD_DIM:] = jnp.broadcast_to(nobody, (KEYS, HEAD_DIM)).astype(BF16)
 
     def prepare(i, most):
         arrival(i).wait()
@@ -321,9 +330,16 @@
             hat = centre * inverse * gains[:, n : n + 1]
             sizes.append(jnp.maximum(most[n], mean_down(hat * hat)))
             if n == 0:
-                q_turned_ref[:, rows] = hat.astype(BF16)
+                q_turned_ref[:HEAD_DIM, rows] = hat.astype(BF16)
             else:
-                k_hat_ref[rows, :] = hat.astype(BF16).T
+                k_hat_ref[rows, :HEAD_DIM] = hat.astype(BF16).T
+        seg_q = [extra_ref[i * PAIR + b, 0:1, :].astype(F32) for b in range(PAIR)]
+        own = jnp.concatenate(seg_q, 1).astype(I32)
+        segment = lax.broadcasted_iota(I32, (HEAD_DIM, TILE), 0)
+        q_turned_ref[HEAD_DIM:, rows] = jnp.where(segment == own, 0.0, NEG).astype(BF16)
+        row = lax.broadcasted_iota(I32, (TILE, HEAD_DIM), 0) + i * TILE
+        inside = (row >= seg_from) & (row < seg_to)
+        k_hat_ref[rows, HEAD_DIM:] = jnp.where(inside, 1.0, 0.0).astype(BF16)
         for n in range(2):
             leaving(i, n).start()
         sums[i] = jnp.zeros((HEAD_DIM, TILE), F32)
@@ -336,13 +352,11 @@
     bound = jnp.max(most_q) * jnp.max(most_k) * HEAD_DIM
 
     def scores_of(pairs):
-        tiles = [
-            dot(k_hat_ref[pl.ds(at, KEYS), :], q_turned_ref[:, tile_at(i)]) for _, i, at, _ in pairs
-        ]
-        return [
-            masked(tile, span_rows_ref, i, mask_at)
-            for tile, (_, i, _, mask_at) in zip(tiles, pairs)
-        ]
+        tiles = []
+        for _, i, at, mask_at in pairs:
+            at = pl.multiple_of(jnp.where(mask_at < 0, LENGTH, at), BLOCK)
+            tiles.append(dot(k_hat_ref[pl.ds(at, KEYS), :], q_turned_ref[:, tile_at(i)]))
+        return tiles
 
     @pl.when(jnp.logical_not(bound <= SAFE_LOGIT * SAFE_LOGIT))
     def _():
@@ -425,7 +439,7 @@
         in_specs=[HBM_SPEC, VMEM_SPEC],
         out_specs=[SMEM_SPEC] * 2 + [VMEM_SPEC] + [HBM_SPEC] * 3 + [VMEM_SPEC] * 2 + [HBM_SPEC],
         out_shape=[
-            shape((3, MOST_PAIRS), I32),
+            shape((3, MOST_PAIRS + UNROLL), I32),
             shape((1,), I32),
             shape((TILES, 2, TILE), I32),
             *[shape(*hat) for hat in hats],
@@ -435,7 +449,8 @@
             shape((TILES, HEAD_DIM, TILE), F32),
         ],
         scratch_shapes=[
-            *[pltpu.VMEM(*hat) for hat in hats],
+            pltpu.VMEM((2 * HEAD_DIM, LENGTH), BF16),
+            pltpu.VMEM((LENGTH + KEYS, 2 * HEAD_DIM), BF16),
             pltpu.VMEM((BLOCKS, 3 * BLOCK, 128), BF16),
             pltpu.VMEM((BLOCKS, EXTRA, 128), BF16),
             pltpu.SMEM((IMAGES + 1,), I32),

time: 172 us -> 169 us (0.983)
  Pallas kernels: 71.9 us -> 68 us
  starting transfers between devices: 42.6 us -> 44.5 us
    pallas_call x1, Pallas kernels: 23.3 us -> 20.5 us  [run_attend(): pl.pallas_call(attend_kernel, in_specs=[HBM_SPEC, VMEM_SPEC], out_specs=[...]
    ppermute x9, starting transfers between devices: 14.5 us -> 16.4 us  [over_packs(): moved.append(lax.ppermute(value, 'pack', pairs))]
  transfers between devices with their start and end apart: 13 -> 13, of which waited for: 6 -> 6; matrix products, arithmetic and copies ran while one was open for 3% -> 3% of each run, Pallas kernels for 31% -> 29%
where the time goes in v7:
time: 169 us; the launch traced here: 168 us
  Pallas kernels  68 us (40%)
  waiting for transfers between devices  48.9 us (29%)
  starting transfers between devices  44.5 us (26%)
  other arithmetic  4.58 us (3%)
    all_to_all x4, waiting for transfers between devices, exchange(): return lax.all_to_all(slab, 'seq', split_axis=0, concat_axis=0, tiled=True)  46.9 us
    all_to_all x4, starting transfers between devices, exchange(): return lax.all_to_all(slab, 'seq', split_axis=0, concat_axis=0, tiled=True)  28 us
    pallas_call x1, Pallas kernels, run_backward(): pl.pallas_call(backward_kernel, in_specs=[SMEM_SPEC] * 2 + [HBM_SPEC] * 4...  22.6 us
    pallas_call x1, Pallas kernels, run_attend(): pl.pallas_call(attend_kernel, in_specs=[HBM_SPEC, VMEM_SPEC], out_specs=[...  20.5 us
    ppermute x9, starting transfers between devices, over_packs(): moved.append(lax.ppermute(value, 'pack', pairs))  16.4 us
    pallas_call x1, Pallas kernels, run_loss(): pl.pallas_call(loss_kernel, in_specs=[SMEM_SPEC] * 4 + [HBM_SPEC] * 3, ou...  11.2 us
    pallas_call x2, Pallas kernels, pack_rows(): pl.pallas_call(functools.partial(pack_kernel, count), in_specs=[HBM_SPEC]...  7.9 us
    pallas_call x2, Pallas kernels, unpack_rows(): pl.pallas_call(functools.partial(unpack_kernel, turned), in_specs=[HBM_SP...  5.91 us
  transfers between devices with their start and end apart: 13, of which 6 were waited for; matrix products, arithmetic and copies ran while one was open for 3% of the time, Pallas kernels for 29%

profile of v7, /device:TPU:1, one launch (start us, length us, event | category | flops | bytes accessed | tf_op | source)
XLA Modules:
  0.0 167.5 jit_solution(10678470343926878235)
XLA Ops:
  0.6 4.8 %pack_first.1 = bf16[32,400,128]{2,1,0:T(8,128)(2,1)} custom-call(bf16[1,128,4096]{2,1,0:T(8,128)(2,1)} %refs_0_.2, bf16[1,128,4096]{2,1,0:T(8,128)(2,1)} %refs_1_.1, bf16[1,128,4096]{2,1,0:T(8,128)(2,1)} %refs_2_.1, s32[1,128]{1,0:T(1,128)} %refs_3_.1), custom_call_target="tpu_custom_call" | custom-call | tf_op jit(solution)/shard_map/pack_first/pallas_call | solution.py:92
  5.4 9.5 %all-to-all-start = ((bf16[32,400,128]{2,1,0:T(8,128)(2,1)}), bf16[32,400,128]{2,1,0:T(8,128)(2,1)}, u32[]{:S(2)}, u32[]{:S(2)}) async-start(bf16[32,400,128]{2,1,0:T(8,128)(2,1)} %pack_first.1), calls=%async_computation | async-start | bytes 6553600 | tf_op jit(solution)/shard_map/all_to_all | solution.py:752
  15.0 0.1 select_reduce_fusion
  15.1 1.4 collective-permute-start
  16.4 2.6 %collective-permute-start.1 = (f32[1,128]{1,0:T(1,128)S(1)}, f32[1,128]{1,0:T(1,128)S(1)}, u32[]{:S(2)}, u32[]{:S(2)}) collective-permute-start(f32[1,128]{1,0:T(1,128)S(1)} %convert_bitcast_fusion), channel_id=1, source_target_pairs={{0,64},{32,96},{64,0},{96,32},{1,65},{33,97},{65,1},{97,33},{2,66}... | collective-permute-start | bytes 1544 | tf_op jit(solution)/shard_map/ppermute | solution.py:747
  19.0 1.1 collective-permute-start.2
  20.1 0.2 collective-permute-done.1
  20.3 1.5 collective-permute-done.2
  21.8 0.6 concatenate.3.refs_1_
  22.4 3.1 %pack_second.1 = bf16[32,144,128]{2,1,0:T(8,128)(2,1)} custom-call(bf16[1,128,4096]{2,1,0:T(8,128)(2,1)} %refs_0_.3, f32[5,128]{1,0:T(8,128)} %concatenate.3.refs_1_), custom_call_target="tpu_custom_call" | custom-call | tf_op jit(solution)/shard_map/pack_second/pallas_call | solution.py:92
  25.6 30.5 %all-to-all-done.all_ref = bf16[32,400,128]{2,1,0:T(8,128)(2,1)} async-done(((bf16[32,400,128]{2,1,0:T(8,128)(2,1)}), bf16[32,400,128]{2,1,0:T(8,128)(2,1)}, u32[]{:S(2)}, u32[]{:S(2)}) %all-to-all-start) | async-done | bytes 3276832 | tf_op jit(solution)/shard_map/all_to_all | solution.py:752
  56.1 5.7 %all-to-all-start.1 = ((bf16[32,144,128]{2,1,0:T(8,128)(2,1)}), bf16[32,144,128]{2,1,0:T(8,128)(2,1)}, u32[]{:S(2)}, u32[]{:S(2)}) async-start(bf16[32,144,128]{2,1,0:T(8,128)(2,1)} %pack_second.1), calls=%async_computation.1 | async-start | bytes 2359296 | tf_op jit(solution)/shard_map/all_to_all | solution.py:752
  61.8 20.5 %attend.1 = (s32[3,112]{1,0:T(4,128)}, s32[1]{0:T(128)}, s32[16,2,256]{2,1,0:T(2,128)}, bf16[128,4096]{1,0:T(8,128)(2,1)}, bf16[4096,128]{1,0:T(8,128)(2,1)}, /*...) custom-call(bf16[32,400,128]{2,1,0:T(8,128)(2,1)} %all-to-all-done.all, ...), custom_call_target="tpu_custom_call" | custom-call | flops 8589934592 | bytes 33554432 | tf_op jit(solution)/shard_map/attend/pallas_call | solution.py:437
  82.3 11.2 %loss_and_grad_value.1 = (bf16[32,272,128]{2,1,0:T(8,128)(2,1)}, bf16[128,4096]{1,0:T(8,128)(2,1)}, f32[16,1,256]{2,1,0:T(1,128)}, f32[1,128]{1,0:T(1,128)}) custom-call(s32[1,16]{1,0:T(1,128)} %labels_ref.1, f32[8]{0:T(128)} %mixture_ref.1, s32[3,112]{1,0:T(4,128)} %get-tuple-element.27.pair_ref, s32[1]{0:T(128)} %get-tuple-element.28.total_ref, ...), custom_call_target="tpu_custom_call" | custom-call | tf_op jit(solution)/shard_map/loss_and_grad_value/pallas_call | solution.py:590
  93.5 7.4 %all-to-all-start.2 = ((bf16[32,272,128]{2,1,0:T(8,128)(2,1)}), bf16[32,272,128]{2,1,0:T(8,128)(2,1)}, u32[]{:S(2)}, u32[]{:S(2)}) async-start(bf16[32,272,128]{2,1,0:T(8,128)(2,1)} %get-tuple-element.31), calls=%async_computation.2 | async-start | bytes 4456448 | tf_op jit(solution)/shard_map/all_to_all | solution.py:752
  100.9 22.6 %backward.1 = (bf16[32,256,128]{2,1,0:T(8,128)(2,1)}, f32[2,128]{1,0:T(2,128)}) custom-call(s32[3,112]{1,0:T(4,128)} %get-tuple-element.27.pair_ref, s32[1]{0:T(128)} %get-tuple-element.28.total_ref, bf16[32,400,128]{2,1,0:T(8,128)(2,1)} %all-to-all-done.all_ref, bf16[128,4096]{1,0:T(8,128)(2,1)} %get-tuple-element.32.q_turned_in, ...), custom_call_target="tpu_custom_call" | custom-call | flops 8589934592 | bytes 33554432 | tf_op jit(solution)/shard_map/backward/pallas_call | solution.py:718
  123.5 7.1 %all-to-all-done.2.in_ref = bf16[32,272,128]{2,1,0:T(8,128)(2,1)} async-done(((bf16[32,272,128]{2,1,0:T(8,128)(2,1)}), bf16[32,272,128]{2,1,0:T(8,128)(2,1)}, u32[]{:S(2)}, u32[]{:S(2)}) %all-to-all-start.2) | async-done | bytes 2228256 | tf_op jit(solution)/shard_map/all_to_all | solution.py:752
  130.7 5.4 %all-to-all-start.3 = ((bf16[32,256,128]{2,1,0:T(8,128)(2,1)}), bf16[32,256,128]{2,1,0:T(8,128)(2,1)}, u32[]{:S(2)}, u32[]{:S(2)}) async-start(bf16[32,256,128]{2,1,0:T(8,128)(2,1)} %get-tuple-element.42), calls=%async_computation.3 | async-start | bytes 4194304 | tf_op jit(solution)/shard_map/all_to_all | solution.py:752
  136.1 1.4 collective-permute-start.3
  137.5 3.6 %collective-permute-start.4 = (f32[2,128]{1,0:T(2,128)S(1)}, f32[2,128]{1,0:T(2,128)S(1)}, u32[]{:S(2)}, u32[]{:S(2)}) collective-permute-start(f32[2,128]{1,0:T(2,128)S(1)} %copy-done.1), channel_id=1, source_target_pairs={{0,64},{32,96},{64,0},{96,32},{1,65},{33,97},{65,1},{97,33},{2,66}... | collective-permute-start | bytes 3080 | tf_op jit(solution)/shard_map/ppermute | solution.py:747
  141.0 2.0 %collective-permute-start.5 = (f32[2,128]{1,0:T(2,128)S(1)}, f32[2,128]{1,0:T(2,128)S(1)}, u32[]{:S(2)}, u32[]{:S(2)}) collective-permute-start(f32[2,128]{1,0:T(2,128)S(1)} %copy-done.1), channel_id=1, source_target_pairs={{0,96},{32,0},{64,32},{96,64},{1,97},{33,1},{65,33},{97,65},{2,98}... | collective-permute-start | bytes 3080 | tf_op jit(solution)/shard_map/ppermute | solution.py:747
  143.0 0.6 reduce_sum.37
  143.6 0.2 collective-permute-done.5
  143.9 0.6 add_add_fusion
  144.4 0.9 convert_reduce_fusion
  145.3 1.2 collective-permute-start.6
  146.5 3.3 %collective-permute-start.7 = (f32[8]{0:T(128)S(1)}, f32[8]{0:T(128)S(1)}, u32[]{:S(2)}, u32[]{:S(2)}) collective-permute-start(f32[8]{0:T(128)S(1)} %convert_reduce_fusion), channel_id=1, source_target_pairs={{0,64},{32,96},{64,0},{96,32},{1,65},{33,97},{65,1},{97,33},{2,66}... | collective-permute-start | bytes 104 | tf_op jit(solution)/shard_map/ppermute | solution.py:747
  149.8 3.0 %unpack_first.1 = (bf16[1,128,4096]{2,1,0:T(8,128)(2,1)}, bf16[1,128,4096]{2,1,0:T(8,128)(2,1)}) custom-call(bf16[32,272,128]{2,1,0:T(8,128)(2,1)} %all-to-all-done.2.in_ref), custom_call_target="tpu_custom_call" | custom-call | tf_op jit(solution)/shard_map/unpack_first/pallas_call | solution.py:141
  152.8 1.3 fusion
  154.1 1.2 broadcast_divide_fusion
  155.3 9.2 %all-to-all-done.3.in_ref = bf16[32,256,128]{2,1,0:T(8,128)(2,1)} async-done(((bf16[32,256,128]{2,1,0:T(8,128)(2,1)}), bf16[32,256,128]{2,1,0:T(8,128)(2,1)}, u32[]{:S(2)}, u32[]{:S(2)}) %all-to-all-start.3) | async-done | bytes 2097184 | tf_op jit(solution)/shard_map/all_to_all | solution.py:752
  164.5 2.9 %unpack_last.1 = (bf16[1,128,4096]{2,1,0:T(8,128)(2,1)}, bf16[1,128,4096]{2,1,0:T(8,128)(2,1)}) custom-call(bf16[32,256,128]{2,1,0:T(8,128)(2,1)} %all-to-all-done.3.in_ref), custom_call_target="tpu_custom_call" | custom-call | tf_op jit(solution)/shard_map/unpack_last/pallas_call | solution.py:141
  (20 shorter events, 0.1 us)
Async XLA Ops:
  5.4 9.5 %copy-start.2 = (s32[1,128]{1,0:T(1,128)S(1)}, s32[1,128]{1,0:T(1,128)}, u32[]{:S(2)}) copy-start(s32[1,128]{1,0:T(1,128)} %refs_3_.1) | copy-start | bytes 1540
  5.4 9.5 %copy-start.3 = (s32[1,16]{1,0:T(1,128)S(1)}, s32[1,16]{1,0:T(1,128)}, u32[]{:S(2)}) copy-start(s32[1,16]{1,0:T(1,128)} %labels_ref.1) | copy-start | bytes 196
  5.4 50.6 %all-to-all-start = ((bf16[32,400,128]{2,1,0:T(8,128)(2,1)}), bf16[32,400,128]{2,1,0:T(8,128)(2,1)}, u32[]{:S(2)}, u32[]{:S(2)}) async-start(bf16[32,400,128]{2,1,0:T(8,128)(2,1)} %pack_first.1), calls=%async_computation | async-start | bytes 6553600 | tf_op jit(solution)/shard_map/all_to_all | solution.py:752
  15.1 5.1 %collective-permute-start = (f32[1,128]{1,0:T(1,128)S(1)}, f32[1,128]{1,0:T(1,128)S(1)}, u32[]{:S(2)}, u32[]{:S(2)}) collective-permute-start(f32[1,128]{1,0:T(1,128)S(1)} %convert_bitcast_fusion), channel_id=1, source_target_pairs={{0,32},{32,64},{64,96},{96,0},{1,33},{33,65},{65,97},{97,1},{2,34}... | collective-permute-start | bytes 1544 | tf_op jit(solution)/shard_map/ppermute | solution.py:747
  16.4 3.9 %collective-permute-start.1 = (f32[1,128]{1,0:T(1,128)S(1)}, f32[1,128]{1,0:T(1,128)S(1)}, u32[]{:S(2)}, u32[]{:S(2)}) collective-permute-start(f32[1,128]{1,0:T(1,128)S(1)} %convert_bitcast_fusion), channel_id=1, source_target_pairs={{0,64},{32,96},{64,0},{96,32},{1,65},{33,97},{65,1},{97,33},{2,66}... | collective-permute-start | bytes 1544 | tf_op jit(solution)/shard_map/ppermute | solution.py:747
  19.0 2.8 %collective-permute-start.2 = (f32[1,128]{1,0:T(1,128)S(1)}, f32[1,128]{1,0:T(1,128)S(1)}, u32[]{:S(2)}, u32[]{:S(2)}) collective-permute-start(f32[1,128]{1,0:T(1,128)S(1)} %convert_bitcast_fusion), channel_id=1, source_target_pairs={{0,96},{32,0},{64,32},{96,64},{1,97},{33,1},{65,33},{97,65},{2,98}... | collective-permute-start | bytes 1544 | tf_op jit(solution)/shard_map/ppermute | solution.py:747
  56.1 26.2 %all-to-all-start.1 = ((bf16[32,144,128]{2,1,0:T(8,128)(2,1)}), bf16[32,144,128]{2,1,0:T(8,128)(2,1)}, u32[]{:S(2)}, u32[]{:S(2)}) async-start(bf16[32,144,128]{2,1,0:T(8,128)(2,1)} %pack_second.1), calls=%async_computation.1 | async-start | bytes 2359296 | tf_op jit(solution)/shard_map/all_to_all | solution.py:752
  93.5 37.2 %all-to-all-start.2 = ((bf16[32,272,128]{2,1,0:T(8,128)(2,1)}), bf16[32,272,128]{2,1,0:T(8,128)(2,1)}, u32[]{:S(2)}, u32[]{:S(2)}) async-start(bf16[32,272,128]{2,1,0:T(8,128)(2,1)} %get-tuple-element.31), calls=%async_computation.2 | async-start | bytes 4456448 | tf_op jit(solution)/shard_map/all_to_all | solution.py:752
  123.5 12.6 %copy-start.1 = (f32[2,128]{1,0:T(2,128)S(1)}, f32[2,128]{1,0:T(2,128)}, u32[]{:S(2)}) copy-start(f32[2,128]{1,0:T(2,128)} %get-tuple-element.46) | copy-start | bytes 3076
  123.5 19.5 %copy-start = (f32[8]{0:T(128)S(1)}, f32[8]{0:T(128)}, u32[]{:S(2)}) copy-start(f32[8]{0:T(128)} %mixture_ref.1) | copy-start | bytes 100
  130.7 22.2 %copy-start.4 = (f32[1,128]{1,0:T(1,128)S(1)}, f32[1,128]{1,0:T(1,128)}, u32[]{:S(2)}) copy-start(f32[1,128]{1,0:T(1,128)} %get-tuple-element.47) | copy-start | bytes 1540
  130.7 33.8 %all-to-all-start.3 = ((bf16[32,256,128]{2,1,0:T(8,128)(2,1)}), bf16[32,256,128]{2,1,0:T(8,128)(2,1)}, u32[]{:S(2)}, u32[]{:S(2)}) async-start(bf16[32,256,128]{2,1,0:T(8,128)(2,1)} %get-tuple-element.42), calls=%async_computation.3 | async-start | bytes 4194304 | tf_op jit(solution)/shard_map/all_to_all | solution.py:752
  136.1 7.5 %collective-permute-start.3 = (f32[2,128]{1,0:T(2,128)S(1)}, f32[2,128]{1,0:T(2,128)S(1)}, u32[]{:S(2)}, u32[]{:S(2)}) collective-permute-start(f32[2,128]{1,0:T(2,128)S(1)} %copy-done.1), channel_id=1, source_target_pairs={{0,32},{32,64},{64,96},{96,0},{1,33},{33,65},{65,97},{97,1},{2,34}... | collective-permute-start | bytes 3080 | tf_op jit(solution)/shard_map/ppermute | solution.py:747
  137.5 6.1 %collective-permute-start.4 = (f32[2,128]{1,0:T(2,128)S(1)}, f32[2,128]{1,0:T(2,128)S(1)}, u32[]{:S(2)}, u32[]{:S(2)}) collective-permute-start(f32[2,128]{1,0:T(2,128)S(1)} %copy-done.1), channel_id=1, source_target_pairs={{0,64},{32,96},{64,0},{96,32},{1,65},{33,97},{65,1},{97,33},{2,66}... | collective-permute-start | bytes 3080 | tf_op jit(solution)/shard_map/ppermute | solution.py:747
  141.0 2.8 %collective-permute-start.5 = (f32[2,128]{1,0:T(2,128)S(1)}, f32[2,128]{1,0:T(2,128)S(1)}, u32[]{:S(2)}, u32[]{:S(2)}) collective-permute-start(f32[2,128]{1,0:T(2,128)S(1)} %copy-done.1), channel_id=1, source_target_pairs={{0,96},{32,0},{64,32},{96,64},{1,97},{33,1},{65,33},{97,65},{2,98}... | collective-permute-start | bytes 3080 | tf_op jit(solution)/shard_map/ppermute | solution.py:747
  145.3 7.5 %collective-permute-start.6 = (f32[8]{0:T(128)S(1)}, f32[8]{0:T(128)S(1)}, u32[]{:S(2)}, u32[]{:S(2)}) collective-permute-start(f32[8]{0:T(128)S(1)} %convert_reduce_fusion), channel_id=1, source_target_pairs={{0,32},{32,64},{64,96},{96,0},{1,33},{33,65},{65,97},{97,1},{2,34}... | collective-permute-start | bytes 104 | tf_op jit(solution)/shard_map/ppermute | solution.py:747
  146.5 6.3 %collective-permute-start.7 = (f32[8]{0:T(128)S(1)}, f32[8]{0:T(128)S(1)}, u32[]{:S(2)}, u32[]{:S(2)}) collective-permute-start(f32[8]{0:T(128)S(1)} %convert_reduce_fusion), channel_id=1, source_target_pairs={{0,64},{32,96},{64,0},{96,32},{1,65},{33,97},{65,1},{97,33},{2,66}... | collective-permute-start | bytes 104 | tf_op jit(solution)/shard_map/ppermute | solution.py:747
  149.8 3.1 %collective-permute-start.8 = (f32[8]{0:T(128)S(1)}, f32[8]{0:T(128)S(1)}, u32[]{:S(2)}, u32[]{:S(2)}) collective-permute-start(f32[8]{0:T(128)S(1)} %convert_reduce_fusion), channel_id=1, source_target_pairs={{0,96},{32,0},{64,32},{96,64},{1,97},{33,1},{65,33},{97,65},{2,98}... | collective-permute-start | bytes 104 | tf_op jit(solution)/shard_map/ppermute | solution.py:747

commit v8 on v7

--- a/solution.py
+++ b/solution.py
@@ -33,7 +33,7 @@
 RING = 4
 SAFE_LOGIT = 70.0
 EXTRA = 16
-CHUNK = 4
+CHUNK = 8
 CHUNKS = HEADS // CHUNK
 VMEM_LIMIT = 63 * 1024 * 1024
 

time: 169 us -> 169 us (level)
  starting transfers between devices: 44.5 us -> 40.2 us
  waiting for transfers between devices: 48.9 us -> 51.9 us
  Pallas kernels: 68 us -> 70.5 us
    ppermute x9, starting transfers between devices: 16.4 us -> 12.1 us  [over_packs(): moved.append(lax.ppermute(value, 'pack', pairs))]
    all_to_all x4, waiting for transfers between devices: 46.9 us -> 49.1 us  [exchange(): return lax.all_to_all(slab, 'seq', split_axis=0, concat_axis=0, tiled=True)]
  transfers between devices with their start and end apart: 13 -> 13, of which waited for: 6 -> 7; matrix products, arithmetic and copies ran while one was open for 3% -> 3% of each run, Pallas kernels for 29% -> 31%
where the time goes in v8:
time: 169 us
  Pallas kernels  70.5 us (42%)
  waiting for transfers between devices  51.9 us (31%)
  starting transfers between devices  40.2 us (24%)
  other arithmetic  4.58 us (3%)
    all_to_all x4, waiting for transfers between devices, exchange(): return lax.all_to_all(slab, 'seq', split_axis=0, concat_axis=0, tiled=True)  49.1 us
    all_to_all x4, starting transfers between devices, exchange(): return lax.all_to_all(slab, 'seq', split_axis=0, concat_axis=0, tiled=True)  28.1 us
    pallas_call x1, Pallas kernels, run_backward(): pl.pallas_call(backward_kernel, in_specs=[SMEM_SPEC] * 2 + [HBM_SPEC] * 4...  24.1 us
    pallas_call x1, Pallas kernels, run_attend(): pl.pallas_call(attend_kernel, in_specs=[HBM_SPEC, VMEM_SPEC], out_specs=[...  21.8 us
    ppermute x9, starting transfers between devices, over_packs(): moved.append(lax.ppermute(value, 'pack', pairs))  12.1 us
    pallas_call x1, Pallas kernels, run_loss(): pl.pallas_call(loss_kernel, in_specs=[SMEM_SPEC] * 4 + [HBM_SPEC] * 3, ou...  11.6 us
    pallas_call x2, Pallas kernels, pack_rows(): pl.pallas_call(functools.partial(pack_kernel, count), in_specs=[HBM_SPEC]...  7.1 us
    pallas_call x2, Pallas kernels, unpack_rows(): pl.pallas_call(functools.partial(unpack_kernel, turned), in_specs=[HBM_SP...  5.92 us
  transfers between devices with their start and end apart: 13, of which 7 were waited for; matrix products, arithmetic and copies ran while one was open for 3% of the time, Pallas kernels for 31%

profile of v8, /device:TPU:1, one launch (start us, length us, event | category | flops | bytes accessed | tf_op | source)
XLA Modules:
  0.0 168.8 jit_solution(12208966060454584589)
XLA Ops:
  0.6 4.2 %pack_first.1 = bf16[32,400,128]{2,1,0:T(8,128)(2,1)} custom-call(bf16[1,128,4096]{2,1,0:T(8,128)(2,1)} %refs_0_.2, bf16[1,128,4096]{2,1,0:T(8,128)(2,1)} %refs_1_.1, bf16[1,128,4096]{2,1,0:T(8,128)(2,1)} %refs_2_.1, s32[1,128]{1,0:T(1,128)} %refs_3_.1), custom_call_target="tpu_custom_call" | custom-call | tf_op jit(solution)/shard_map/pack_first/pallas_call | solution.py:92
  4.8 9.5 %all-to-all-start = ((bf16[32,400,128]{2,1,0:T(8,128)(2,1)}), bf16[32,400,128]{2,1,0:T(8,128)(2,1)}, u32[]{:S(2)}, u32[]{:S(2)}) async-start(bf16[32,400,128]{2,1,0:T(8,128)(2,1)} %pack_first.1), calls=%async_computation | async-start | bytes 6553600 | tf_op jit(solution)/shard_map/all_to_all | solution.py:752
  14.4 1.4 collective-permute-start
  15.8 2.6 %collective-permute-start.1 = (f32[1,128]{1,0:T(1,128)S(1)}, f32[1,128]{1,0:T(1,128)S(1)}, u32[]{:S(2)}, u32[]{:S(2)}) collective-permute-start(f32[1,128]{1,0:T(1,128)S(1)} %convert_bitcast_fusion), channel_id=1, source_target_pairs={{0,64},{32,96},{64,0},{96,32},{1,65},{33,97},{65,1},{97,33},{2,66}... | collective-permute-start | bytes 1544 | tf_op jit(solution)/shard_map/ppermute | solution.py:747
  18.4 1.1 collective-permute-start.2
  19.5 0.2 collective-permute-done.1
  19.7 1.5 collective-permute-done.2
  21.2 0.6 concatenate.3.refs_1_
  21.8 2.9 %pack_second.1 = bf16[32,144,128]{2,1,0:T(8,128)(2,1)} custom-call(bf16[1,128,4096]{2,1,0:T(8,128)(2,1)} %refs_0_.3, f32[5,128]{1,0:T(8,128)} %concatenate.3.refs_1_), custom_call_target="tpu_custom_call" | custom-call | tf_op jit(solution)/shard_map/pack_second/pallas_call | solution.py:92
  24.8 30.7 %all-to-all-done.all_ref = bf16[32,400,128]{2,1,0:T(8,128)(2,1)} async-done(((bf16[32,400,128]{2,1,0:T(8,128)(2,1)}), bf16[32,400,128]{2,1,0:T(8,128)(2,1)}, u32[]{:S(2)}, u32[]{:S(2)}) %all-to-all-start) | async-done | bytes 3276832 | tf_op jit(solution)/shard_map/all_to_all | solution.py:752
  55.5 5.7 %all-to-all-start.1 = ((bf16[32,144,128]{2,1,0:T(8,128)(2,1)}), bf16[32,144,128]{2,1,0:T(8,128)(2,1)}, u32[]{:S(2)}, u32[]{:S(2)}) async-start(bf16[32,144,128]{2,1,0:T(8,128)(2,1)} %pack_second.1), calls=%async_computation.1 | async-start | bytes 2359296 | tf_op jit(solution)/shard_map/all_to_all | solution.py:752
  61.2 21.8 %attend.1 = (s32[3,112]{1,0:T(4,128)}, s32[1]{0:T(128)}, s32[16,2,256]{2,1,0:T(2,128)}, bf16[128,4096]{1,0:T(8,128)(2,1)}, bf16[4096,128]{1,0:T(8,128)(2,1)}, /*...) custom-call(bf16[32,400,128]{2,1,0:T(8,128)(2,1)} %all-to-all-done.all, ...), custom_call_target="tpu_custom_call" | custom-call | flops 8589934592 | bytes 33554432 | tf_op jit(solution)/shard_map/attend/pallas_call | solution.py:437
  83.0 11.6 %loss_and_grad_value.1 = (bf16[32,272,128]{2,1,0:T(8,128)(2,1)}, bf16[128,4096]{1,0:T(8,128)(2,1)}, f32[16,1,256]{2,1,0:T(1,128)}, f32[1,128]{1,0:T(1,128)}) custom-call(s32[1,16]{1,0:T(1,128)} %labels_ref.1, f32[8]{0:T(128)} %mixture_ref.1, s32[3,112]{1,0:T(4,128)} %get-tuple-element.27.pair_ref, s32[1]{0:T(128)} %get-tuple-element.28.total_ref, ...), custom_call_target="tpu_custom_call" | custom-call | tf_op jit(solution)/shard_map/loss_and_grad_value/pallas_call | solution.py:590
  94.6 7.5 %all-to-all-start.2 = ((bf16[32,272,128]{2,1,0:T(8,128)(2,1)}), bf16[32,272,128]{2,1,0:T(8,128)(2,1)}, u32[]{:S(2)}, u32[]{:S(2)}) async-start(bf16[32,272,128]{2,1,0:T(8,128)(2,1)} %get-tuple-element.31), calls=%async_computation.2 | async-start | bytes 4456448 | tf_op jit(solution)/shard_map/all_to_all | solution.py:752
  102.1 24.1 %backward.1 = (bf16[32,256,128]{2,1,0:T(8,128)(2,1)}, f32[2,128]{1,0:T(2,128)}) custom-call(s32[3,112]{1,0:T(4,128)} %get-tuple-element.27.pair_ref, s32[1]{0:T(128)} %get-tuple-element.28.total_ref, bf16[32,400,128]{2,1,0:T(8,128)(2,1)} %all-to-all-done.all_ref, bf16[128,4096]{1,0:T(8,128)(2,1)} %get-tuple-element.32.q_turned_in, ...), custom_call_target="tpu_custom_call" | custom-call | flops 8589934592 | bytes 33554432 | tf_op jit(solution)/shard_map/backward/pallas_call | solution.py:718
  126.2 5.6 %all-to-all-done.2.in_ref = bf16[32,272,128]{2,1,0:T(8,128)(2,1)} async-done(((bf16[32,272,128]{2,1,0:T(8,128)(2,1)}), bf16[32,272,128]{2,1,0:T(8,128)(2,1)}, u32[]{:S(2)}, u32[]{:S(2)}) %all-to-all-start.2) | async-done | bytes 2228256 | tf_op jit(solution)/shard_map/all_to_all | solution.py:752
  131.9 5.4 %all-to-all-start.3 = ((bf16[32,256,128]{2,1,0:T(8,128)(2,1)}), bf16[32,256,128]{2,1,0:T(8,128)(2,1)}, u32[]{:S(2)}, u32[]{:S(2)}) async-start(bf16[32,256,128]{2,1,0:T(8,128)(2,1)} %get-tuple-element.42), calls=%async_computation.3 | async-start | bytes 4194304 | tf_op jit(solution)/shard_map/all_to_all | solution.py:752
  137.4 2.0 %collective-permute-start.4 = (f32[2,128]{1,0:T(2,128)S(1)}, f32[2,128]{1,0:T(2,128)S(1)}, u32[]{:S(2)}, u32[]{:S(2)}) collective-permute-start(f32[2,128]{1,0:T(2,128)S(1)} %copy-done.1), channel_id=1, source_target_pairs={{0,64},{32,96},{64,0},{96,32},{1,65},{33,97},{65,1},{97,33},{2,66}... | collective-permute-start | bytes 3080 | tf_op jit(solution)/shard_map/ppermute | solution.py:747
  139.4 1.2 collective-permute-start.5
  140.6 0.6 reduce_sum.37
  141.2 0.2 collective-permute-done.3
  141.4 0.8 collective-permute-done.5
  142.2 0.6 add_add_fusion
  142.8 0.9 convert_reduce_fusion
  143.7 1.3 collective-permute-start.6
  144.9 2.4 %collective-permute-start.7 = (f32[8]{0:T(128)S(1)}, f32[8]{0:T(128)S(1)}, u32[]{:S(2)}, u32[]{:S(2)}) collective-permute-start(f32[8]{0:T(128)S(1)} %convert_reduce_fusion), channel_id=1, source_target_pairs={{0,64},{32,96},{64,0},{96,32},{1,65},{33,97},{65,1},{97,33},{2,66}... | collective-permute-start | bytes 104 | tf_op jit(solution)/shard_map/ppermute | solution.py:747
  147.3 0.1 collective-permute-start.8
  147.4 3.0 %unpack_first.1 = (bf16[1,128,4096]{2,1,0:T(8,128)(2,1)}, bf16[1,128,4096]{2,1,0:T(8,128)(2,1)}) custom-call(bf16[32,272,128]{2,1,0:T(8,128)(2,1)} %all-to-all-done.2.in_ref), custom_call_target="tpu_custom_call" | custom-call | tf_op jit(solution)/shard_map/unpack_first/pallas_call | solution.py:141
  150.5 1.3 fusion
  151.7 1.2 broadcast_divide_fusion
  152.9 12.8 %all-to-all-done.3.in_ref = bf16[32,256,128]{2,1,0:T(8,128)(2,1)} async-done(((bf16[32,256,128]{2,1,0:T(8,128)(2,1)}), bf16[32,256,128]{2,1,0:T(8,128)(2,1)}, u32[]{:S(2)}, u32[]{:S(2)}) %all-to-all-start.3) | async-done | bytes 2097184 | tf_op jit(solution)/shard_map/all_to_all | solution.py:752
  165.7 2.9 %unpack_last.1 = (bf16[1,128,4096]{2,1,0:T(8,128)(2,1)}, bf16[1,128,4096]{2,1,0:T(8,128)(2,1)}) custom-call(bf16[32,256,128]{2,1,0:T(8,128)(2,1)} %all-to-all-done.3.in_ref), custom_call_target="tpu_custom_call" | custom-call | tf_op jit(solution)/shard_map/unpack_last/pallas_call | solution.py:141
  (20 shorter events, 0.2 us)
Async XLA Ops:
  4.8 9.5 %copy-start.2 = (s32[1,128]{1,0:T(1,128)S(1)}, s32[1,128]{1,0:T(1,128)}, u32[]{:S(2)}) copy-start(s32[1,128]{1,0:T(1,128)} %refs_3_.1) | copy-start | bytes 1540
  4.8 9.5 %copy-start.3 = (s32[1,16]{1,0:T(1,128)S(1)}, s32[1,16]{1,0:T(1,128)}, u32[]{:S(2)}) copy-start(s32[1,16]{1,0:T(1,128)} %labels_ref.1) | copy-start | bytes 196
  4.8 50.6 %all-to-all-start = ((bf16[32,400,128]{2,1,0:T(8,128)(2,1)}), bf16[32,400,128]{2,1,0:T(8,128)(2,1)}, u32[]{:S(2)}, u32[]{:S(2)}) async-start(bf16[32,400,128]{2,1,0:T(8,128)(2,1)} %pack_first.1), calls=%async_computation | async-start | bytes 6553600 | tf_op jit(solution)/shard_map/all_to_all | solution.py:752
  14.4 5.1 %collective-permute-start = (f32[1,128]{1,0:T(1,128)S(1)}, f32[1,128]{1,0:T(1,128)S(1)}, u32[]{:S(2)}, u32[]{:S(2)}) collective-permute-start(f32[1,128]{1,0:T(1,128)S(1)} %convert_bitcast_fusion), channel_id=1, source_target_pairs={{0,32},{32,64},{64,96},{96,0},{1,33},{33,65},{65,97},{97,1},{2,34}... | collective-permute-start | bytes 1544 | tf_op jit(solution)/shard_map/ppermute | solution.py:747
  15.8 3.9 %collective-permute-start.1 = (f32[1,128]{1,0:T(1,128)S(1)}, f32[1,128]{1,0:T(1,128)S(1)}, u32[]{:S(2)}, u32[]{:S(2)}) collective-permute-start(f32[1,128]{1,0:T(1,128)S(1)} %convert_bitcast_fusion), channel_id=1, source_target_pairs={{0,64},{32,96},{64,0},{96,32},{1,65},{33,97},{65,1},{97,33},{2,66}... | collective-permute-start | bytes 1544 | tf_op jit(solution)/shard_map/ppermute | solution.py:747
  18.4 2.8 %collective-permute-start.2 = (f32[1,128]{1,0:T(1,128)S(1)}, f32[1,128]{1,0:T(1,128)S(1)}, u32[]{:S(2)}, u32[]{:S(2)}) collective-permute-start(f32[1,128]{1,0:T(1,128)S(1)} %convert_bitcast_fusion), channel_id=1, source_target_pairs={{0,96},{32,0},{64,32},{96,64},{1,97},{33,1},{65,33},{97,65},{2,98}... | collective-permute-start | bytes 1544 | tf_op jit(solution)/shard_map/ppermute | solution.py:747
  55.5 27.6 %all-to-all-start.1 = ((bf16[32,144,128]{2,1,0:T(8,128)(2,1)}), bf16[32,144,128]{2,1,0:T(8,128)(2,1)}, u32[]{:S(2)}, u32[]{:S(2)}) async-start(bf16[32,144,128]{2,1,0:T(8,128)(2,1)} %pack_second.1), calls=%async_computation.1 | async-start | bytes 2359296 | tf_op jit(solution)/shard_map/all_to_all | solution.py:752
  94.6 37.2 %all-to-all-start.2 = ((bf16[32,272,128]{2,1,0:T(8,128)(2,1)}), bf16[32,272,128]{2,1,0:T(8,128)(2,1)}, u32[]{:S(2)}, u32[]{:S(2)}) async-start(bf16[32,272,128]{2,1,0:T(8,128)(2,1)} %get-tuple-element.31), calls=%async_computation.2 | async-start | bytes 4456448 | tf_op jit(solution)/shard_map/all_to_all | solution.py:752
  126.2 11.1 %copy-start.1 = (f32[2,128]{1,0:T(2,128)S(1)}, f32[2,128]{1,0:T(2,128)}, u32[]{:S(2)}) copy-start(f32[2,128]{1,0:T(2,128)} %get-tuple-element.46) | copy-start | bytes 3076
  126.2 14.3 %copy-start = (f32[8]{0:T(128)S(1)}, f32[8]{0:T(128)}, u32[]{:S(2)}) copy-start(f32[8]{0:T(128)} %mixture_ref.1) | copy-start | bytes 100
  131.9 18.6 %copy-start.4 = (f32[1,128]{1,0:T(1,128)S(1)}, f32[1,128]{1,0:T(1,128)}, u32[]{:S(2)}) copy-start(f32[1,128]{1,0:T(1,128)} %get-tuple-element.47) | copy-start | bytes 1540
  131.9 33.8 %all-to-all-start.3 = ((bf16[32,256,128]{2,1,0:T(8,128)(2,1)}), bf16[32,256,128]{2,1,0:T(8,128)(2,1)}, u32[]{:S(2)}, u32[]{:S(2)}) async-start(bf16[32,256,128]{2,1,0:T(8,128)(2,1)} %get-tuple-element.42), calls=%async_computation.3 | async-start | bytes 4194304 | tf_op jit(solution)/shard_map/all_to_all | solution.py:752
  137.3 4.1 %collective-permute-start.3 = (f32[2,128]{1,0:T(2,128)S(1)}, f32[2,128]{1,0:T(2,128)S(1)}, u32[]{:S(2)}, u32[]{:S(2)}) collective-permute-start(f32[2,128]{1,0:T(2,128)S(1)} %copy-done.1), channel_id=1, source_target_pairs={{0,32},{32,64},{64,96},{96,0},{1,33},{33,65},{65,97},{97,1},{2,34}... | collective-permute-start | bytes 3080 | tf_op jit(solution)/shard_map/ppermute | solution.py:747
  137.4 4.0 %collective-permute-start.4 = (f32[2,128]{1,0:T(2,128)S(1)}, f32[2,128]{1,0:T(2,128)S(1)}, u32[]{:S(2)}, u32[]{:S(2)}) collective-permute-start(f32[2,128]{1,0:T(2,128)S(1)} %copy-done.1), channel_id=1, source_target_pairs={{0,64},{32,96},{64,0},{96,32},{1,65},{33,97},{65,1},{97,33},{2,66}... | collective-permute-start | bytes 3080 | tf_op jit(solution)/shard_map/ppermute | solution.py:747
  139.4 2.8 %collective-permute-start.5 = (f32[2,128]{1,0:T(2,128)S(1)}, f32[2,128]{1,0:T(2,128)S(1)}, u32[]{:S(2)}, u32[]{:S(2)}) collective-permute-start(f32[2,128]{1,0:T(2,128)S(1)} %copy-done.1), channel_id=1, source_target_pairs={{0,96},{32,0},{64,32},{96,64},{1,97},{33,1},{65,33},{97,65},{2,98}... | collective-permute-start | bytes 3080 | tf_op jit(solution)/shard_map/ppermute | solution.py:747
  143.7 6.8 %collective-permute-start.6 = (f32[8]{0:T(128)S(1)}, f32[8]{0:T(128)S(1)}, u32[]{:S(2)}, u32[]{:S(2)}) collective-permute-start(f32[8]{0:T(128)S(1)} %convert_reduce_fusion), channel_id=1, source_target_pairs={{0,32},{32,64},{64,96},{96,0},{1,33},{33,65},{65,97},{97,1},{2,34}... | collective-permute-start | bytes 104 | tf_op jit(solution)/shard_map/ppermute | solution.py:747
  144.9 5.5 %collective-permute-start.7 = (f32[8]{0:T(128)S(1)}, f32[8]{0:T(128)S(1)}, u32[]{:S(2)}, u32[]{:S(2)}) collective-permute-start(f32[8]{0:T(128)S(1)} %convert_reduce_fusion), channel_id=1, source_target_pairs={{0,64},{32,96},{64,0},{96,32},{1,65},{33,97},{65,1},{97,33},{2,66}... | collective-permute-start | bytes 104 | tf_op jit(solution)/shard_map/ppermute | solution.py:747
  147.3 3.1 %collective-permute-start.8 = (f32[8]{0:T(128)S(1)}, f32[8]{0:T(128)S(1)}, u32[]{:S(2)}, u32[]{:S(2)}) collective-permute-start(f32[8]{0:T(128)S(1)} %convert_reduce_fusion), channel_id=1, source_target_pairs={{0,96},{32,0},{64,32},{96,64},{1,97},{33,1},{65,33},{97,65},{2,98}... | collective-permute-start | bytes 104 | tf_op jit(solution)/shard_map/ppermute | solution.py:747

commit v9 on v8

--- a/solution.py
+++ b/solution.py
@@ -26,7 +26,7 @@
 TILES = LENGTH // TILE
 PAIR = TILE // BLOCK
 KEYS = 256
-UNROLL = 8
+UNROLL = 10
 MOST_PAIRS = (LENGTH * (1024 // TILE + 1) + TILES * (BLOCK - 1 + KEYS - 1)) // KEYS
 MOST_STEPS = MOST_PAIRS // UNROLL + 1
 MOST_PAIRS = MOST_STEPS * UNROLL

time: 169 us -> 167 us (0.988); the launches traced: 169 us -> 165 us
  Pallas kernels: 70.5 us -> 64.4 us
  starting transfers between devices: 40.2 us -> 44 us
    ppermute x9, starting transfers between devices: 12.1 us -> 16 us  [over_packs(): moved.append(lax.ppermute(value, 'pack', pairs))]
    pallas_call x1, Pallas kernels: 21.8 us -> 19.2 us  [run_attend(): pl.pallas_call(attend_kernel, in_specs=[HBM_SPEC, VMEM_SPEC], out_specs=[...]
    pallas_call x1, Pallas kernels: 24.1 us -> 21.6 us  [run_backward(): pl.pallas_call(backward_kernel, in_specs=[SMEM_SPEC] * 2 + [HBM_SPEC] * 4...]
  transfers between devices with their start and end apart: 13 -> 13, of which waited for: 7 -> 6; matrix products, arithmetic and copies ran while one was open for 3% -> 3% of each run, Pallas kernels for 31% -> 28%
where the time goes in v9:
time: 167 us; the launch traced here: 165 us
  Pallas kernels  64.4 us (39%)
  waiting for transfers between devices  50.5 us (30%)
  starting transfers between devices  44 us (26%)
  other arithmetic  4.58 us (3%)
    all_to_all x4, waiting for transfers between devices, exchange(): return lax.all_to_all(slab, 'seq', split_axis=0, concat_axis=0, tiled=True)  47.6 us
    all_to_all x4, starting transfers between devices, exchange(): return lax.all_to_all(slab, 'seq', split_axis=0, concat_axis=0, tiled=True)  28 us
    pallas_call x1, Pallas kernels, run_backward(): pl.pallas_call(backward_kernel, in_specs=[SMEM_SPEC] * 2 + [HBM_SPEC] * 4...  21.6 us
    pallas_call x1, Pallas kernels, run_attend(): pl.pallas_call(attend_kernel, in_specs=[HBM_SPEC, VMEM_SPEC], out_specs=[...  19.2 us
    ppermute x9, starting transfers between devices, over_packs(): moved.append(lax.ppermute(value, 'pack', pairs))  16 us
    pallas_call x1, Pallas kernels, run_loss(): pl.pallas_call(loss_kernel, in_specs=[SMEM_SPEC] * 4 + [HBM_SPEC] * 3, ou...  10.6 us
    pallas_call x2, Pallas kernels, pack_rows(): pl.pallas_call(functools.partial(pack_kernel, count), in_specs=[HBM_SPEC]...  7.11 us
    pallas_call x2, Pallas kernels, unpack_rows(): pl.pallas_call(functools.partial(unpack_kernel, turned), in_specs=[HBM_SP...  5.92 us
  transfers between devices with their start and end apart: 13, of which 6 were waited for; matrix products, arithmetic and copies ran while one was open for 3% of the time, Pallas kernels for 28%

profile of v9, /device:TPU:1, one launch (start us, length us, event | category | flops | bytes accessed | tf_op | source)
XLA Modules:
  0.0 165.1 jit_solution(15118810615538609287)
XLA Ops:
  0.6 4.2 %pack_first.1 = bf16[32,400,128]{2,1,0:T(8,128)(2,1)} custom-call(bf16[1,128,4096]{2,1,0:T(8,128)(2,1)} %refs_0_.2, bf16[1,128,4096]{2,1,0:T(8,128)(2,1)} %refs_1_.1, bf16[1,128,4096]{2,1,0:T(8,128)(2,1)} %refs_2_.1, s32[1,128]{1,0:T(1,128)} %refs_3_.1), custom_call_target="tpu_custom_call" | custom-call | tf_op jit(solution)/shard_map/pack_first/pallas_call | solution.py:92
  4.8 9.5 %all-to-all-start = ((bf16[32,400,128]{2,1,0:T(8,128)(2,1)}), bf16[32,400,128]{2,1,0:T(8,128)(2,1)}, u32[]{:S(2)}, u32[]{:S(2)}) async-start(bf16[32,400,128]{2,1,0:T(8,128)(2,1)} %pack_first.1), calls=%async_computation | async-start | bytes 6553600 | tf_op jit(solution)/shard_map/all_to_all | solution.py:752
  14.4 1.4 collective-permute-start
  15.8 2.6 %collective-permute-start.1 = (f32[1,128]{1,0:T(1,128)S(1)}, f32[1,128]{1,0:T(1,128)S(1)}, u32[]{:S(2)}, u32[]{:S(2)}) collective-permute-start(f32[1,128]{1,0:T(1,128)S(1)} %convert_bitcast_fusion), channel_id=1, source_target_pairs={{0,64},{32,96},{64,0},{96,32},{1,65},{33,97},{65,1},{97,33},{2,66}... | collective-permute-start | bytes 1544 | tf_op jit(solution)/shard_map/ppermute | solution.py:747
  18.4 1.1 collective-permute-start.2
  19.5 0.2 collective-permute-done.1
  19.7 1.5 collective-permute-done.2
  21.2 0.6 concatenate.3.refs_1_
  21.8 3.0 %pack_second.1 = bf16[32,144,128]{2,1,0:T(8,128)(2,1)} custom-call(bf16[1,128,4096]{2,1,0:T(8,128)(2,1)} %refs_0_.3, f32[5,128]{1,0:T(8,128)} %concatenate.3.refs_1_), custom_call_target="tpu_custom_call" | custom-call | tf_op jit(solution)/shard_map/pack_second/pallas_call | solution.py:92
  24.8 30.7 %all-to-all-done.all_ref = bf16[32,400,128]{2,1,0:T(8,128)(2,1)} async-done(((bf16[32,400,128]{2,1,0:T(8,128)(2,1)}), bf16[32,400,128]{2,1,0:T(8,128)(2,1)}, u32[]{:S(2)}, u32[]{:S(2)}) %all-to-all-start) | async-done | bytes 3276832 | tf_op jit(solution)/shard_map/all_to_all | solution.py:752
  55.5 5.7 %all-to-all-start.1 = ((bf16[32,144,128]{2,1,0:T(8,128)(2,1)}), bf16[32,144,128]{2,1,0:T(8,128)(2,1)}, u32[]{:S(2)}, u32[]{:S(2)}) async-start(bf16[32,144,128]{2,1,0:T(8,128)(2,1)} %pack_second.1), calls=%async_computation.1 | async-start | bytes 2359296 | tf_op jit(solution)/shard_map/all_to_all | solution.py:752
  61.2 19.2 %attend.1 = (s32[3,120]{1,0:T(4,128)}, s32[1]{0:T(128)}, s32[16,2,256]{2,1,0:T(2,128)}, bf16[128,4096]{1,0:T(8,128)(2,1)}, bf16[4096,128]{1,0:T(8,128)(2,1)}, /*...) custom-call(bf16[32,400,128]{2,1,0:T(8,128)(2,1)} %all-to-all-done.al, ...), custom_call_target="tpu_custom_call" | custom-call | flops 8589934592 | bytes 33554432 | tf_op jit(solution)/shard_map/attend/pallas_call | solution.py:437
  80.4 10.6 %loss_and_grad_value.1 = (bf16[32,272,128]{2,1,0:T(8,128)(2,1)}, bf16[128,4096]{1,0:T(8,128)(2,1)}, f32[16,1,256]{2,1,0:T(1,128)}, f32[1,128]{1,0:T(1,128)}) custom-call(s32[1,16]{1,0:T(1,128)} %labels_ref.1, f32[8]{0:T(128)} %mixture_ref.1, s32[3,120]{1,0:T(4,128)} %get-tuple-element.27.pair_ref, s32[1]{0:T(128)} %get-tuple-element.28.total_ref, ...), custom_call_target="tpu_custom_call" | custom-call | tf_op jit(solution)/shard_map/loss_and_grad_value/pallas_call | solution.py:590
  90.9 7.4 %all-to-all-start.2 = ((bf16[32,272,128]{2,1,0:T(8,128)(2,1)}), bf16[32,272,128]{2,1,0:T(8,128)(2,1)}, u32[]{:S(2)}, u32[]{:S(2)}) async-start(bf16[32,272,128]{2,1,0:T(8,128)(2,1)} %get-tuple-element.31), calls=%async_computation.2 | async-start | bytes 4456448 | tf_op jit(solution)/shard_map/all_to_all | solution.py:752
  98.4 21.6 %backward.1 = (bf16[32,256,128]{2,1,0:T(8,128)(2,1)}, f32[2,128]{1,0:T(2,128)}) custom-call(s32[3,120]{1,0:T(4,128)} %get-tuple-element.27.pair_ref, s32[1]{0:T(128)} %get-tuple-element.28.total_ref, bf16[32,400,128]{2,1,0:T(8,128)(2,1)} %all-to-all-done.all_ref, bf16[128,4096]{1,0:T(8,128)(2,1)} %get-tuple-element.32.q_turned_in, ...), custom_call_target="tpu_custom_call" | custom-call | flops 8589934592 | bytes 33554432 | tf_op jit(solution)/shard_map/backward/pallas_call | solution.py:718
  120.0 8.1 %all-to-all-done.2.in_ref = bf16[32,272,128]{2,1,0:T(8,128)(2,1)} async-done(((bf16[32,272,128]{2,1,0:T(8,128)(2,1)}), bf16[32,272,128]{2,1,0:T(8,128)(2,1)}, u32[]{:S(2)}, u32[]{:S(2)}) %all-to-all-start.2) | async-done | bytes 2228256 | tf_op jit(solution)/shard_map/all_to_all | solution.py:752
  128.1 5.4 %all-to-all-start.3 = ((bf16[32,256,128]{2,1,0:T(8,128)(2,1)}), bf16[32,256,128]{2,1,0:T(8,128)(2,1)}, u32[]{:S(2)}, u32[]{:S(2)}) async-start(bf16[32,256,128]{2,1,0:T(8,128)(2,1)} %get-tuple-element.42), calls=%async_computation.3 | async-start | bytes 4194304 | tf_op jit(solution)/shard_map/all_to_all | solution.py:752
  133.5 3.6 %collective-permute-start.3 = (f32[2,128]{1,0:T(2,128)S(1)}, f32[2,128]{1,0:T(2,128)S(1)}, u32[]{:S(2)}, u32[]{:S(2)}) collective-permute-start(f32[2,128]{1,0:T(2,128)S(1)} %copy-done.1), channel_id=1, source_target_pairs={{0,32},{32,64},{64,96},{96,0},{1,33},{33,65},{65,97},{97,1},{2,34}... | collective-permute-start | bytes 3080 | tf_op jit(solution)/shard_map/ppermute | solution.py:747
  137.2 2.6 %collective-permute-start.4 = (f32[2,128]{1,0:T(2,128)S(1)}, f32[2,128]{1,0:T(2,128)S(1)}, u32[]{:S(2)}, u32[]{:S(2)}) collective-permute-start(f32[2,128]{1,0:T(2,128)S(1)} %copy-done.1), channel_id=1, source_target_pairs={{0,64},{32,96},{64,0},{96,32},{1,65},{33,97},{65,1},{97,33},{2,66}... | collective-permute-start | bytes 3080 | tf_op jit(solution)/shard_map/ppermute | solution.py:747
  139.8 1.1 collective-permute-start.5
  140.8 0.6 reduce_sum.37
  141.5 1.1 collective-permute-done.5
  142.6 0.6 add_add_fusion
  143.2 0.9 convert_reduce_fusion
  144.1 0.2 collective-permute-start.6
  144.3 3.3 %collective-permute-start.7 = (f32[8]{0:T(128)S(1)}, f32[8]{0:T(128)S(1)}, u32[]{:S(2)}, u32[]{:S(2)}) collective-permute-start(f32[8]{0:T(128)S(1)} %convert_reduce_fusion), channel_id=1, source_target_pairs={{0,64},{32,96},{64,0},{96,32},{1,65},{33,97},{65,1},{97,33},{2,66}... | collective-permute-start | bytes 104 | tf_op jit(solution)/shard_map/ppermute | solution.py:747
  147.6 0.1 collective-permute-start.8
  147.7 3.0 %unpack_first.1 = (bf16[1,128,4096]{2,1,0:T(8,128)(2,1)}, bf16[1,128,4096]{2,1,0:T(8,128)(2,1)}) custom-call(bf16[32,272,128]{2,1,0:T(8,128)(2,1)} %all-to-all-done.2.in_ref), custom_call_target="tpu_custom_call" | custom-call | tf_op jit(solution)/shard_map/unpack_first/pallas_call | solution.py:141
  150.7 1.3 fusion
  152.0 1.2 broadcast_divide_fusion
  153.2 8.8 %all-to-all-done.3.in_ref = bf16[32,256,128]{2,1,0:T(8,128)(2,1)} async-done(((bf16[32,256,128]{2,1,0:T(8,128)(2,1)}), bf16[32,256,128]{2,1,0:T(8,128)(2,1)}, u32[]{:S(2)}, u32[]{:S(2)}) %all-to-all-start.3) | async-done | bytes 2097184 | tf_op jit(solution)/shard_map/all_to_all | solution.py:752
  162.0 2.9 %unpack_last.1 = (bf16[1,128,4096]{2,1,0:T(8,128)(2,1)}, bf16[1,128,4096]{2,1,0:T(8,128)(2,1)}) custom-call(bf16[32,256,128]{2,1,0:T(8,128)(2,1)} %all-to-all-done.3.in_ref), custom_call_target="tpu_custom_call" | custom-call | tf_op jit(solution)/shard_map/unpack_last/pallas_call | solution.py:141
  (20 shorter events, 0.2 us)
Async XLA Ops:
  4.8 9.5 %copy-start.2 = (s32[1,128]{1,0:T(1,128)S(1)}, s32[1,128]{1,0:T(1,128)}, u32[]{:S(2)}) copy-start(s32[1,128]{1,0:T(1,128)} %refs_3_.1) | copy-start | bytes 1540
  4.8 9.5 %copy-start.3 = (s32[1,16]{1,0:T(1,128)S(1)}, s32[1,16]{1,0:T(1,128)}, u32[]{:S(2)}) copy-start(s32[1,16]{1,0:T(1,128)} %labels_ref.1) | copy-start | bytes 196
  4.8 50.6 %all-to-all-start = ((bf16[32,400,128]{2,1,0:T(8,128)(2,1)}), bf16[32,400,128]{2,1,0:T(8,128)(2,1)}, u32[]{:S(2)}, u32[]{:S(2)}) async-start(bf16[32,400,128]{2,1,0:T(8,128)(2,1)} %pack_first.1), calls=%async_computation | async-start | bytes 6553600 | tf_op jit(solution)/shard_map/all_to_all | solution.py:752
  14.4 5.1 %collective-permute-start = (f32[1,128]{1,0:T(1,128)S(1)}, f32[1,128]{1,0:T(1,128)S(1)}, u32[]{:S(2)}, u32[]{:S(2)}) collective-permute-start(f32[1,128]{1,0:T(1,128)S(1)} %convert_bitcast_fusion), channel_id=1, source_target_pairs={{0,32},{32,64},{64,96},{96,0},{1,33},{33,65},{65,97},{97,1},{2,34}... | collective-permute-start | bytes 1544 | tf_op jit(solution)/shard_map/ppermute | solution.py:747
  15.8 3.9 %collective-permute-start.1 = (f32[1,128]{1,0:T(1,128)S(1)}, f32[1,128]{1,0:T(1,128)S(1)}, u32[]{:S(2)}, u32[]{:S(2)}) collective-permute-start(f32[1,128]{1,0:T(1,128)S(1)} %convert_bitcast_fusion), channel_id=1, source_target_pairs={{0,64},{32,96},{64,0},{96,32},{1,65},{33,97},{65,1},{97,33},{2,66}... | collective-permute-start | bytes 1544 | tf_op jit(solution)/shard_map/ppermute | solution.py:747
  18.4 2.8 %collective-permute-start.2 = (f32[1,128]{1,0:T(1,128)S(1)}, f32[1,128]{1,0:T(1,128)S(1)}, u32[]{:S(2)}, u32[]{:S(2)}) collective-permute-start(f32[1,128]{1,0:T(1,128)S(1)} %convert_bitcast_fusion), channel_id=1, source_target_pairs={{0,96},{32,0},{64,32},{96,64},{1,97},{33,1},{65,33},{97,65},{2,98}... | collective-permute-start | bytes 1544 | tf_op jit(solution)/shard_map/ppermute | solution.py:747
  55.5 24.9 %all-to-all-start.1 = ((bf16[32,144,128]{2,1,0:T(8,128)(2,1)}), bf16[32,144,128]{2,1,0:T(8,128)(2,1)}, u32[]{:S(2)}, u32[]{:S(2)}) async-start(bf16[32,144,128]{2,1,0:T(8,128)(2,1)} %pack_second.1), calls=%async_computation.1 | async-start | bytes 2359296 | tf_op jit(solution)/shard_map/all_to_all | solution.py:752
  90.9 37.2 %all-to-all-start.2 = ((bf16[32,272,128]{2,1,0:T(8,128)(2,1)}), bf16[32,272,128]{2,1,0:T(8,128)(2,1)}, u32[]{:S(2)}, u32[]{:S(2)}) async-start(bf16[32,272,128]{2,1,0:T(8,128)(2,1)} %get-tuple-element.31), calls=%async_computation.2 | async-start | bytes 4456448 | tf_op jit(solution)/shard_map/all_to_all | solution.py:752
  120.0 13.5 %copy-start.1 = (f32[2,128]{1,0:T(2,128)S(1)}, f32[2,128]{1,0:T(2,128)}, u32[]{:S(2)}) copy-start(f32[2,128]{1,0:T(2,128)} %get-tuple-element.46) | copy-start | bytes 3076
  120.0 20.8 %copy-start = (f32[8]{0:T(128)S(1)}, f32[8]{0:T(128)}, u32[]{:S(2)}) copy-start(f32[8]{0:T(128)} %mixture_ref.1) | copy-start | bytes 100
  128.1 22.6 %copy-start.4 = (f32[1,128]{1,0:T(1,128)S(1)}, f32[1,128]{1,0:T(1,128)}, u32[]{:S(2)}) copy-start(f32[1,128]{1,0:T(1,128)} %get-tuple-element.47) | copy-start | bytes 1540
  128.1 33.8 %all-to-all-start.3 = ((bf16[32,256,128]{2,1,0:T(8,128)(2,1)}), bf16[32,256,128]{2,1,0:T(8,128)(2,1)}, u32[]{:S(2)}, u32[]{:S(2)}) async-start(bf16[32,256,128]{2,1,0:T(8,128)(2,1)} %get-tuple-element.42), calls=%async_computation.3 | async-start | bytes 4194304 | tf_op jit(solution)/shard_map/all_to_all | solution.py:752
  133.5 7.9 %collective-permute-start.3 = (f32[2,128]{1,0:T(2,128)S(1)}, f32[2,128]{1,0:T(2,128)S(1)}, u32[]{:S(2)}, u32[]{:S(2)}) collective-permute-start(f32[2,128]{1,0:T(2,128)S(1)} %copy-done.1), channel_id=1, source_target_pairs={{0,32},{32,64},{64,96},{96,0},{1,33},{33,65},{65,97},{97,1},{2,34}... | collective-permute-start | bytes 3080 | tf_op jit(solution)/shard_map/ppermute | solution.py:747
  137.2 4.3 %collective-permute-start.4 = (f32[2,128]{1,0:T(2,128)S(1)}, f32[2,128]{1,0:T(2,128)S(1)}, u32[]{:S(2)}, u32[]{:S(2)}) collective-permute-start(f32[2,128]{1,0:T(2,128)S(1)} %copy-done.1), channel_id=1, source_target_pairs={{0,64},{32,96},{64,0},{96,32},{1,65},{33,97},{65,1},{97,33},{2,66}... | collective-permute-start | bytes 3080 | tf_op jit(solution)/shard_map/ppermute | solution.py:747
  139.8 2.8 %collective-permute-start.5 = (f32[2,128]{1,0:T(2,128)S(1)}, f32[2,128]{1,0:T(2,128)S(1)}, u32[]{:S(2)}, u32[]{:S(2)}) collective-permute-start(f32[2,128]{1,0:T(2,128)S(1)} %copy-done.1), channel_id=1, source_target_pairs={{0,96},{32,0},{64,32},{96,64},{1,97},{33,1},{65,33},{97,65},{2,98}... | collective-permute-start | bytes 3080 | tf_op jit(solution)/shard_map/ppermute | solution.py:747
  144.1 6.6 %collective-permute-start.6 = (f32[8]{0:T(128)S(1)}, f32[8]{0:T(128)S(1)}, u32[]{:S(2)}, u32[]{:S(2)}) collective-permute-start(f32[8]{0:T(128)S(1)} %convert_reduce_fusion), channel_id=1, source_target_pairs={{0,32},{32,64},{64,96},{96,0},{1,33},{33,65},{65,97},{97,1},{2,34}... | collective-permute-start | bytes 104 | tf_op jit(solution)/shard_map/ppermute | solution.py:747
  144.3 6.4 %collective-permute-start.7 = (f32[8]{0:T(128)S(1)}, f32[8]{0:T(128)S(1)}, u32[]{:S(2)}, u32[]{:S(2)}) collective-permute-start(f32[8]{0:T(128)S(1)} %convert_reduce_fusion), channel_id=1, source_target_pairs={{0,64},{32,96},{64,0},{96,32},{1,65},{33,97},{65,1},{97,33},{2,66}... | collective-permute-start | bytes 104 | tf_op jit(solution)/shard_map/ppermute | solution.py:747
  147.6 3.1 %collective-permute-start.8 = (f32[8]{0:T(128)S(1)}, f32[8]{0:T(128)S(1)}, u32[]{:S(2)}, u32[]{:S(2)}) collective-permute-start(f32[8]{0:T(128)S(1)} %convert_reduce_fusion), channel_id=1, source_target_pairs={{0,96},{32,0},{64,32},{96,64},{1,97},{33,1},{65,33},{97,65},{2,98}... | collective-permute-start | bytes 104 | tf_op jit(solution)/shard_map/ppermute | solution.py:747
